TPU v7x, 256 devices: a whole 4x4x8 slice. The times are simulated.
256 devices in a mesh: dp: 64 (over x, z, y_hi), pipe: 4 (over y_lo, core).
Axes of the slice: x: 4, y: 4 (y_hi: 2, y_lo: 2; y = y_hi * 2 + y_lo), z: 8, core: 2. Of those that a mesh axis runs over, the one named last changes fastest.
Arguments:
- section_inputs: bfloat16 [4, 64, 2, 4, 8, 4, 256], P('pipe', 'dp'), may hold values from -3 to 3
- top_grad: bfloat16 [64, 2, 4, 8, 4, 256], P('dp'), may hold values from -6 to 6
- norm_gain: float32 [4, 256], P('pipe'), may hold values from 0.1 to 1.9
- norm_shift: float32 [4, 256], P('pipe'), may hold values from -3 to 3
- conv_weight: bfloat16 [4, 6912, 256], P('pipe', 'dp'), may hold values from -0.078125 to 0.078125
Outputs:
- input_grads: bfloat16 [4, 64, 2, 4, 8, 4, 256], P('pipe', 'dp')
- weight_grads: float32 [4, 6912, 256], P('pipe', 'dp')
All inputs are finite; a program needn't handle non-finite values.
Results may differ from a plain program's by a relative error of at most 0.008.
Values may be sent and summed in bfloat16 or wider, within the bound.
No kernel may reach another device: no remote copies, remote signals or barrier semaphores. Data moves between devices by JAX's collectives and lax.ppermute only.
A program may use at most 64 MiB of HBM per device.

v0:
```python
import jax
import jax.numpy as jnp
from jax import lax
from jax.sharding import PartitionSpec as P

GROUPS = 32
F = 4
H = 8
W = 4
M = 2


def from_behind(block, axis, distance):
    devices = range(lax.axis_size(axis))
    route = [(i - distance, i) for i in devices if i - distance in devices]
    return lax.ppermute(block, axis, route)


def norm_forward(x_float, gain_row, shift_row):
    dims_full = x_float.shape
    channels = dims_full[-1]
    grouped = x_float.reshape(
        dims_full[:-3] + (dims_full[-3] * dims_full[-2], GROUPS, channels // GROUPS)
    )
    average = jnp.mean(grouped, axis=(-3, -1), keepdims=True)
    variance = jnp.mean(jnp.square(grouped - average), axis=(-3, -1), keepdims=True)
    inv_std = lax.rsqrt(variance + 1e-06)
    x_hat = ((grouped - average) * inv_std).reshape(dims_full)
    normed = x_hat * gain_row + shift_row
    return (normed, x_hat, inv_std)


def norm_backward(grad_act, normed, x_hat, inv_std, gain_row):
    sigmoid_n = jax.nn.sigmoid(normed)
    grad_hat = grad_act * sigmoid_n * (1.0 + normed * (1.0 - sigmoid_n)) * gain_row
    dims_full = grad_hat.shape
    grouped_shape = inv_std.shape[:-3] + (
        dims_full[-3] * dims_full[-2],
        GROUPS,
        dims_full[-1] // GROUPS,
    )
    grad_grouped = grad_hat.reshape(grouped_shape)
    hat_grouped = x_hat.reshape(grouped_shape)
    first_mean = jnp.mean(grad_grouped, axis=(-3, -1), keepdims=True)
    second_mean = jnp.mean(grad_grouped * hat_grouped, axis=(-3, -1), keepdims=True)
    result = inv_std * (grad_grouped - first_mean - hat_grouped * second_mean)
    return result.reshape(dims_full)


def tap_offsets():
    return [
        (k_time, k_high, k_wide)
        for k_time in range(3)
        for k_high in range(3)
        for k_wide in range(3)
    ]


def local(section_inputs, top_grad, norm_gain, norm_shift, conv_weight):
    x_local = section_inputs[0]
    clip_count = x_local.shape[0]
    channels = x_local.shape[-1]
    gain_row = norm_gain[0]
    shift_row = norm_shift[0]
    section_idx = lax.axis_index("pipe")
    section_count = lax.axis_size("pipe")
    kernel_full = lax.all_gather(conv_weight[0], "dp", axis=0, tiled=True)
    w_taps = (
        kernel_full.reshape(27, channels, channels)
        .transpose(0, 2, 1)
        .reshape(27 * channels, channels)
    )
    frames = F
    blocks = F // frames
    unit_total = M * blocks
    dy_padded = jnp.pad(top_grad, ((0, 0), (0, 0), (0, 2), (1, 1), (1, 1), (0, 0)))
    grad_buffer = jnp.where(section_idx == section_count - 1, dy_padded, jnp.zeros_like(dy_padded))
    dx_all = jnp.zeros_like(x_local)
    for step_idx in range(unit_total + section_count - 1):
        unit_idx = step_idx - (section_count - 1 - section_idx)
        active = (unit_idx >= 0) & (unit_idx < unit_total)
        unit_clip = jnp.clip(unit_idx, 0, unit_total - 1)
        micro_idx = unit_clip // blocks
        frame_from = (blocks - 1 - unit_clip % blocks) * frames
        window = lax.dynamic_slice(
            grad_buffer,
            (0, micro_idx, frame_from, 0, 0, 0),
            (clip_count, 1, frames + 2, H + 2, W + 2, channels),
        )[:, 0]
        tap_list = [
            window[
                :,
                2 - k_time : 2 - k_time + frames,
                2 - k_high : 2 - k_high + H,
                2 - k_wide : 2 - k_wide + W,
            ]
            for k_time, k_high, k_wide in tap_offsets()
        ]
        columns = jnp.stack(tap_list, axis=-2).reshape(-1, 27 * channels)
        grad_act = jnp.dot(columns, w_taps, preferred_element_type=jnp.float32).reshape(
            clip_count, frames, H, W, channels
        )
        x_block = lax.dynamic_slice(
            x_local, (0, micro_idx, frame_from, 0, 0, 0), (clip_count, 1, frames, H, W, channels)
        )[:, 0]
        normed, x_hat, inv_std = norm_forward(x_block.astype(jnp.float32), gain_row, shift_row)
        grad_in = norm_backward(grad_act, normed, x_hat, inv_std, gain_row).astype(jnp.bfloat16)
        current = lax.dynamic_slice(
            dx_all, (0, micro_idx, frame_from, 0, 0, 0), (clip_count, 1, frames, H, W, channels)
        )
        dx_all = lax.dynamic_update_slice(
            dx_all,
            jnp.where(active, grad_in[:, None], current),
            (0, micro_idx, frame_from, 0, 0, 0),
        )
        arrived = from_behind(grad_in, "pipe", -1)
        later_idx = step_idx - (section_count - 2 - section_idx)
        accept = (later_idx >= 0) & (later_idx < unit_total) & (section_idx < section_count - 1)
        later_clip = jnp.clip(later_idx, 0, unit_total - 1)
        later_micro = later_clip // blocks
        later_from = (blocks - 1 - later_clip % blocks) * frames
        arrived_pad = jnp.pad(arrived, ((0, 0), (0, 0), (1, 1), (1, 1), (0, 0)))[:, None]
        kept_rows = lax.dynamic_slice(
            grad_buffer,
            (0, later_micro, later_from, 0, 0, 0),
            (clip_count, 1, frames, H + 2, W + 2, channels),
        )
        grad_buffer = lax.dynamic_update_slice(
            grad_buffer,
            jnp.where(accept, arrived_pad, kept_rows),
            (0, later_micro, later_from, 0, 0, 0),
        )
    normed_all, x_hat_all, inv_std_all = norm_forward(
        x_local.astype(jnp.float32), gain_row, shift_row
    )
    acts = jax.nn.silu(normed_all).astype(jnp.bfloat16)
    a_pad = jnp.pad(acts, ((0, 0), (0, 0), (2, 0), (1, 1), (1, 1), (0, 0)))
    a_columns = jnp.stack(
        [
            a_pad[:, :, k_time : k_time + F, k_high : k_high + H, k_wide : k_wide + W]
            for k_time, k_high, k_wide in tap_offsets()
        ],
        axis=-2,
    ).reshape(-1, 27 * channels)
    grad_flat = grad_buffer[:, :, :F, 1 : H + 1, 1 : W + 1].reshape(-1, channels)
    summed = lax.psum_scatter(
        lax.dot_general(
            a_columns, grad_flat, (((0,), (0,)), ((), ())), preferred_element_type=jnp.float32
        ),
        "dp",
        scatter_dimension=0,
        tiled=True,
    )
    weight_part = summed / (clip_count * lax.axis_size("dp"))
    return (dx_all[None], weight_part[None])


def solution(mesh):
    placed = (
        P("pipe", "dp", None, None, None, None, None),
        P("dp", None, None, None, None, None),
        P("pipe", None),
        P("pipe", None),
        P("pipe", "dp", None),
    )
    return jax.shard_map(
        local,
        mesh=mesh,
        in_specs=placed,
        out_specs=(P("pipe", "dp", None, None, None, None, None), P("pipe", "dp", None)),
        check_vma=False,
    )
```

profile of v0, /device:TPU:6, one launch (start us, length us, event | category | flops | bytes accessed | tf_op | source)
XLA Modules:
  0.0 528.3 jit_solution(10869290642801841096)
XLA Ops:
  7.2 1.6 copy.457
  36.3 120.2 %all-gather.3.cloned.1.call-done = bf16[1,6912,256]{2,0,1:T(2,128)(2,1)} async-done(((bf16[1,108,256]{2,0,1:T(2,128)(2,1)}), bf16[1,6912,256]{2,0,1:T(2,128)(2,1)}) %all-gather.3.cloned.1.call-update) | async-done | bytes 3538960 | tf_op jit(solution)/shard_map/all_gather | solution.py:67
  156.5 5.4 %copy.572 = bf16[1,6912,256]{2,1,0:T(8,128)(2,1)} copy(bf16[1,6912,256]{2,0,1:T(2,128)(2,1)} %all-gather.3.cloned.1.call-done) | data formatting | bytes 7077888
  161.9 4.4 copy.458
  166.4 3.4 fusion.157
  182.1 1.6 bitcast_dynamic-update-slice_fusion.1
  197.8 1.7 fusion.27
  201.3 1.9 fusion.156
  214.8 1.6 fusion.152
  217.7 1.7 constant_dynamic-update-slice_fusion.138
  220.2 1.7 fusion.26
  223.7 1.9 fusion.155
  237.2 1.6 fusion.151
  240.3 1.6 constant_dynamic-update-slice_fusion.137
  241.9 2.5 collective-permute-done.2
  244.4 1.7 fusion.25
  247.9 1.9 fusion.154
  261.5 1.6 fusion.150
  264.4 1.6 constant_dynamic-update-slice_fusion.136
  266.0 1.6 copy.747
  268.7 1.6 fusion.24
  272.2 1.9 fusion.153
  276.2 1.7 bitcast_dynamic-update-slice_fusion
  279.2 1.6 constant_dynamic-update-slice_fusion.135
  280.8 5.8 %copy.567 = bf16[1,2,4,8,4,27,256]{6,5,4,3,2,1,0:T(8,128)(2,1)S(1)} copy(bf16[1,2,4,8,4,27,256]{6,4,3,2,1,5,0:T(4,128)(2,1)} %constant_dynamic-update-slice_fusion.135) | data formatting | bytes 7077888 | tf_op jit(solution)/shard_map/stack | solution.py:138
  286.6 5.5 %copy.578 = bf16[32,8,27,256]{3,1,2,0:T(8,128)(2,1)} copy(bf16[32,8,27,256]{3,2,1,0:T(8,128)(2,1)S(1)} %bitcast.1270) | data formatting | bytes 7077888
  292.3 6.1 %fusion.163 = f32[6912,256]{1,0:T(8,128)} fusion(bf16[256,6912]{1,0:T(8,128)(2,1)} %bitcast.1269, bf16[256,256]{1,0:T(8,128)(2,1)S(1)} %reshape.938), kind=kOutput, calls=%fused_computation.551 | convolution fusion | flops 905969664 | bytes 10747904 | tf_op jit(solution)/shard_map/dot_general | solution.py:147
  298.3 205.5 %fusion = f32[112,256]{1,0:T(8,128)S(1)} fusion(f32[6912,256]{1,0:T(8,128)} %fusion.163), kind=kCustom, calls=%all-reduce-scatter | all-reduce-scatter fusion | flops 1835009 | bytes 7193600
  503.8 1.9 collective-permute-start.6
  505.7 3.0 collective-permute-start.5
  508.8 3.8 collective-permute-start.7
  514.6 5.5 %collective-permute-done.7 = f32[28,256]{1,0:T(8,128)S(1)} collective-permute-done((f32[28,256]{1,0:T(8,128)S(1)}, f32[28,256]{1,0:T(8,128)S(1)}, u32[]{:S(2)}, u32[]{:S(2)}) %collective-permute-start.7) | collective-permute-done | bytes 28704
  (369 shorter events, 106.7 us)
Async XLA Ops:
  7.2 4.7 copy-start.3
  7.2 4.7 copy-start.15
  7.2 149.3 %all-gather.3.cloned.1.call-start = ((), (), s32[]{:S(2)}) async-start(), calls=%async_computation | async-start | bytes 7188480 | tf_op jit(solution)/shard_map/all_gather | solution.py:67
  11.7 3.6 copy-start.17
  11.7 3.6 copy-start.20
  12.0 6.4 %copy-start.5 = (bf16[1,1,1,4,8,4,256]{6,5,4,3,2,1,0:T(4,128)(2,1)}, bf16[1,1,1,4,8,4,256]{6,5,4,3,2,1,0:T(4,128)(2,1)S(1)}, u32[]{:S(2)}) copy-start(bf16[1,1,1,4,8,4,256]{6,5,4,3,2,1,0:T(4,128)(2,1)S(1)} %get-tuple-element.30) | copy-start | bytes 196612
  12.0 6.4 %copy-start.7 = (bf16[1,1,1,4,8,4,256]{6,5,4,3,2,1,0:T(4,128)(2,1)}, bf16[1,1,1,4,8,4,256]{6,5,4,3,2,1,0:T(4,128)(2,1)S(1)}, u32[]{:S(2)}) copy-start(bf16[1,1,1,4,8,4,256]{6,5,4,3,2,1,0:T(4,128)(2,1)S(1)} %get-tuple-element.31) | copy-start | bytes 196612
  12.0 6.4 %copy-start.9 = (bf16[1,1,1,4,8,4,256]{6,5,4,3,2,1,0:T(4,128)(2,1)}, bf16[1,1,1,4,8,4,256]{6,5,4,3,2,1,0:T(4,128)(2,1)S(1)}, u32[]{:S(2)}) copy-start(bf16[1,1,1,4,8,4,256]{6,5,4,3,2,1,0:T(4,128)(2,1)S(1)} %get-tuple-element.32) | copy-start | bytes 196612
  12.0 6.3 %copy-start.11 = (bf16[1,1,1,4,8,4,256]{6,5,4,3,2,1,0:T(4,128)(2,1)}, bf16[1,1,1,4,8,4,256]{6,5,4,3,2,1,0:T(4,128)(2,1)S(1)}, u32[]{:S(2)}) copy-start(bf16[1,1,1,4,8,4,256]{6,5,4,3,2,1,0:T(4,128)(2,1)S(1)} %get-tuple-element.33) | copy-start | bytes 196612
  12.1 6.3 %copy-start.13 = (bf16[1,1,1,4,8,4,256]{6,5,4,3,2,1,0:T(4,128)(2,1)}, bf16[1,1,1,4,8,4,256]{6,5,4,3,2,1,0:T(4,128)(2,1)S(1)}, u32[]{:S(2)}) copy-start(bf16[1,1,1,4,8,4,256]{6,5,4,3,2,1,0:T(4,128)(2,1)S(1)} %get-tuple-element.34) | copy-start | bytes 196612
  13.0 7.5 %copy-start.16 = (f32[4,256]{1,0:T(4,128)}, f32[4,256]{1,0:T(4,128)S(1)}, u32[]{:S(2)}) copy-start(f32[4,256]{1,0:T(4,128)S(1)} %sub.460) | copy-start | bytes 12292
  15.6 15.0 %copy-start = (bf16[1,2,4,8,4,256]{5,4,3,2,1,0:T(4,128)(2,1)}, bf16[1,2,4,8,4,256]{5,4,3,2,1,0:T(4,128)(2,1)S(1)}, u32[]{:S(2)}) copy-start(bf16[1,2,4,8,4,256]{5,4,3,2,1,0:T(4,128)(2,1)S(1)} %fusion.22) | copy-start | bytes 393220
  30.5 4.4 copy-start.1
  35.2 126.7 %copy-start.4 = (bf16[1,4,8,4,27,256]{5,2,4,3,1,0:T(8,128)(2,1)}, bf16[1,4,8,4,27,256]{5,2,4,3,1,0:T(8,128)(2,1)S(1)}, u32[]{:S(2)}) copy-start(bf16[1,4,8,4,27,256]{5,2,4,3,1,0:T(8,128)(2,1)S(1)} %constant_dynamic-update-slice_fusion) | copy-start | bytes 5308420
  183.7 14.1 %collective-permute-start = (bf16[1,4,8,4,256]{4,2,3,1,0:T(8,128)(2,1)}, bf16[1,4,8,4,256]{4,2,3,1,0:T(8,128)(2,1)}, u32[]{:S(2)}, u32[]{:S(2)}) collective-permute-start(bf16[1,4,8,4,256]{4,2,3,1,0:T(8,128)(2,1)} %bitcast.65), channel_id=1, source_target_pairs={{1,0},{2,1},{3,2},{5,4},{6,5},{7,6},{9,8},{10,9},{11,10},{13,12},{... | collective-permute-start | bytes 196616 | tf_op jit(solution)/shard_map/ppermute | solution.py:16
  200.5 0.8 copy-start.12
  200.5 0.8 copy-start.18
  216.4 3.8 collective-permute-start.1
  222.8 0.8 copy-start.10
  222.8 0.8 copy-start.19
  238.8 5.6 %collective-permute-start.2 = (bf16[1,4,8,4,256]{4,2,3,1,0:T(8,128)(2,1)S(1)}, bf16[1,4,8,4,256]{4,2,3,1,0:T(8,128)(2,1)S(1)}, u32[]{:S(2)}, u32[]{:S(2)}) collective-permute-start(bf16[1,4,8,4,256]{4,2,3,1,0:T(8,128)(2,1)S(1)} %bitcast.1280), channel_id=1, source_target_pairs={{1,0},{2,1},{3,2},{5,4},{6,5},{7,6},{9,8},{10,9},{11,10},{13,12},{... | collective-permute-start | bytes 196616 | tf_op jit(solution)/shard_map/ppermute | solution.py:16
  247.0 0.8 copy-start.8
  247.1 0.8 copy-start.23
  263.1 5.6 %collective-permute-start.3 = (bf16[1,4,8,4,256]{4,2,3,1,0:T(8,128)(2,1)S(1)}, bf16[1,4,8,4,256]{4,2,3,1,0:T(8,128)(2,1)S(1)}, u32[]{:S(2)}, u32[]{:S(2)}) collective-permute-start(bf16[1,4,8,4,256]{4,2,3,1,0:T(8,128)(2,1)S(1)} %bitcast.1278), channel_id=1, source_target_pairs={{1,0},{2,1},{3,2},{5,4},{6,5},{7,6},{9,8},{10,9},{11,10},{13,12},{... | collective-permute-start | bytes 196616 | tf_op jit(solution)/shard_map/ppermute | solution.py:16
  271.3 0.8 copy-start.6
  277.9 14.2 %collective-permute-start.4 = (bf16[1,4,8,4,256]{4,2,3,1,0:T(8,128)(2,1)S(1)}, bf16[1,4,8,4,256]{4,2,3,1,0:T(8,128)(2,1)S(1)}, u32[]{:S(2)}, u32[]{:S(2)}) collective-permute-start(bf16[1,4,8,4,256]{4,2,3,1,0:T(8,128)(2,1)S(1)} %bitcast.1277), channel_id=1, source_target_pairs={{1,0},{2,1},{3,2},{5,4},{6,5},{7,6},{9,8},{10,9},{11,10},{13,12},{... | collective-permute-start | bytes 196616 | tf_op jit(solution)/shard_map/ppermute | solution.py:16
  286.6 5.5 %copy-start.2 = (bf16[1,2,6,10,6,256]{5,3,4,2,1,0:T(8,128)(2,1)S(1)}, bf16[1,2,6,10,6,256]{5,3,4,2,1,0:T(8,128)(2,1)}, u32[]{:S(2)}) copy-start(bf16[1,2,6,10,6,256]{5,3,4,2,1,0:T(8,128)(2,1)} %fusion.24) | copy-start | bytes 1105924
  298.3 214.3 %copy-start.28 = (u32[256]{0:T(256)S(1)}, u32[256]{0:T(256)}, u32[]{:S(2)}) copy-start(u32[256]{0:T(256)} %constant.243) | copy-start | bytes 3076
  298.3 215.5 %copy-start.14 = (bf16[1,1,2,4,8,4,256]{6,4,5,3,2,1,0:T(8,128)(2,1)S(1)}, bf16[1,1,2,4,8,4,256]{6,4,5,3,2,1,0:T(8,128)(2,1)}, u32[]{:S(2)}) copy-start(bf16[1,1,2,4,8,4,256]{6,4,5,3,2,1,0:T(8,128)(2,1)} %get-tuple-element.20) | copy-start | bytes 393220
  503.8 16.2 %collective-permute-start.6 = (f32[112,256]{1,0:T(8,128)S(1)}, f32[112,256]{1,0:T(8,128)S(1)}, u32[]{:S(2)}, u32[]{:S(2)}) collective-permute-start(f32[112,256]{1,0:T(8,128)S(1)} %fusion), channel_id=1, source_target_pairs={{0,8},{4,12},{8,16},{12,20},{16,24},{20,28},{24,32},{28,36},{32,40... | collective-permute-start | bytes 344072
  505.7 14.3 %collective-permute-start.5 = (f32[112,256]{1,0:T(8,128)S(1)}, f32[112,256]{1,0:T(8,128)S(1)}, u32[]{:S(2)}, u32[]{:S(2)}) collective-permute-start(f32[112,256]{1,0:T(8,128)S(1)} %fusion), channel_id=1, source_target_pairs={{0,4},{4,8},{8,12},{12,16},{16,20},{20,24},{24,28},{28,32},{32,36}... | collective-permute-start | bytes 344072
  508.8 11.2 %collective-permute-start.7 = (f32[28,256]{1,0:T(8,128)S(1)}, f32[28,256]{1,0:T(8,128)S(1)}, u32[]{:S(2)}, u32[]{:S(2)}) collective-permute-start(f32[28,256]{1,0:T(8,128)S(1)} %slice.785), channel_id=1, source_target_pairs={{0,12},{4,16},{8,20},{12,24},{16,28},{20,32},{24,36},{28,40},{32,4... | collective-permute-start | bytes 86024
  (6 other events, 4.9 us)
Sparse Core Ops, SparseCore 0:
  12.3 144.1 all-gather.2
where the time goes:
time: 537 us; the launch traced here: 528 us
  blocking collectives  205 us (38%)
  waiting for transfers between devices  130 us (24%)
  local copies, waits for them, and re-layouts  103 us (19%)
  other arithmetic  40.8 us (8%)
  matrix products  17.2 us (3%)
  between operations  16.6 us (3%)
  starting transfers between devices  15.4 us (3%)
    unnamed x1, blocking collectives  205 us
    all_gather x1, waiting for transfers between devices, local(): kernel_full = lax.all_gather(conv_weight[0], 'dp', axis=0, tiled=True)  120 us
    unnamed x223, local copies, waits for them, and re-layouts  40.3 us
    mul x20, local copies, waits for them, and re-layouts, norm_backward(): result = inv_std * (grad_grouped - first_mean - hat_grouped * second_mean)  21.5 us
    dot_general x5, matrix products, local(): jnp.dot(columns, w_taps, preferred_element_type=jnp.float32)  11.2 us
  transfers between devices with their start and end apart: 9, of which 5 were waited for; matrix products, arithmetic and copies ran while one was open for 11% of the time, Pallas kernels for 0%

commit v1 on v0

v1 whole, which is shorter than its diff:
```python
import functools

import jax
import jax.numpy as jnp
import numpy as np
from jax import lax
from jax.experimental import pallas as pl
from jax.experimental.pallas import tpu as pltpu
from jax.sharding import Mesh, PartitionSpec as P

C = 256
F = 4
H = 8
W = 4
M = 2
HW = H * W
POS = M * F * HW
ROWS = 27 * C
NX, NZ, NYH = 4, 8, 2
PART = ROWS // (NX * NZ * NYH)
PAIR = NYH * PART
CHUNK = NZ * PAIR
HALF = CHUNK // 2
CLIPS = NX * NZ * NYH
BF = jnp.bfloat16
F32 = jnp.float32
HI = lax.Precision.HIGHEST
VMEM = pl.BlockSpec(memory_space=pltpu.VMEM)
SMEM = pl.BlockSpec(memory_space=pltpu.SMEM)
ANY = pl.BlockSpec(memory_space=pl.ANY)


def shift_matrices():
    s = np.zeros((9, C, C), np.float32)
    for kh in range(3):
        for kw in range(3):
            for h in range(H):
                for w in range(W):
                    h2, w2 = h - kh + 1, w - kw + 1
                    if 0 <= h2 < H and 0 <= w2 < W:
                        for f in range(C // HW):
                            s[kh * 3 + kw, f * HW + h * W + w, f * HW + h2 * W + w2] = 1
    return s


def group_matrix():
    c = np.arange(C) // 8
    return (c[:, None] == c[None, :]).astype(np.float32) / (8 * HW)


def spread(per_frame):
    frames = per_frame.shape[0]
    return jnp.broadcast_to(per_frame[:, None, :], (frames, HW, C)).reshape(frames * HW, C)


def frame_mean(value, group):
    sums = jnp.sum(value.reshape(-1, HW, C), axis=1)
    return jnp.dot(sums, group, precision=HI, preferred_element_type=F32)


def time_major(m, t):
    return (t * M + m) * HW


def plain(m, t):
    return (m * F + t) * HW


def forward_kernel(x_ref, gain_ref, shift_ref, group_ref, act_ref, xhat_ref, coef_ref, inv_ref, buf):
    for m in range(M):
        for t in range(F):
            buf[pl.ds(time_major(m, t), HW), :] = x_ref[pl.ds(plain(m, t), HW), :].astype(F32)
    group = group_ref[...]
    x = buf[...]
    centred = x - spread(frame_mean(x, group))
    inv = lax.rsqrt(frame_mean(centred * centred, group) + 1e-06)
    xhat = centred * spread(inv)
    gain = gain_ref[...]
    normed = xhat * gain + shift_ref[...]
    sig = jax.nn.sigmoid(normed)
    act_ref[...] = (normed * sig).astype(BF)
    xhat_ref[...] = xhat
    coef_ref[...] = sig * (1.0 + normed * (1.0 - sig)) * gain
    inv_ref[...] = inv


def forward(x, gain, shift, group):
    return pl.pallas_call(
        forward_kernel,
        out_shape=(
            jax.ShapeDtypeStruct((POS, C), BF),
            jax.ShapeDtypeStruct((POS, C), F32),
            jax.ShapeDtypeStruct((POS, C), F32),
            jax.ShapeDtypeStruct((POS // HW, C), F32),
        ),
        in_specs=[VMEM] * 4,
        out_specs=(VMEM,) * 4,
        scratch_shapes=[pltpu.VMEM((POS, C), F32)],
        compiler_params=pltpu.CompilerParams(vmem_limit_bytes=8 << 20),
        name="norm_forward",
    )(x, gain, shift, group)


def conv_kernel(
    flags, own, left, right, far_a, far_b, g_ref, s_ref, xhat_ref, coef_ref, inv_ref, group_ref,
    out_ref, kbuf, gs, sem,
):
    x = flags[0]
    pieces = (
        (own, x * CHUNK, CHUNK),
        (left, lax.rem(x + NX - 1, NX) * CHUNK, CHUNK),
        (right, lax.rem(x + 1, NX) * CHUNK, CHUNK),
        (far_a, lax.rem(x + 2, NX) * CHUNK, HALF),
        (far_b, lax.rem(x + 2, NX) * CHUNK + HALF, HALF),
    )
    copies = [
        pltpu.make_async_copy(ref, kbuf.at[pl.ds(pl.multiple_of(at, 32), rows), :], sem.at[i])
        for i, (ref, at, rows) in enumerate(pieces)
    ]
    for copy in copies:
        copy.start()
    g = g_ref[...]
    for j in range(9):
        gs[j, pl.ds(0, POS), :] = jnp.dot(
            s_ref[j], g, preferred_element_type=F32
        ).astype(BF)
        gs[j, pl.ds(POS, 2 * M * HW), :] = jnp.zeros((2 * M * HW, C), BF)
    for copy in copies:
        copy.wait()
    grad_act = None
    for kt in range(3):
        for j in range(9):
            term = lax.dot_general(
                gs[j, pl.ds((2 - kt) * M * HW, POS), :],
                kbuf[pl.ds((kt * 9 + j) * C, C), :],
                (((1,), (1,)), ((), ())),
                preferred_element_type=F32,
            )
            grad_act = term if grad_act is None else grad_act + term
    group = group_ref[...]
    xhat = xhat_ref[...]
    grad_hat = grad_act * coef_ref[...]
    first = spread(frame_mean(grad_hat, group))
    second = spread(frame_mean(grad_hat * xhat, group))
    out_ref[...] = (spread(inv_ref[...]) * (grad_hat - first - xhat * second)).astype(BF)


def conv_back(flags, pieces, g, s, xhat, coef, inv, group):
    return pl.pallas_call(
        conv_kernel,
        out_shape=jax.ShapeDtypeStruct((POS, C), BF),
        in_specs=[SMEM] + [ANY] * 5 + [VMEM] * 6,
        out_specs=VMEM,
        scratch_shapes=[
            pltpu.VMEM((ROWS, C), BF),
            pltpu.VMEM((9, POS + 2 * M * HW, C), BF),
            pltpu.SemaphoreType.DMA((5,)),
        ],
        compiler_params=pltpu.CompilerParams(vmem_limit_bytes=24 << 20),
        cost_estimate=pl.CostEstimate(flops=2 * POS * ROWS * C, bytes_accessed=2 * ROWS * C, transcendentals=0),
        name="conv_back",
    )(flags, *pieces, g, s, xhat, coef, inv, group)


def columns_kernel(flags, own, left, right, far_a, far_b, s_ref, at_ref, turned):
    blocks = ((own, 0), (own, 1), (left, 0), (left, 1), (right, 0), (right, 1), (far_a, None), (far_b, None))
    for t in range(2):
        turned[t] = jnp.zeros((C, C), BF)
    for t in range(F):
        rows = [
            ref[pl.ds(t * HW if m is None else time_major(m, t), HW), :] for ref, m in blocks
        ]
        turned[t + 2] = jnp.concatenate(rows, axis=0).astype(F32).T.astype(BF)
    first = lax.div(flags[0] * (CHUNK // 64), 4)
    for k in range(8):
        tap = jnp.minimum(first + k, 26)
        kt = lax.div(tap, 9)
        j = lax.rem(tap, 9)
        moved = s_ref[j]
        for t in range(F):
            at_ref[pl.ds(k * C, C), pl.ds(t * C, C)] = jnp.dot(
                turned[t + kt], moved, preferred_element_type=F32
            ).astype(BF)


def columns(flags, acts, s):
    return pl.pallas_call(
        columns_kernel,
        out_shape=jax.ShapeDtypeStruct((8 * C, F * C), BF),
        in_specs=[SMEM] + [VMEM] * 6,
        out_specs=VMEM,
        scratch_shapes=[pltpu.VMEM((F + 2, C, C), BF)],
        compiler_params=pltpu.CompilerParams(vmem_limit_bytes=24 << 20),
        name="act_columns",
    )(flags, *acts, s)


def weight_kernel(flags, at_ref, own, left, right, far_a, far_b, out_ref, part, gbuf, sem):
    x = flags[0]
    offset = lax.rem(x * (CHUNK // 64), 4) * 64
    steps = CHUNK // (2 * PAIR)
    copies = [
        pltpu.make_async_copy(
            at_ref.at[pl.ds(pl.multiple_of(offset + i * 2 * PAIR, 16), 2 * PAIR), :], part.at[i], sem.at[i]
        )
        for i in range(steps)
    ]
    for copy in copies:
        copy.start()
    blocks = ((own, 0), (own, 1), (left, 0), (left, 1), (right, 0), (right, 1), (far_a, None), (far_b, None))
    for t in range(F):
        for b, (ref, m) in enumerate(blocks):
            gbuf[pl.ds(t * C + b * HW, HW), :] = ref[pl.ds(t * HW if m is None else time_major(m, t), HW), :]
    for i in range(steps):
        copies[i].wait()
        total = jnp.dot(part[i], gbuf[...], preferred_element_type=F32)
        out_ref[2 * i] = total[:PAIR].astype(BF)
        out_ref[2 * i + 1] = total[PAIR:].astype(BF)


def weight_back(flags, at, grads):
    steps = CHUNK // (2 * PAIR)
    return pl.pallas_call(
        weight_kernel,
        out_shape=jax.ShapeDtypeStruct((NZ, PAIR, C), BF),
        in_specs=[SMEM, ANY] + [VMEM] * 5,
        out_specs=VMEM,
        scratch_shapes=[
            pltpu.VMEM((steps, 2 * PAIR, F * C), BF),
            pltpu.VMEM((F * C, C), BF),
            pltpu.SemaphoreType.DMA((steps,)),
        ],
        compiler_params=pltpu.CompilerParams(vmem_limit_bytes=16 << 20),
        cost_estimate=pl.CostEstimate(flops=2 * CHUNK * F * C * C, bytes_accessed=6 << 20, transcendentals=0),
        name="weight_back",
    )(flags, at, *grads)


def ring(axis, step):
    n = lax.axis_size(axis)
    return [(i, (i + step) % n) for i in range(n)]


def gather_x(block, first_half, second_half):
    left = lax.ppermute(block, "x", ring("x", 1))
    right = lax.ppermute(block, "x", ring("x", -1))
    far_a = lax.ppermute(first_half(left), "x", ring("x", 1))
    far_b = lax.ppermute(second_half(right), "x", ring("x", -1))
    return block, left, right, far_a, far_b


def to_time_major(value):
    return value.reshape(M, F, HW, C).transpose(1, 0, 2, 3).reshape(POS, C)


def halves_of_clip():
    def pick(m):
        return lambda b: b.reshape(F, M, HW, C)[:, m].reshape(F * HW, C)

    return pick(0), pick(1)


def local(section_inputs, top_grad, norm_gain, norm_shift, conv_weight):
    s = jnp.asarray(shift_matrices(), BF)
    group = jnp.asarray(group_matrix(), F32)
    x_at = lax.axis_index("x")
    yh = lax.axis_index("yh")
    section = lax.axis_index("yl") * 2 + lax.axis_index("c")
    flags = x_at.astype(jnp.int32).reshape(1)

    rows = conv_weight[0]
    other = lax.ppermute(rows, "yh", ring("yh", 1))
    pair = jnp.where(yh == 0, jnp.concatenate([rows, other]), jnp.concatenate([other, rows]))
    chunk = lax.all_to_all(
        jnp.broadcast_to(pair[None], (NZ, PAIR, C)), "z", 0, 0, tiled=True
    ).reshape(CHUNK, C)
    kernel_pieces = gather_x(chunk, lambda b: b[:HALF], lambda b: b[HALF:])

    act, xhat, coef, inv = forward(section_inputs.reshape(POS, C), norm_gain, norm_shift, group)
    at = columns(flags, gather_x(act, *halves_of_clip()), s)

    g = to_time_major(top_grad.reshape(POS, C))
    for k in range(3):
        sent = conv_back(flags, kernel_pieces, g, s, xhat, coef, inv, group)
        src, dst = 3 - k, 2 - k
        arrived = lax.ppermute(sent, ("yl", "c"), [(src, dst)])
        g = jnp.where(section == dst, arrived, g)
    grads = gather_x(g, *halves_of_clip())
    dx = conv_back(flags, kernel_pieces, g, s, xhat, coef, inv, group)

    partial = weight_back(flags, at, grads)
    summed = jnp.sum(lax.all_to_all(partial, "z", 0, 0, tiled=True).astype(F32), axis=0)
    low, high = summed[:PART], summed[PART:]
    arrived = lax.ppermute(jnp.where(yh == 0, high, low), "yh", ring("yh", 1))
    weight_part = (jnp.where(yh == 0, low, high) + arrived) * (1.0 / CLIPS)

    dx = dx.reshape(F, M, HW, C).transpose(1, 0, 2, 3).reshape(section_inputs.shape)
    return dx, weight_part[None]


def solution(mesh):
    fine = Mesh(mesh.devices.reshape(NX, NZ, NYH, 2, 2), ("x", "z", "yh", "yl", "c"))
    dp, pipe = ("x", "z", "yh"), ("yl", "c")
    placed = (
        P(pipe, dp, None, None, None, None, None),
        P(dp, None, None, None, None, None),
        P(pipe, None),
        P(pipe, None),
        P(pipe, dp, None),
    )
    return jax.shard_map(
        local,
        mesh=fine,
        in_specs=placed,
        out_specs=(P(pipe, dp, None, None, None, None, None), P(pipe, dp, None)),
        check_vma=False,
    )
```

time: 537 us -> 168 us (0.31); the launches traced: 528 us -> 166 us
  blocking collectives: 205 us -> 61.6 us
  waiting for transfers between devices: 130 us -> 24.2 us
  local copies, waits for them, and re-layouts: 103 us -> 21.2 us
  other arithmetic: 40.8 us -> 4.69 us
  Pallas kernels: 0 us -> 23.3 us
  matrix products: 17.2 us -> 0 us
  between operations: 16.6 us -> 0.96 us
  starting transfers between devices: 15.4 us -> 30 us
    unnamed x1 -> x0, blocking collectives: 205 us -> none
    all_gather x1 -> x0, waiting for transfers between devices: 120 us -> none  [local(): kernel_full = lax.all_gather(conv_weight[0], 'dp', axis=0, tiled=True)]
    all_to_all x0 -> x2, blocking collectives: none -> 61.6 us  [the longest x1 32.5 us: local(): lax.all_to_all(jnp.broadcast_to(pair[None], (NZ, PAIR, C)), 'z', 0, 0, ti...]
    unnamed x223 -> x50, local copies, waits for them, and re-layouts: 40.3 us -> 13.2 us
    ppermute x5 -> x17, starting transfers between devices: 6.58 us -> 30 us  [the longest x3 9.75 us: gather_x(): far_a = lax.ppermute(first_half(left), 'x', ring('x', 1))]
    pallas_call x0 -> x7, Pallas kernels: none -> 23.3 us  [the longest x4 16.2 us: conv_back(): pl.pallas_call(conv_kernel, out_shape=jax.ShapeDtypeStruct((POS, C), BF),...]
    mul x22 -> x0, local copies, waits for them, and re-layouts: 21.7 us -> none  [the longest x20 21.5 us: norm_backward(): result = inv_std * (grad_grouped - first_mean - hat_grouped * second_mean)]
    ppermute x5 -> x17, waiting for transfers between devices: 4.42 us -> 24.2 us  [the longest x3 16.3 us: gather_x(): right = lax.ppermute(block, 'x', ring('x', -1))]
  transfers between devices with their start and end apart: 9 -> 17, of which waited for: 5 -> 3; matrix products, arithmetic and copies ran while one was open for 11% -> 5% of each run, Pallas kernels for 0% -> 5%
where the time goes in v1:
time: 168 us; the launch traced here: 166 us
  blocking collectives  61.6 us (37%)
  starting transfers between devices  30 us (18%)
  waiting for transfers between devices  24.2 us (14%)
  Pallas kernels  23.3 us (14%)
  local copies, waits for them, and re-layouts  21.2 us (13%)
  other arithmetic  4.69 us (3%)
    all_to_all x1, blocking collectives, local(): lax.all_to_all(jnp.broadcast_to(pair[None], (NZ, PAIR, C)), 'z', 0, 0, ti...  32.5 us
    all_to_all x1, blocking collectives, local(): lax.all_to_all(partial, 'z', 0, 0, tiled=True).astype(F32)  29.1 us
    ppermute x3, waiting for transfers between devices, gather_x(): right = lax.ppermute(block, 'x', ring('x', -1))  16.3 us
    pallas_call x4, Pallas kernels, conv_back(): pl.pallas_call(conv_kernel, out_shape=jax.ShapeDtypeStruct((POS, C), BF),...  16.2 us
    unnamed x50, local copies, waits for them, and re-layouts  13.2 us
    ppermute x3, starting transfers between devices, gather_x(): far_a = lax.ppermute(first_half(left), 'x', ring('x', 1))  9.75 us
    ppermute x3, starting transfers between devices, gather_x(): left = lax.ppermute(block, 'x', ring('x', 1))  8.85 us
    ppermute x3, waiting for transfers between devices, local(): arrived = lax.ppermute(sent, ('yl', 'c'), [(src, dst)])  5.23 us
  transfers between devices with their start and end apart: 17, of which 3 were waited for; matrix products, arithmetic and copies ran while one was open for 5% of the time, Pallas kernels for 5%

profile of v1, /device:TPU:6, one launch (start us, length us, event | category | flops | bytes accessed | tf_op | source)
XLA Modules:
  0.0 166.0 jit_solution(12557939502657559146)
XLA Ops:
  0.6 3.3 %collective-permute-start = (bf16[108,256]{1,0:T(8,128)(2,1)}, bf16[108,256]{1,0:T(8,128)(2,1)S(1)}, u32[]{:S(2)}, u32[]{:S(2)}) collective-permute-start(bf16[108,256]{1,0:T(8,128)(2,1)} %bitcast.44), channel_id=1, source_target_pairs={{0,4},{4,0},{1,5},{5,1},{2,6},{6,2},{3,7},{7,3},{8,12},{12,8},{9,1... | collective-permute-start | bytes 165896 | tf_op jit(solution)/shard_map/ppermute | solution.py:272
  3.9 2.7 %collective-permute-done = bf16[108,256]{1,0:T(8,128)(2,1)S(1)} collective-permute-done((bf16[108,256]{1,0:T(8,128)(2,1)}, bf16[108,256]{1,0:T(8,128)(2,1)S(1)}, u32[]{:S(2)}, u32[]{:S(2)}) %collective-permute-start) | collective-permute-done | bytes 55328 | tf_op jit(solution)/shard_map/ppermute | solution.py:272
  7.7 32.5 %all_to_all.10 = bf16[8,216,256]{2,1,0:T(8,128)(2,1)S(1)} all-to-all(bf16[8,216,256]{2,1,0:T(8,128)(2,1)S(1)} %broadcast_in_dim.4), channel_id=1, replica_groups=mesh['x'=4,'z'=8,'yh'=2,'yl'=2,'c'=2] {'z'}, dimensions={0} | all-to-all | bytes 1769472 | tf_op jit(solution)/shard_map/all_to_all | solution.py:274
  41.0 2.4 %collective-permute-start.1 = (bf16[1728,256]{1,0:T(8,128)(2,1)S(1)}, bf16[1728,256]{1,0:T(8,128)(2,1)S(1)}, u32[]{:S(2)}, u32[]{:S(2)}) collective-permute-start(bf16[1728,256]{1,0:T(8,128)(2,1)S(1)} %bitcast.31), channel_id=1, source_target_pairs={{0,64},{64,128},{128,192},{192,0},{1,65},{65,129},{129,193},{193,1... | collective-permute-start | bytes 2654216 | tf_op jit(solution)/shard_map/ppermute | solution.py:245
  43.4 16.3 %collective-permute-done.2.right = bf16[1728,256]{1,0:T(8,128)(2,1)S(1)} collective-permute-done((bf16[1728,256]{1,0:T(8,128)(2,1)S(1)}, bf16[1728,256]{1,0:T(8,128)(2,1)S(1)}, u32[]{:S(2)}, u32[]{:S(2)}) %collective-permute-start.2) | collective-permute-done | bytes 884768 | tf_op jit(solution)/shard_map/ppermute | solution.py:246
  62.2 3.2 %collective-permute-start.3 = (bf16[864,256]{1,0:T(8,128)(2,1)}, bf16[864,256]{1,0:T(8,128)(2,1)}, u32[]{:S(2)}, u32[]{:S(2)}) collective-permute-start(bf16[864,256]{1,0:T(8,128)(2,1)} %slice.32), channel_id=1, source_target_pairs={{0,64},{64,128},{128,192},{192,0},{1,65},{65,129},{129,193},{193,1... | collective-permute-start | bytes 1327112 | tf_op jit(solution)/shard_map/ppermute | solution.py:247
  66.1 1.6 reshape_reshape.3
  70.5 1.5 norm_forward.1
  72.0 1.3 copy-done.2
  74.3 4.4 %conv_back.4 = bf16[256,256]{1,0:T(8,128)(2,1)} custom-call(s32[1]{0:T(128)} %bitcast.flags, bf16[1728,256]{1,0:T(8,128)(2,1)S(1)} %bitcast.32, bf16[1728,256]{1,0:T(8,128)(2,1)S(1)} %copy-done.2, bf16[1728,256]{1,0:T(8,128)(2,1)S(1)} %collective-permute-done.2.right, bf16[864,256]{1,0:T(8,128)(2,1)} %collective-permute-done.3.far_a, ...), custom_call_target="tpu_custom_call" | custom-call | flops 905969664 | bytes 3538944 | tf_op jit(solution)/shard_map/conv_back/pallas_call | solution.py:149
  78.7 1.3 collective-permute-start.5
  80.0 1.2 copy-done.3
  82.2 0.9 copy-done.12
  83.1 0.9 copy-done.16
  84.1 3.7 %conv_back.5 = bf16[256,256]{1,0:T(8,128)(2,1)S(1)} custom-call(s32[1]{0:T(128)} %bitcast.flags, bf16[1728,256]{1,0:T(8,128)(2,1)S(1)} %bitcast.33, bf16[1728,256]{1,0:T(8,128)(2,1)S(1)} %copy-done.3, bf16[1728,256]{1,0:T(8,128)(2,1)S(1)} %collective-permute-done.2.right, bf16[864,256]{1,0:T(8,128)(2,1)} %collective-permute-done.3.far_a, ...), custom_call_target="tpu_custom_call" | custom-call | flops 905969664 | bytes 3538944 | tf_op jit(solution)/shard_map/conv_back/pallas_call | solution.py:149
  87.8 1.3 collective-permute-start.6
  90.0 1.2 copy-done.4
  92.2 0.9 copy-done.13
  93.1 0.9 copy-done.17
  94.1 4.4 %conv_back.6 = bf16[256,256]{1,0:T(8,128)(2,1)} custom-call(s32[1]{0:T(128)} %bitcast.flags, bf16[1728,256]{1,0:T(8,128)(2,1)S(1)} %bitcast.34, bf16[1728,256]{1,0:T(8,128)(2,1)S(1)} %copy-done.4, bf16[1728,256]{1,0:T(8,128)(2,1)S(1)} %collective-permute-done.2.right, bf16[864,256]{1,0:T(8,128)(2,1)} %collective-permute-done.3.far_a, ...), custom_call_target="tpu_custom_call" | custom-call | flops 905969664 | bytes 3538944 | tf_op jit(solution)/shard_map/conv_back/pallas_call | solution.py:149
  98.4 1.3 collective-permute-start.7
  100.0 3.2 %collective-permute-start.8 = (bf16[256,256]{1,0:T(8,128)(2,1)}, bf16[256,256]{1,0:T(8,128)(2,1)}, u32[]{:S(2)}, u32[]{:S(2)}) collective-permute-start(bf16[256,256]{1,0:T(8,128)(2,1)} %get-tuple-element.9.own), channel_id=1, source_target_pairs={{0,64},{64,128},{128,192},{192,0},{1,65},{65,129},{129,193},{193,1... | collective-permute-start | bytes 393224 | tf_op jit(solution)/shard_map/ppermute | solution.py:245
  103.2 5.2 %collective-permute-done.7 = bf16[256,256]{1,0:T(8,128)(2,1)} collective-permute-done((bf16[256,256]{1,0:T(8,128)(2,1)}, bf16[256,256]{1,0:T(8,128)(2,1)}, u32[]{:S(2)}, u32[]{:S(2)}) %collective-permute-start.7) | collective-permute-done | bytes 131104 | tf_op jit(solution)/shard_map/ppermute | solution.py:286
  109.5 3.2 %collective-permute-start.12 = (bf16[256,256]{1,0:T(8,128)(2,1)S(1)}, bf16[256,256]{1,0:T(8,128)(2,1)S(1)}, u32[]{:S(2)}, u32[]{:S(2)}) collective-permute-start(bf16[256,256]{1,0:T(8,128)(2,1)S(1)} %broadcast_select_fusion.2.g_ref.own), channel_id=1, source_target_pairs={{0,64},{64,128},{128,192},{192,0},{1,65},{65,129},{129,193},{193,1... | collective-permute-start | bytes 393224 | tf_op jit(solution)/shard_map/ppermute | solution.py:245
  114.4 3.2 %collective-permute-start.10 = (bf16[128,256]{1,0:T(8,128)(2,1)S(1)}, bf16[128,256]{1,0:T(8,128)(2,1)S(1)}, u32[]{:S(2)}, u32[]{:S(2)}) collective-permute-start(bf16[128,256]{1,0:T(8,128)(2,1)S(1)} %bitcast.42), channel_id=1, source_target_pairs={{0,64},{64,128},{128,192},{192,0},{1,65},{65,129},{129,193},{193,1... | collective-permute-start | bytes 196616 | tf_op jit(solution)/shard_map/ppermute | solution.py:247
  117.7 3.3 %collective-permute-start.14 = (bf16[128,256]{1,0:T(8,128)(2,1)S(1)}, bf16[128,256]{1,0:T(8,128)(2,1)S(1)}, u32[]{:S(2)}, u32[]{:S(2)}) collective-permute-start(bf16[128,256]{1,0:T(8,128)(2,1)S(1)} %bitcast.43), channel_id=1, source_target_pairs={{0,64},{64,128},{128,192},{192,0},{1,65},{65,129},{129,193},{193,1... | collective-permute-start | bytes 196616 | tf_op jit(solution)/shard_map/ppermute | solution.py:247
  121.0 2.5 %act_columns.1.at_ref = bf16[2048,1024]{1,0:T(8,128)(2,1)S(1)} custom-call(s32[1]{0:T(128)} %bitcast.flags, bf16[256,256]{1,0:T(8,128)(2,1)} %get-tuple-element.9.own, bf16[256,256]{1,0:T(8,128)(2,1)} %collective-permute-done.8.left, bf16[256,256]{1,0:T(8,128)(2,1)} %collective-permute-done.9.right, bf16[128,256]{1,0:T(8,128)(2,1)S(1)} %collective-permute-done.10.far_a, ...), custom_call_target="tpu_custom_call" | custom-call | tf_op jit(solution)/shard_map/act_columns/pallas_call | solution.py:187
  123.5 3.2 %weight_back.1 = bf16[8,216,256]{2,1,0:T(8,128)(2,1)S(1)} custom-call(s32[1]{0:T(128)} %bitcast.flags, bf16[2048,1024]{1,0:T(8,128)(2,1)S(1)} %act_columns.1.at_ref, bf16[256,256]{1,0:T(8,128)(2,1)S(1)} %broadcast_select_fusion.2.g_ref.own, bf16[256,256]{1,0:T(8,128)(2,1)S(1)} %collective-permute-done.12.left, ...), custom_call_target="tpu_custom_call" | custom-call | flops 905969664 | bytes 6291456 | tf_op jit(solution)/shard_map/weight_back/pallas_call | solution.py:223
  126.8 29.1 %all_to_all.11 = bf16[8,216,256]{2,1,0:T(8,128)(2,1)S(1)} all-to-all(bf16[8,216,256]{2,1,0:T(8,128)(2,1)S(1)} %weight_back.1), channel_id=1, replica_groups=mesh['x'=4,'z'=8,'yh'=2,'yl'=2,'c'=2] {'z'}, dimensions={0} | all-to-all | bytes 1769472 | tf_op jit(solution)/shard_map/all_to_all | solution.py:292
  156.8 2.9 %collective-permute-start.16 = (f32[108,256]{1,0:T(8,128)}, f32[108,256]{1,0:T(8,128)}, u32[]{:S(2)}, u32[]{:S(2)}) collective-permute-start(f32[108,256]{1,0:T(8,128)} %slice_select_fusion), channel_id=1, source_target_pairs={{0,4},{4,0},{1,5},{5,1},{2,6},{6,2},{3,7},{7,3},{8,12},{12,8},{9,1... | collective-permute-start | bytes 331784 | tf_op jit(solution)/shard_map/ppermute | solution.py:294
  159.7 3.7 %conv_back.7 = bf16[256,256]{1,0:T(8,128)(2,1)S(1)} custom-call(s32[1]{0:T(128)} %bitcast.flags, bf16[1728,256]{1,0:T(8,128)(2,1)S(1)} %bitcast.35, bf16[1728,256]{1,0:T(8,128)(2,1)S(1)} %copy-done.5, bf16[1728,256]{1,0:T(8,128)(2,1)S(1)} %collective-permute-done.2.right, bf16[864,256]{1,0:T(8,128)(2,1)} %collective-permute-done.3.far_a, ...), custom_call_target="tpu_custom_call" | custom-call | flops 905969664 | bytes 3538944 | tf_op jit(solution)/shard_map/conv_back/pallas_call | solution.py:149
  164.2 1.0 add_multiply_fusion
  (81 shorter events, 17.1 us)
Async XLA Ops:
  0.6 6.0 %collective-permute-start = (bf16[108,256]{1,0:T(8,128)(2,1)}, bf16[108,256]{1,0:T(8,128)(2,1)S(1)}, u32[]{:S(2)}, u32[]{:S(2)}) collective-permute-start(bf16[108,256]{1,0:T(8,128)(2,1)} %bitcast.44), channel_id=1, source_target_pairs={{0,4},{4,0},{1,5},{5,1},{2,6},{6,2},{3,7},{7,3},{8,12},{12,8},{9,1... | collective-permute-start | bytes 165896 | tf_op jit(solution)/shard_map/ppermute | solution.py:272
  7.6 57.8 %copy-start.24 = (bf16[1,1,2,4,8,4,256]{6,5,4,3,2,1,0:T(4,128)(2,1)S(1)}, bf16[1,1,2,4,8,4,256]{6,5,4,3,2,1,0:T(4,128)(2,1)}, u32[]{:S(2)}) copy-start(bf16[1,1,2,4,8,4,256]{6,5,4,3,2,1,0:T(4,128)(2,1)} %param.7) | copy-start | bytes 393220
  7.6 61.0 %copy-start.21 = (f32[1,256]{1,0:T(1,128)S(1)}, f32[1,256]{1,0:T(1,128)}, u32[]{:S(2)}) copy-start(f32[1,256]{1,0:T(1,128)} %gain_ref.1) | copy-start | bytes 3076
  7.6 61.0 %copy-start.22 = (f32[1,256]{1,0:T(1,128)S(1)}, f32[1,256]{1,0:T(1,128)}, u32[]{:S(2)}) copy-start(f32[1,256]{1,0:T(1,128)} %shift_ref.1) | copy-start | bytes 3076
  40.1 31.9 %copy-start = (bf16[9,256,256]{2,1,0:T(8,128)(2,1)S(1)}, bf16[9,256,256]{2,1,0:T(8,128)(2,1)}, u32[]{:S(2)}) copy-start(bf16[9,256,256]{2,1,0:T(8,128)(2,1)} %constant.29.clone.s_ref) | copy-start | bytes 3538948
  40.1 19.5 %collective-permute-start.2 = (bf16[1728,256]{1,0:T(8,128)(2,1)S(1)}, bf16[1728,256]{1,0:T(8,128)(2,1)S(1)}, u32[]{:S(2)}, u32[]{:S(2)}) collective-permute-start(bf16[1728,256]{1,0:T(8,128)(2,1)S(1)} %bitcast.30), channel_id=1, source_target_pairs={{0,192},{64,0},{128,64},{192,128},{1,193},{65,1},{129,65},{193,129... | collective-permute-start | bytes 2654216 | tf_op jit(solution)/shard_map/ppermute | solution.py:246
  41.0 19.5 %collective-permute-start.1 = (bf16[1728,256]{1,0:T(8,128)(2,1)S(1)}, bf16[1728,256]{1,0:T(8,128)(2,1)S(1)}, u32[]{:S(2)}, u32[]{:S(2)}) collective-permute-start(bf16[1728,256]{1,0:T(8,128)(2,1)S(1)} %bitcast.31), channel_id=1, source_target_pairs={{0,64},{64,128},{128,192},{192,0},{1,65},{65,129},{129,193},{193,1... | collective-permute-start | bytes 2654216 | tf_op jit(solution)/shard_map/ppermute | solution.py:245
  60.4 11.5 %collective-permute-start.4 = (bf16[864,256]{1,0:T(8,128)(2,1)}, bf16[864,256]{1,0:T(8,128)(2,1)S(1)}, u32[]{:S(2)}, u32[]{:S(2)}) collective-permute-start(bf16[864,256]{1,0:T(8,128)(2,1)} %slice.33), channel_id=1, source_target_pairs={{0,192},{64,0},{128,64},{192,128},{1,193},{65,1},{129,65},{193,129... | collective-permute-start | bytes 1327112 | tf_op jit(solution)/shard_map/ppermute | solution.py:248
  62.2 9.8 %collective-permute-start.3 = (bf16[864,256]{1,0:T(8,128)(2,1)}, bf16[864,256]{1,0:T(8,128)(2,1)}, u32[]{:S(2)}, u32[]{:S(2)}) collective-permute-start(bf16[864,256]{1,0:T(8,128)(2,1)} %slice.32), channel_id=1, source_target_pairs={{0,64},{64,128},{128,192},{192,0},{1,65},{65,129},{129,193},{193,1... | collective-permute-start | bytes 1327112 | tf_op jit(solution)/shard_map/ppermute | solution.py:247
  68.6 1.0 copy-start.6
  72.0 6.7 %copy-start.11 = (f32[256,256]{1,0:T(8,128)}, f32[256,256]{1,0:T(8,128)S(1)}, u32[]{:S(2)}) copy-start(f32[256,256]{1,0:T(8,128)S(1)} %get-tuple-element.6.xhat_ref) | copy-start | bytes 786436
  72.0 6.7 %copy-start.15 = (f32[256,256]{1,0:T(8,128)}, f32[256,256]{1,0:T(8,128)S(1)}, u32[]{:S(2)}) copy-start(f32[256,256]{1,0:T(8,128)S(1)} %get-tuple-element.7.coef_ref) | copy-start | bytes 786436
  72.0 1.4 copy-start.2
  78.7 1.3 collective-permute-start.5
  80.0 1.2 copy-start.3
  84.1 3.7 %copy-start.19 = (bf16[256,256]{1,0:T(8,128)(2,1)}, bf16[256,256]{1,0:T(8,128)(2,1)S(1)}, u32[]{:S(2)}) copy-start(bf16[256,256]{1,0:T(8,128)(2,1)S(1)} %broadcast_select_fusion.g_ref) | copy-start | bytes 393220
  87.8 1.3 collective-permute-start.6
  90.0 1.2 copy-start.4
  98.4 10.0 %collective-permute-start.7 = (bf16[256,256]{1,0:T(8,128)(2,1)}, bf16[256,256]{1,0:T(8,128)(2,1)}, u32[]{:S(2)}, u32[]{:S(2)}) collective-permute-start(bf16[256,256]{1,0:T(8,128)(2,1)} %conv_back.6), channel_id=1, source_target_pairs={{1,0},{5,4},{9,8},{13,12},{17,16},{21,20},{25,24},{29,28},{33,32},... | collective-permute-start | bytes 393224 | tf_op jit(solution)/shard_map/ppermute | solution.py:286
  99.7 13.0 %collective-permute-start.9 = (bf16[256,256]{1,0:T(8,128)(2,1)}, bf16[256,256]{1,0:T(8,128)(2,1)}, u32[]{:S(2)}, u32[]{:S(2)}) collective-permute-start(bf16[256,256]{1,0:T(8,128)(2,1)} %get-tuple-element.9.own), channel_id=1, source_target_pairs={{0,192},{64,0},{128,64},{192,128},{1,193},{65,1},{129,65},{193,129... | collective-permute-start | bytes 393224 | tf_op jit(solution)/shard_map/ppermute | solution.py:246
  100.0 13.5 %collective-permute-start.8 = (bf16[256,256]{1,0:T(8,128)(2,1)}, bf16[256,256]{1,0:T(8,128)(2,1)}, u32[]{:S(2)}, u32[]{:S(2)}) collective-permute-start(bf16[256,256]{1,0:T(8,128)(2,1)} %get-tuple-element.9.own), channel_id=1, source_target_pairs={{0,64},{64,128},{128,192},{192,0},{1,65},{65,129},{129,193},{193,1... | collective-permute-start | bytes 393224 | tf_op jit(solution)/shard_map/ppermute | solution.py:245
  109.4 8.3 %collective-permute-start.13 = (bf16[256,256]{1,0:T(8,128)(2,1)S(1)}, bf16[256,256]{1,0:T(8,128)(2,1)S(1)}, u32[]{:S(2)}, u32[]{:S(2)}) collective-permute-start(bf16[256,256]{1,0:T(8,128)(2,1)S(1)} %broadcast_select_fusion.2.g_ref.own), channel_id=1, source_target_pairs={{0,192},{64,0},{128,64},{192,128},{1,193},{65,1},{129,65},{193,129... | collective-permute-start | bytes 393224 | tf_op jit(solution)/shard_map/ppermute | solution.py:246
  109.5 8.3 %collective-permute-start.12 = (bf16[256,256]{1,0:T(8,128)(2,1)S(1)}, bf16[256,256]{1,0:T(8,128)(2,1)S(1)}, u32[]{:S(2)}, u32[]{:S(2)}) collective-permute-start(bf16[256,256]{1,0:T(8,128)(2,1)S(1)} %broadcast_select_fusion.2.g_ref.own), channel_id=1, source_target_pairs={{0,64},{64,128},{128,192},{192,0},{1,65},{65,129},{129,193},{193,1... | collective-permute-start | bytes 393224 | tf_op jit(solution)/shard_map/ppermute | solution.py:245
  113.5 7.5 %collective-permute-start.11 = (bf16[128,256]{1,0:T(8,128)(2,1)S(1)}, bf16[128,256]{1,0:T(8,128)(2,1)S(1)}, u32[]{:S(2)}, u32[]{:S(2)}) collective-permute-start(bf16[128,256]{1,0:T(8,128)(2,1)S(1)} %bitcast.40), channel_id=1, source_target_pairs={{0,192},{64,0},{128,64},{192,128},{1,193},{65,1},{129,65},{193,129... | collective-permute-start | bytes 196616 | tf_op jit(solution)/shard_map/ppermute | solution.py:248
  114.4 6.6 %collective-permute-start.10 = (bf16[128,256]{1,0:T(8,128)(2,1)S(1)}, bf16[128,256]{1,0:T(8,128)(2,1)S(1)}, u32[]{:S(2)}, u32[]{:S(2)}) collective-permute-start(bf16[128,256]{1,0:T(8,128)(2,1)S(1)} %bitcast.42), channel_id=1, source_target_pairs={{0,64},{64,128},{128,192},{192,0},{1,65},{65,129},{129,193},{193,1... | collective-permute-start | bytes 196616 | tf_op jit(solution)/shard_map/ppermute | solution.py:247
  117.6 5.9 %collective-permute-start.15 = (bf16[128,256]{1,0:T(8,128)(2,1)S(1)}, bf16[128,256]{1,0:T(8,128)(2,1)S(1)}, u32[]{:S(2)}, u32[]{:S(2)}) collective-permute-start(bf16[128,256]{1,0:T(8,128)(2,1)S(1)} %bitcast.41), channel_id=1, source_target_pairs={{0,192},{64,0},{128,64},{192,128},{1,193},{65,1},{129,65},{193,129... | collective-permute-start | bytes 196616 | tf_op jit(solution)/shard_map/ppermute | solution.py:248
  117.7 5.8 %collective-permute-start.14 = (bf16[128,256]{1,0:T(8,128)(2,1)S(1)}, bf16[128,256]{1,0:T(8,128)(2,1)S(1)}, u32[]{:S(2)}, u32[]{:S(2)}) collective-permute-start(bf16[128,256]{1,0:T(8,128)(2,1)S(1)} %bitcast.43), channel_id=1, source_target_pairs={{0,64},{64,128},{128,192},{192,0},{1,65},{65,129},{129,193},{193,1... | collective-permute-start | bytes 196616 | tf_op jit(solution)/shard_map/ppermute | solution.py:247
  126.8 32.9 %copy-start.5 = (bf16[1728,256]{1,0:T(8,128)(2,1)S(1)}, bf16[1728,256]{1,0:T(8,128)(2,1)}, u32[]{:S(2)}) copy-start(bf16[1728,256]{1,0:T(8,128)(2,1)} %copy-done.1) | copy-start | bytes 2654212
  126.8 32.9 %copy-start.10 = (f32[256,256]{1,0:T(8,128)S(1)}, f32[256,256]{1,0:T(8,128)}, u32[]{:S(2)}) copy-start(f32[256,256]{1,0:T(8,128)} %constant.30.clone.group_ref) | copy-start | bytes 786436
  126.8 32.9 %copy-start.14 = (f32[256,256]{1,0:T(8,128)S(1)}, f32[256,256]{1,0:T(8,128)}, u32[]{:S(2)}) copy-start(f32[256,256]{1,0:T(8,128)} %copy-done.11) | copy-start | bytes 786436
  126.8 32.9 %copy-start.18 = (f32[256,256]{1,0:T(8,128)S(1)}, f32[256,256]{1,0:T(8,128)}, u32[]{:S(2)}) copy-start(f32[256,256]{1,0:T(8,128)} %copy-done.15) | copy-start | bytes 786436
  156.8 7.4 %collective-permute-start.16 = (f32[108,256]{1,0:T(8,128)}, f32[108,256]{1,0:T(8,128)}, u32[]{:S(2)}, u32[]{:S(2)}) collective-permute-start(f32[108,256]{1,0:T(8,128)} %slice_select_fusion), channel_id=1, source_target_pairs={{0,4},{4,0},{1,5},{5,1},{2,6},{6,2},{3,7},{7,3},{8,12},{12,8},{9,1... | collective-permute-start | bytes 331784 | tf_op jit(solution)/shard_map/ppermute | solution.py:294
  (10 other events, 9.2 us)

commit v2 on v1

v2 whole, which is shorter than its diff:
```python
import jax
import jax.numpy as jnp
import numpy as np
from jax import lax
from jax.experimental import pallas as pl
from jax.experimental.pallas import tpu as pltpu
from jax.sharding import Mesh, PartitionSpec as P

C = 256
F = 4
H = 8
W = 4
M = 2
HW = H * W
POS = M * F * HW
ROWS = 27 * C
NX, NZ, NYH = 4, 8, 2
N_PIPE = 4
PART = ROWS // (NX * NZ * NYH)
PAIR = NYH * PART
CHUNK = NZ * PAIR
HC = C // NYH
SLOTS = NZ * HC
CLIPS = NX * NZ * NYH
GRANT = 24 << 20
BF = jnp.bfloat16
F32 = jnp.float32
HI = lax.Precision.HIGHEST
VMEM = pl.BlockSpec(memory_space=pltpu.VMEM)
SMEM = pl.BlockSpec(memory_space=pltpu.SMEM)
HBM = pl.BlockSpec(memory_space=pltpu.HBM)


def shift_matrices():
    s = np.zeros((9, HC, HC), np.float32)
    for kh in range(3):
        for kw in range(3):
            for h in range(H):
                for w in range(W):
                    h2, w2 = h - kh + 1, w - kw + 1
                    if 0 <= h2 < H and 0 <= w2 < W:
                        for f in range(HC // HW):
                            s[kh * 3 + kw, f * HW + h * W + w, f * HW + h2 * W + w2] = 1
    return s


def group_matrix(channels):
    row = lax.div(lax.broadcasted_iota(jnp.int32, (channels, channels), 0), 8)
    column = lax.div(lax.broadcasted_iota(jnp.int32, (channels, channels), 1), 8)
    return jnp.where(row == column, 1.0 / (8 * HW), 0.0).astype(F32)


def spread(per_frame):
    frames, channels = per_frame.shape
    return jnp.broadcast_to(per_frame[:, None, :], (frames, HW, channels)).reshape(frames * HW, channels)


def frame_mean(value, group):
    sums = jnp.sum(value.reshape(-1, HW, value.shape[-1]), axis=1)
    return jnp.dot(sums, group, precision=HI, preferred_element_type=F32)


def time_major(m, t):
    return (t * M + m) * HW


def plain(m, t):
    return (m * F + t) * HW


def normalise(x, group):
    centred = x - spread(frame_mean(x, group))
    inv = lax.rsqrt(frame_mean(centred * centred, group) + 1e-06)
    return centred * spread(inv), inv


def forward_kernel(x_ref, gain_ref, shift_ref, act_ref, buf):
    for m in range(M):
        for t in range(F):
            buf[pl.ds(time_major(m, t), HW), :] = x_ref[pl.ds(plain(m, t), HW), :].astype(F32)
    xhat, _ = normalise(buf[...], group_matrix(C))
    normed = xhat * gain_ref[...] + shift_ref[...]
    act_ref[...] = (normed * jax.nn.sigmoid(normed)).astype(BF)


def forward(x, gain, shift):
    return pl.pallas_call(
        forward_kernel,
        out_shape=jax.ShapeDtypeStruct((POS, C), BF),
        in_specs=[VMEM] * 3,
        out_specs=VMEM,
        scratch_shapes=[pltpu.VMEM((POS, C), F32)],
        compiler_params=pltpu.CompilerParams(vmem_limit_bytes=GRANT),
        name="norm_forward",
    )(x, gain, shift)


def pair_row(k, m, t):
    return ((t * NYH + k) * M + m) * HW


def factors_kernel(flags, mine, theirs, gain_ref, shift_ref, out_ref, buf):
    first = flags[1] == 0
    for m in range(M):
        for t in range(F):
            a = mine[pl.ds(plain(m, t), HW), :].astype(F32)
            b = theirs[pl.ds(plain(m, t), HW), :].astype(F32)
            buf[pl.ds(pair_row(0, m, t), HW), :] = jnp.where(first, a, b)
            buf[pl.ds(pair_row(1, m, t), HW), :] = jnp.where(first, b, a)
    xhat, inv = normalise(buf[...], group_matrix(HC))
    gain = gain_ref[...]
    normed = xhat * gain + shift_ref[...]
    sig = jax.nn.sigmoid(normed)
    out_ref[0] = xhat
    out_ref[1] = sig * (1.0 + normed * (1.0 - sig)) * gain
    out_ref[2] = spread(inv)


def factors(flags, mine, theirs, gain, shift):
    return pl.pallas_call(
        factors_kernel,
        out_shape=jax.ShapeDtypeStruct((3, NYH * POS, HC), F32),
        in_specs=[SMEM] + [VMEM] * 4,
        out_specs=VMEM,
        scratch_shapes=[pltpu.VMEM((NYH * POS, HC), F32)],
        compiler_params=pltpu.CompilerParams(vmem_limit_bytes=GRANT),
        name="norm_factors",
    )(flags, mine, theirs, gain, shift)


def conv_kernel(
    flags, same, cross, s_ref, own, left, right, far_a, far_b, fac_ref,
    out_ref, kbuf, fac, gs, krows, sem,
):
    x = flags[0]
    yh = flags[1]
    rows = NYH * POS
    pieces = (
        (own, x * SLOTS, SLOTS),
        (left, lax.rem(x + NX - 1, NX) * SLOTS, SLOTS),
        (right, lax.rem(x + 1, NX) * SLOTS, SLOTS),
        (far_a, lax.rem(x + 2, NX) * SLOTS, SLOTS // 2),
        (far_b, lax.rem(x + 2, NX) * SLOTS + SLOTS // 2, SLOTS // 2),
    )
    later = [
        pltpu.make_async_copy(ref, kbuf.at[pl.ds(pl.multiple_of(at, HC), size), :], sem.at[i])
        for i, (ref, at, size) in enumerate(pieces)
    ]
    last = pltpu.make_async_copy(fac_ref, fac, sem.at[5])
    for copy in later + [last]:
        copy.start()
    kept, got = same[...], cross[...]
    g = jnp.concatenate([jnp.where(yh == 0, kept, got), jnp.where(yh == 0, got, kept)], axis=1)
    for j in range(9):
        for r in range(rows // HC):
            gs[pl.ds(r * HC, HC), pl.ds(j * C, C)] = jnp.dot(
                s_ref[j], g[r * HC : (r + 1) * HC], preferred_element_type=F32
            ).astype(BF)
    for copy in later:
        copy.wait()
    slot = lax.broadcasted_iota(jnp.int32, (HC, C), 0)
    for kt in range(3):
        for j in range(9):
            row = (kt * 9 + j) * C + yh * HC
            window = lax.div(row, PAIR)
            after = jnp.minimum(window + 1, NX * NZ - 1)
            here = kbuf[pl.ds(pl.multiple_of(window * HC, HC), HC), :]
            there = kbuf[pl.ds(pl.multiple_of(after * HC, HC), HC), :]
            krows[pl.ds(kt * HC, HC), pl.ds(j * C, C)] = jnp.where(
                slot < (window + 1) * PAIR - row, here, there
            )
    product = lax.dot_general(
        gs[...], krows[...], (((1,), (1,)), ((), ())), preferred_element_type=F32
    )
    frame = rows // F
    grad_act = product[:, 2 * HC :]
    for kt in range(2):
        ahead = (2 - kt) * frame
        part = product[ahead:, kt * HC : (kt + 1) * HC]
        grad_act = grad_act + jnp.concatenate([part, jnp.zeros((ahead, HC), F32)], axis=0)
    last.wait()
    xhat = fac[0]
    grad_hat = grad_act * fac[1]
    sums = jnp.concatenate(
        [jnp.sum(v.reshape(-1, HW, HC), axis=1) for v in (grad_hat, grad_hat * xhat)], axis=0
    )
    means = jnp.dot(sums, group_matrix(HC), precision=HI, preferred_element_type=F32)
    frames = rows // HW
    result = fac[2] * (grad_hat - spread(means[:frames]) - xhat * spread(means[frames:]))
    out_ref[...] = result.astype(BF)


def conv_back(flags, g, s, pieces, fac):
    rows = NYH * POS
    return pl.pallas_call(
        conv_kernel,
        out_shape=jax.ShapeDtypeStruct((rows, HC), BF),
        in_specs=[SMEM] + [VMEM] * 3 + [HBM] * 6,
        out_specs=VMEM,
        scratch_shapes=[
            pltpu.VMEM((NX * SLOTS, C), BF),
            pltpu.VMEM((3, rows, HC), F32),
            pltpu.VMEM((rows, 9 * C), BF),
            pltpu.VMEM((3 * HC, 9 * C), BF),
            pltpu.SemaphoreType.DMA((6,)),
        ],
        compiler_params=pltpu.CompilerParams(vmem_limit_bytes=GRANT),
        cost_estimate=pl.CostEstimate(flops=2 * POS * ROWS * C, bytes_accessed=ROWS * C, transcendentals=0),
        name="conv_back",
    )(flags, *g, s, *pieces, fac)


def columns_kernel(flags, own, left, right, far_a, far_b, s_ref, at_ref, turned):
    blocks = ((own, 0), (own, 1), (left, 0), (left, 1), (right, 0), (right, 1), (far_a, None), (far_b, None))
    for t in range(2):
        turned[t] = jnp.zeros((C, C), BF)
    for t in range(F):
        rows = [
            ref[pl.ds(t * HW if m is None else time_major(m, t), HW), :] for ref, m in blocks
        ]
        turned[t + 2] = jnp.concatenate(rows, axis=0).astype(F32).T.astype(BF)
    first = lax.div(flags[0] * (CHUNK // 64), 4)
    for k in range(8):
        tap = jnp.minimum(first + k, 26)
        kt = lax.div(tap, 9)
        j = lax.rem(tap, 9)
        moved = s_ref[j]
        for t in range(F):
            for r in range(C // HC):
                at_ref[pl.ds(k * C, C), pl.ds(t * C + r * HC, HC)] = jnp.dot(
                    turned[t + kt, :, pl.ds(r * HC, HC)], moved, preferred_element_type=F32
                ).astype(BF)


def columns(flags, acts, s):
    return pl.pallas_call(
        columns_kernel,
        out_shape=jax.ShapeDtypeStruct((8 * C, F * C), BF),
        in_specs=[SMEM] + [VMEM] * 6,
        out_specs=VMEM,
        scratch_shapes=[pltpu.VMEM((F + 2, C, C), BF)],
        compiler_params=pltpu.CompilerParams(vmem_limit_bytes=GRANT),
        name="act_columns",
    )(flags, *acts, s)


def weight_kernel(flags, at_ref, own, left, right, far_a, far_b, out_ref, gbuf):
    offset = lax.rem(flags[0] * (CHUNK // 64), 4) * 64
    blocks = ((own, 0), (own, 1), (left, 0), (left, 1), (right, 0), (right, 1), (far_a, None), (far_b, None))
    for t in range(F):
        for b, (ref, m) in enumerate(blocks):
            gbuf[pl.ds(t * C + b * HW, HW), :] = ref[pl.ds(t * HW if m is None else time_major(m, t), HW), :]
    for i in range(CHUNK // (2 * PAIR)):
        rows = at_ref[pl.ds(pl.multiple_of(offset + i * 2 * PAIR, 16), 2 * PAIR), :]
        total = jnp.dot(rows, gbuf[...], preferred_element_type=F32) * (1.0 / CLIPS)
        for k in range(4):
            out_ref[4 * i + k] = total[k * PART : (k + 1) * PART].astype(BF)


def weight_back(flags, at, grads):
    return pl.pallas_call(
        weight_kernel,
        out_shape=jax.ShapeDtypeStruct((NZ * NYH, PART, C), BF),
        in_specs=[SMEM] + [VMEM] * 6,
        out_specs=VMEM,
        scratch_shapes=[pltpu.VMEM((F * C, C), BF)],
        compiler_params=pltpu.CompilerParams(vmem_limit_bytes=GRANT),
        cost_estimate=pl.CostEstimate(flops=2 * CHUNK * F * C * C, bytes_accessed=6 << 20, transcendentals=0),
        name="weight_back",
    )(flags, at, *grads)


def ring(axis, step):
    n = lax.axis_size(axis)
    return [(i, (i + step) % n) for i in range(n)]


def gather_x(block, first_half, second_half, between=None):
    left = lax.ppermute(block, "x", ring("x", 1))
    right = lax.ppermute(block, "x", ring("x", -1))
    if between is not None:
        left, right, between = lax.optimization_barrier((left, right, between))
    far_a = lax.ppermute(first_half(left), "x", ring("x", 1))
    far_b = lax.ppermute(second_half(right), "x", ring("x", -1))
    blocks = (block, left, right, far_a, far_b)
    return blocks if between is None else (blocks, between)


def halves_of_clip():
    def pick(m):
        return lambda b: b.reshape(F, M, HW, C)[:, m].reshape(F * HW, C)

    return pick(0), pick(1)


def local(section_inputs, top_grad, norm_gain, norm_shift, conv_weight):
    s = jnp.asarray(shift_matrices(), BF)
    x_at = lax.axis_index("x")
    yh = lax.axis_index("yh")
    dp = (x_at * NZ + lax.axis_index("z")) * NYH + yh
    section = lax.axis_index("yl") * 2 + lax.axis_index("c")
    flags = jnp.stack([x_at, yh]).astype(jnp.int32)
    swap = ring("yh", 1)

    def mine(value, axis):
        return lax.dynamic_slice_in_dim(value, yh * HC, HC, axis)

    def theirs(value, axis):
        return lax.dynamic_slice_in_dim(value, (1 - yh) * HC, HC, axis)

    def in_order(kept, got, axis):
        return jnp.concatenate([jnp.where(yh == 0, kept, got), jnp.where(yh == 0, got, kept)], axis=axis)

    channel = lax.rem(dp * PART + lax.broadcasted_iota(jnp.int32, (C, PART), 1), C)
    place = (channel == lax.broadcasted_iota(jnp.int32, (C, PART), 0)).astype(BF)
    slots = jnp.dot(place, conv_weight[0], preferred_element_type=F32).astype(BF)
    window = mine(slots, 0) + lax.ppermute(theirs(slots, 0), "yh", swap)
    x_in = section_inputs.reshape(POS, C)
    act = forward(x_in, norm_gain, norm_shift)
    window, act = lax.optimization_barrier((window, act))
    chunk = lax.all_to_all(
        jnp.broadcast_to(window[None], (NZ, HC, C)), "z", 0, 0, tiled=True
    ).reshape(SLOTS, C)
    fac = factors(
        flags, mine(x_in, 1), lax.ppermute(theirs(x_in, 1), "yh", swap),
        mine(norm_gain, 1), mine(norm_shift, 1),
    )

    top = top_grad.reshape(M, F, HW, C).transpose(1, 0, 2, 3).reshape(F, 1, M * HW, C)
    both = in_order(top, lax.ppermute(top, "yh", swap), 1).reshape(NYH * POS, C)
    arrived = (mine(both, 1), theirs(both, 1))
    kernel_rows, (arrived, fac) = gather_x(
        chunk, lambda b: b[: SLOTS // 2], lambda b: b[SLOTS // 2 :], (arrived, fac)
    )
    own_g = top.reshape(POS, C)
    pair_dx = None
    for k in range(4):
        if k > 0:
            two = [lax.dynamic_index_in_dim(v.reshape(F, NYH, M * HW, HC), yh, 1, False) for v in arrived]
            own_g = jnp.where(section == 3 - k, in_order(*two, -1).reshape(POS, C), own_g)
        sent = conv_back(flags, arrived, s, kernel_rows, fac)
        if k == 0:
            sent, act = lax.optimization_barrier((sent, act))
            acts = gather_x(act, *halves_of_clip())
        pair_dx = sent if k == 0 else jnp.where(section == 3 - k, sent, pair_dx)
        if k < 3:
            src, dst = 3 - k, 2 - k
            cross = lax.ppermute(
                sent, ("yh", "yl", "c"), [(y * N_PIPE + src, (1 - y) * N_PIPE + dst) for y in range(NYH)]
            )
            arrived = (lax.ppermute(sent, ("yl", "c"), [(src, dst)]), cross)

    own_g, acts = lax.optimization_barrier((own_g, acts))
    at = columns(flags, acts, s)
    partial = weight_back(flags, at, gather_x(own_g, *halves_of_clip()))
    weight_part = jnp.sum(lax.all_to_all(partial, ("z", "yh"), 0, 0, tiled=True).astype(F32), axis=0)

    pair_dx = pair_dx.reshape(F, NYH, M, HW, HC)
    kept = lax.dynamic_index_in_dim(pair_dx, yh, 1, False)
    got = lax.ppermute(lax.dynamic_index_in_dim(pair_dx, 1 - yh, 1, False), "yh", swap)
    dx = in_order(kept, got, -1).transpose(1, 0, 2, 3).reshape(section_inputs.shape)
    return dx, weight_part[None]


def solution(mesh):
    fine = Mesh(mesh.devices.reshape(NX, NZ, NYH, 2, 2), ("x", "z", "yh", "yl", "c"))
    dp, pipe = ("x", "z", "yh"), ("yl", "c")
    placed = (
        P(pipe, dp, None, None, None, None, None),
        P(dp, None, None, None, None, None),
        P(pipe, None),
        P(pipe, None),
        P(pipe, dp, None),
    )
    return jax.shard_map(
        local,
        mesh=fine,
        in_specs=placed,
        out_specs=(P(pipe, dp, None, None, None, None, None), P(pipe, dp, None)),
        check_vma=False,
    )
```

time: 168 us -> 136 us (0.81)
  blocking collectives: 61.6 us -> 0 us
  waiting for transfers between devices: 24.2 us -> 48.1 us
  starting transfers between devices: 30 us -> 49.6 us
  local copies, waits for them, and re-layouts: 21.2 us -> 11.6 us
  Pallas kernels: 23.3 us -> 20.7 us
    all_to_all x2 -> x0, blocking collectives: 61.6 us -> none  [the longest x1 32.5 us: local(): lax.all_to_all(jnp.broadcast_to(pair[None], (NZ, PAIR, C)), 'z', 0, 0, ti...]
    all_to_all x0 -> x2, waiting for transfers between devices: none -> 24.4 us  [the longest x1 12.5 us: local(): lax.all_to_all(partial, ('z', 'yh'), 0, 0, tiled=True).astype(F32)]
    all_to_all x0 -> x2, starting transfers between devices: none -> 13 us  [the longest x1 8.47 us: local(): lax.all_to_all(jnp.broadcast_to(window[None], (NZ, HC, C)), 'z', 0, 0, ti...]
    unnamed x50 -> x29, local copies, waits for them, and re-layouts: 13.2 us -> 5.57 us
    ppermute x5 -> x10, starting transfers between devices: 10.1 us -> 16.7 us  [the longest x3 3.28 us: local(): lax.ppermute(sent, ('yh', 'yl', 'c'), [(y * N_PIPE + src, (1 - y) * N_PIP...]
    ppermute x3, waiting for transfers between devices: 0.01 us -> 4.36 us  [gather_x(): far_b = lax.ppermute(second_half(right), 'x', ring('x', -1))]
    ppermute x3, waiting for transfers between devices: 16.3 us -> 12.5 us  [gather_x(): right = lax.ppermute(block, 'x', ring('x', -1))]
    pallas_call x6 -> x7, Pallas kernels: 20.9 us -> 18.2 us  [the longest x4 14 us: conv_back(): pl.pallas_call(conv_kernel, out_shape=jax.ShapeDtypeStruct((rows, HC), BF...]
  transfers between devices with their start and end apart: 17 -> 24, of which waited for: 3 -> 7; matrix products, arithmetic and copies ran while one was open for 5% -> 5% of each run, Pallas kernels for 5% -> 12%
where the time goes in v2:
time: 136 us; the launch traced here: 135 us
  starting transfers between devices  49.6 us (36%)
  waiting for transfers between devices  48.1 us (35%)
  Pallas kernels  20.7 us (15%)
  local copies, waits for them, and re-layouts  11.6 us (9%)
  other arithmetic  3.46 us (3%)
    pallas_call x4, Pallas kernels, conv_back(): pl.pallas_call(conv_kernel, out_shape=jax.ShapeDtypeStruct((rows, HC), BF...  14 us
    all_to_all x1, waiting for transfers between devices, local(): lax.all_to_all(partial, ('z', 'yh'), 0, 0, tiled=True).astype(F32)  12.5 us
    ppermute x3, waiting for transfers between devices, gather_x(): right = lax.ppermute(block, 'x', ring('x', -1))  12.5 us
    all_to_all x1, waiting for transfers between devices, local(): lax.all_to_all(jnp.broadcast_to(window[None], (NZ, HC, C)), 'z', 0, 0, ti...  11.9 us
    ppermute x3, starting transfers between devices, gather_x(): far_a = lax.ppermute(first_half(left), 'x', ring('x', 1))  9.74 us
    all_to_all x1, starting transfers between devices, local(): lax.all_to_all(jnp.broadcast_to(window[None], (NZ, HC, C)), 'z', 0, 0, ti...  8.47 us
    ppermute x3, starting transfers between devices, gather_x(): left = lax.ppermute(block, 'x', ring('x', 1))  8 us
    unnamed x29, local copies, waits for them, and re-layouts  5.57 us
  transfers between devices with their start and end apart: 24, of which 7 were waited for; matrix products, arithmetic and copies ran while one was open for 5% of the time, Pallas kernels for 12%

profile of v2, /device:TPU:6, one launch (start us, length us, event | category | flops | bytes accessed | tf_op | source)
XLA Modules:
  0.0 134.6 jit_solution(6432609618805374791)
XLA Ops:
  1.7 3.3 %collective-permute-start = (bf16[128,256]{1,0:T(8,128)(2,1)S(1)}, bf16[128,256]{1,0:T(8,128)(2,1)S(1)}, u32[]{:S(2)}, u32[]{:S(2)}) collective-permute-start(bf16[128,256]{1,0:T(8,128)(2,1)S(1)} %constant_dynamic-slice_fusion.6), channel_id=1, source_target_pairs={{0,4},{4,0},{1,5},{5,1},{2,6},{6,2},{3,7},{7,3},{8,12},{12,8},{9,1... | collective-permute-start | bytes 196616 | tf_op jit(solution)/shard_map/ppermute | solution.py:317
  7.2 1.4 %norm_forward.1.own = bf16[256,256]{1,0:T(8,128)(2,1)} custom-call(bf16[256,256]{1,0:T(8,128)(2,1)S(1)} %reshape.89.x_ref, f32[1,256]{1,0:T(1,128)S(1)} %copy-done.11, f32[1,256]{1,0:T(1,128)S(1)} %copy-done.10), custom_call_target="tpu_custom_call" | custom-call | tf_op jit(solution)/shard_map/norm_forward/pallas_call | solution.py:87
  9.5 8.5 %all-to-all-start = ((bf16[8,128,256]{2,1,0:T(8,128)(2,1)}), bf16[8,128,256]{2,1,0:T(8,128)(2,1)S(1)}, u32[]{:S(2)}, u32[]{:S(2)}) async-start(bf16[8,128,256]{2,1,0:T(8,128)(2,1)} %broadcast_in_dim.4), calls=%async_computation | async-start | bytes 1048576 | tf_op jit(solution)/shard_map/all_to_all | solution.py:321
  18.0 2.1 %collective-permute-start.4 = (bf16[256,128]{1,0:T(8,128)(2,1)S(1)}, bf16[256,128]{1,0:T(8,128)(2,1)S(1)}, u32[]{:S(2)}, u32[]{:S(2)}) collective-permute-start(bf16[256,128]{1,0:T(8,128)(2,1)S(1)} %get-tuple-element.46), channel_id=1, source_target_pairs={{0,4},{4,0},{1,5},{5,1},{2,6},{6,2},{3,7},{7,3},{8,12},{12,8},{9,1... | collective-permute-start | bytes 196616 | tf_op jit(solution)/shard_map/ppermute | solution.py:325
  21.1 1.6 %collective-permute-start.3 = (bf16[4,1,64,256]{3,2,1,0:T(8,128)(2,1)S(1)}, bf16[4,1,64,256]{3,2,1,0:T(8,128)(2,1)S(1)}, u32[]{:S(2)}, u32[]{:S(2)}) collective-permute-start(bf16[4,1,64,256]{3,2,1,0:T(8,128)(2,1)S(1)} %bitcast.91), channel_id=1, source_target_pairs={{0,4},{4,0},{1,5},{5,1},{2,6},{6,2},{3,7},{7,3},{8,12},{12,8},{9,1... | collective-permute-start | bytes 393224 | tf_op jit(solution)/shard_map/ppermute | solution.py:330
  23.4 11.9 %all-to-all-done = bf16[8,128,256]{2,1,0:T(8,128)(2,1)S(1)} async-done(((bf16[8,128,256]{2,1,0:T(8,128)(2,1)}), bf16[8,128,256]{2,1,0:T(8,128)(2,1)S(1)}, u32[]{:S(2)}, u32[]{:S(2)}) %all-to-all-start) | async-done | bytes 524320 | tf_op jit(solution)/shard_map/all_to_all | solution.py:321
  36.0 2.4 %collective-permute-start.1 = (bf16[1024,256]{1,0:T(8,128)(2,1)S(1)}, bf16[1024,256]{1,0:T(8,128)(2,1)S(1)}, u32[]{:S(2)}, u32[]{:S(2)}) collective-permute-start(bf16[1024,256]{1,0:T(8,128)(2,1)S(1)} %bitcast.80), channel_id=1, source_target_pairs={{0,64},{64,128},{128,192},{192,0},{1,65},{65,129},{129,193},{193,1... | collective-permute-start | bytes 1572872 | tf_op jit(solution)/shard_map/ppermute | solution.py:279
  39.8 9.5 %collective-permute-done.2.right = bf16[1024,256]{1,0:T(8,128)(2,1)S(1)} collective-permute-done((bf16[1024,256]{1,0:T(8,128)(2,1)S(1)}, bf16[1024,256]{1,0:T(8,128)(2,1)S(1)}, u32[]{:S(2)}, u32[]{:S(2)}) %collective-permute-start.2) | collective-permute-done | bytes 524320 | tf_op jit(solution)/shard_map/ppermute | solution.py:280
  49.5 3.2 %collective-permute-start.5 = (bf16[512,256]{1,0:T(8,128)(2,1)S(1)}, bf16[512,256]{1,0:T(8,128)(2,1)S(1)}, u32[]{:S(2)}, u32[]{:S(2)}) collective-permute-start(bf16[512,256]{1,0:T(8,128)(2,1)S(1)} %slice.18), channel_id=1, source_target_pairs={{0,64},{64,128},{128,192},{192,0},{1,65},{65,129},{129,193},{193,1... | collective-permute-start | bytes 786440 | tf_op jit(solution)/shard_map/ppermute | solution.py:283
  52.7 4.4 %collective-permute-done.6.far_b = bf16[512,256]{1,0:T(8,128)(2,1)S(1)} collective-permute-done((bf16[512,256]{1,0:T(8,128)(2,1)S(1)}, bf16[512,256]{1,0:T(8,128)(2,1)S(1)}, u32[]{:S(2)}, u32[]{:S(2)}) %collective-permute-start.6) | collective-permute-done | bytes 262176 | tf_op jit(solution)/shard_map/ppermute | solution.py:284
  57.1 3.4 %conv_back.4 = bf16[512,128]{1,0:T(8,128)(2,1)S(1)} custom-call(s32[2]{0:T(128)S(1)} %pad_add_fusion.flags, bf16[512,128]{1,0:T(8,128)(2,1)S(1)} %get-tuple-element.18.same, bf16[512,128]{1,0:T(8,128)(2,1)S(1)} %get-tuple-element.19.cross, bf16[9,128,128]{2,1,0:T(8,128)(2,1)S(1)} %copy-done.1, bf16[1024,256]{1,0:T(8,128)(2,1)S(1)} %bitcast.81, ...), custom_call_target="tpu_custom_call" | custom-call | flops 905969664 | bytes 1769472 | tf_op jit(solution)/shard_map/conv_back/pallas_call | solution.py:195
  61.8 1.2 collective-permute-start.15
  63.0 2.4 %collective-permute-start.14 = (bf16[256,256]{1,0:T(8,128)(2,1)}, bf16[256,256]{1,0:T(8,128)(2,1)}, u32[]{:S(2)}, u32[]{:S(2)}) collective-permute-start(bf16[256,256]{1,0:T(8,128)(2,1)} %norm_forward.1.own), channel_id=1, source_target_pairs={{0,64},{64,128},{128,192},{192,0},{1,65},{65,129},{129,193},{193,1... | collective-permute-start | bytes 393224 | tf_op jit(solution)/shard_map/ppermute | solution.py:279
  65.4 3.4 %conv_back.5 = bf16[512,128]{1,0:T(8,128)(2,1)S(1)} custom-call(s32[2]{0:T(128)S(1)} %pad_add_fusion.flags, bf16[512,128]{1,0:T(8,128)(2,1)S(1)} %collective-permute-done.7.same, bf16[512,128]{1,0:T(8,128)(2,1)S(1)} %collective-permute-done.8.cross, bf16[9,128,128]{2,1,0:T(8,128)(2,1)S(1)} %copy-done.1, bf16[1024,256]{1,0:T(8,128)(2,1)S(1)} %bitcast.82, ...), custom_call_target="tpu_custom_call" | custom-call | flops 905969664 | bytes 1769472 | tf_op jit(solution)/shard_map/conv_back/pallas_call | solution.py:195
  68.8 1.3 collective-permute-start.10
  70.2 1.3 collective-permute-start.9
  73.2 3.2 %collective-permute-start.16 = (bf16[128,256]{1,0:T(8,128)(2,1)S(1)}, bf16[128,256]{1,0:T(8,128)(2,1)S(1)}, u32[]{:S(2)}, u32[]{:S(2)}) collective-permute-start(bf16[128,256]{1,0:T(8,128)(2,1)S(1)} %bitcast.103), channel_id=1, source_target_pairs={{0,64},{64,128},{128,192},{192,0},{1,65},{65,129},{129,193},{193,1... | collective-permute-start | bytes 196616 | tf_op jit(solution)/shard_map/ppermute | solution.py:283
  76.4 3.8 %conv_back.6 = bf16[512,128]{1,0:T(8,128)(2,1)S(1)} custom-call(s32[2]{0:T(128)S(1)} %pad_add_fusion.flags, bf16[512,128]{1,0:T(8,128)(2,1)} %collective-permute-done.9.same, bf16[512,128]{1,0:T(8,128)(2,1)} %collective-permute-done.10.cross, bf16[9,128,128]{2,1,0:T(8,128)(2,1)S(1)} %copy-done.1, bf16[1024,256]{1,0:T(8,128)(2,1)S(1)} %bitcast.83, ...), custom_call_target="tpu_custom_call" | custom-call | flops 905969664 | bytes 1769472 | tf_op jit(solution)/shard_map/conv_back/pallas_call | solution.py:195
  80.3 1.3 collective-permute-start.12
  81.6 1.3 collective-permute-start.11
  84.7 3.4 %collective-permute-done.12.cross = bf16[512,128]{1,0:T(8,128)(2,1)S(1)} collective-permute-done((bf16[512,128]{1,0:T(8,128)(2,1)S(1)}, bf16[512,128]{1,0:T(8,128)(2,1)S(1)}, u32[]{:S(2)}, u32[]{:S(2)}) %collective-permute-start.12) | collective-permute-done | bytes 131104 | tf_op jit(solution)/shard_map/ppermute | solution.py:348
  88.3 3.2 %collective-permute-start.18 = (bf16[256,256]{1,0:T(8,128)(2,1)S(1)}, bf16[256,256]{1,0:T(8,128)(2,1)S(1)}, u32[]{:S(2)}, u32[]{:S(2)}) collective-permute-start(bf16[256,256]{1,0:T(8,128)(2,1)S(1)} %maximum_select_fusion.own), channel_id=1, source_target_pairs={{0,64},{64,128},{128,192},{192,0},{1,65},{65,129},{129,193},{193,1... | collective-permute-start | bytes 393224 | tf_op jit(solution)/shard_map/ppermute | solution.py:279
  91.5 2.9 %collective-permute-done.19.right = bf16[256,256]{1,0:T(8,128)(2,1)S(1)} collective-permute-done((bf16[256,256]{1,0:T(8,128)(2,1)S(1)}, bf16[256,256]{1,0:T(8,128)(2,1)S(1)}, u32[]{:S(2)}, u32[]{:S(2)}) %collective-permute-start.19) | collective-permute-done | bytes 131104 | tf_op jit(solution)/shard_map/ppermute | solution.py:280
  94.6 3.3 %collective-permute-start.20 = (bf16[128,256]{1,0:T(8,128)(2,1)S(1)}, bf16[128,256]{1,0:T(8,128)(2,1)S(1)}, u32[]{:S(2)}, u32[]{:S(2)}) collective-permute-start(bf16[128,256]{1,0:T(8,128)(2,1)S(1)} %bitcast.105), channel_id=1, source_target_pairs={{0,64},{64,128},{128,192},{192,0},{1,65},{65,129},{129,193},{193,1... | collective-permute-start | bytes 196616 | tf_op jit(solution)/shard_map/ppermute | solution.py:283
  97.8 2.5 %act_columns.1.at_ref = bf16[2048,1024]{1,0:T(8,128)(2,1)S(1)} custom-call(s32[2]{0:T(128)S(1)} %pad_add_fusion.flags, bf16[256,256]{1,0:T(8,128)(2,1)} %norm_forward.1.own, bf16[256,256]{1,0:T(8,128)(2,1)} %collective-permute-done.14.left, bf16[256,256]{1,0:T(8,128)(2,1)} %collective-permute-done.15.right, ...), custom_call_target="tpu_custom_call" | custom-call | tf_op jit(solution)/shard_map/act_columns/pallas_call | solution.py:236
  100.3 1.6 %weight_back.1 = bf16[16,108,256]{2,1,0:T(8,128)(2,1)S(1)} custom-call(s32[2]{0:T(128)S(1)} %pad_add_fusion.flags, bf16[2048,1024]{1,0:T(8,128)(2,1)S(1)} %act_columns.1.at_ref, bf16[256,256]{1,0:T(8,128)(2,1)S(1)} %maximum_select_fusion.own, bf16[256,256]{1,0:T(8,128)(2,1)S(1)} %collective-permute-done.18.left, ...), custom_call_target="tpu_custom_call" | custom-call | flops 905969664 | bytes 6291456 | tf_op jit(solution)/shard_map/weight_back/pallas_call | solution.py:261
  102.9 4.5 %all-to-all-start.1 = ((bf16[16,108,256]{2,1,0:T(8,128)(2,1)}), bf16[16,108,256]{2,1,0:T(8,128)(2,1)}, u32[]{:S(2)}, u32[]{:S(2)}) async-start(bf16[16,108,256]{2,1,0:T(8,128)(2,1)} %copy-done.2), calls=%async_computation.1 | async-start | bytes 1835008 | tf_op jit(solution)/shard_map/all_to_all | solution.py:356
  109.3 3.4 %conv_back.7 = bf16[512,128]{1,0:T(8,128)(2,1)S(1)} custom-call(s32[2]{0:T(128)S(1)} %pad_add_fusion.flags, bf16[512,128]{1,0:T(8,128)(2,1)S(1)} %copy-done.7, bf16[512,128]{1,0:T(8,128)(2,1)S(1)} %copy-done.5, bf16[9,128,128]{2,1,0:T(8,128)(2,1)S(1)} %copy-done.1, bf16[1024,256]{1,0:T(8,128)(2,1)S(1)} %bitcast.84, ...), custom_call_target="tpu_custom_call" | custom-call | flops 905969664 | bytes 1769472 | tf_op jit(solution)/shard_map/conv_back/pallas_call | solution.py:195
  112.7 3.1 %collective-permute-start.13 = (bf16[4,2,32,128]{3,2,1,0:T(8,128)(2,1)S(1)}, bf16[4,2,32,128]{3,2,1,0:T(8,128)(2,1)S(1)}, u32[]{:S(2)}, u32[]{:S(2)}) collective-permute-start(bf16[4,2,32,128]{3,2,1,0:T(8,128)(2,1)S(1)} %dynamic-slice_bitcast_fusion), channel_id=1, source_target_pairs={{0,4},{4,0},{1,5},{5,1},{2,6},{6,2},{3,7},{7,3},{8,12},{12,8},{9,1... | collective-permute-start | bytes 196616 | tf_op jit(solution)/shard_map/ppermute | solution.py:360
  115.8 3.5 %collective-permute-done.13 = bf16[4,2,32,128]{3,2,1,0:T(8,128)(2,1)S(1)} collective-permute-done((bf16[4,2,32,128]{3,2,1,0:T(8,128)(2,1)S(1)}, bf16[4,2,32,128]{3,2,1,0:T(8,128)(2,1)S(1)}, u32[]{:S(2)}, u32[]{:S(2)}) %collective-permute-start.13) | collective-permute-done | bytes 65568 | tf_op jit(solution)/shard_map/ppermute | solution.py:360
  120.1 12.5 %all-to-all-done.1 = bf16[16,108,256]{2,1,0:T(8,128)(2,1)} async-done(((bf16[16,108,256]{2,1,0:T(8,128)(2,1)}), bf16[16,108,256]{2,1,0:T(8,128)(2,1)}, u32[]{:S(2)}, u32[]{:S(2)}) %all-to-all-start.1) | async-done | bytes 884768 | tf_op jit(solution)/shard_map/all_to_all | solution.py:356
  132.6 1.3 convert_reduce_fusion
  (85 shorter events, 17.4 us)
Async XLA Ops:
  0.6 56.4 %copy-start.1 = (bf16[9,128,128]{2,1,0:T(8,128)(2,1)S(1)}, bf16[9,128,128]{2,1,0:T(8,128)(2,1)}, u32[]{:S(2)}) copy-start(bf16[9,128,128]{2,1,0:T(8,128)(2,1)} %constant.63.clone.s_ref) | copy-start | bytes 884740
  1.7 7.0 %collective-permute-start = (bf16[128,256]{1,0:T(8,128)(2,1)S(1)}, bf16[128,256]{1,0:T(8,128)(2,1)S(1)}, u32[]{:S(2)}, u32[]{:S(2)}) collective-permute-start(bf16[128,256]{1,0:T(8,128)(2,1)S(1)} %constant_dynamic-slice_fusion.6), channel_id=1, source_target_pairs={{0,4},{4,0},{1,5},{5,1},{2,6},{6,2},{3,7},{7,3},{8,12},{12,8},{9,1... | collective-permute-start | bytes 196616 | tf_op jit(solution)/shard_map/ppermute | solution.py:317
  9.5 25.7 %all-to-all-start = ((bf16[8,128,256]{2,1,0:T(8,128)(2,1)}), bf16[8,128,256]{2,1,0:T(8,128)(2,1)S(1)}, u32[]{:S(2)}, u32[]{:S(2)}) async-start(bf16[8,128,256]{2,1,0:T(8,128)(2,1)} %broadcast_in_dim.4), calls=%async_computation | async-start | bytes 1048576 | tf_op jit(solution)/shard_map/all_to_all | solution.py:321
  18.0 20.5 %collective-permute-start.4 = (bf16[256,128]{1,0:T(8,128)(2,1)S(1)}, bf16[256,128]{1,0:T(8,128)(2,1)S(1)}, u32[]{:S(2)}, u32[]{:S(2)}) collective-permute-start(bf16[256,128]{1,0:T(8,128)(2,1)S(1)} %get-tuple-element.46), channel_id=1, source_target_pairs={{0,4},{4,0},{1,5},{5,1},{2,6},{6,2},{3,7},{7,3},{8,12},{12,8},{9,1... | collective-permute-start | bytes 196616 | tf_op jit(solution)/shard_map/ppermute | solution.py:325
  21.1 28.3 %copy-start.12 = (bf16[2,4,32,256]{3,2,0,1:T(8,128)(2,1)}, bf16[2,4,32,256]{3,2,0,1:T(8,128)(2,1)S(1)}, u32[]{:S(2)}) copy-start(bf16[2,4,32,256]{3,2,0,1:T(8,128)(2,1)S(1)} %copy.22) | copy-start | bytes 393220
  21.1 18.6 %collective-permute-start.3 = (bf16[4,1,64,256]{3,2,1,0:T(8,128)(2,1)S(1)}, bf16[4,1,64,256]{3,2,1,0:T(8,128)(2,1)S(1)}, u32[]{:S(2)}, u32[]{:S(2)}) collective-permute-start(bf16[4,1,64,256]{3,2,1,0:T(8,128)(2,1)S(1)} %bitcast.91), channel_id=1, source_target_pairs={{0,4},{4,0},{1,5},{5,1},{2,6},{6,2},{3,7},{7,3},{8,12},{12,8},{9,1... | collective-permute-start | bytes 393224 | tf_op jit(solution)/shard_map/ppermute | solution.py:330
  35.2 14.1 %collective-permute-start.2 = (bf16[1024,256]{1,0:T(8,128)(2,1)S(1)}, bf16[1024,256]{1,0:T(8,128)(2,1)S(1)}, u32[]{:S(2)}, u32[]{:S(2)}) collective-permute-start(bf16[1024,256]{1,0:T(8,128)(2,1)S(1)} %bitcast.79), channel_id=1, source_target_pairs={{0,192},{64,0},{128,64},{192,128},{1,193},{65,1},{129,65},{193,129... | collective-permute-start | bytes 1572872 | tf_op jit(solution)/shard_map/ppermute | solution.py:280
  36.0 13.3 %collective-permute-start.1 = (bf16[1024,256]{1,0:T(8,128)(2,1)S(1)}, bf16[1024,256]{1,0:T(8,128)(2,1)S(1)}, u32[]{:S(2)}, u32[]{:S(2)}) collective-permute-start(bf16[1024,256]{1,0:T(8,128)(2,1)S(1)} %bitcast.80), channel_id=1, source_target_pairs={{0,64},{64,128},{128,192},{192,0},{1,65},{65,129},{129,193},{193,1... | collective-permute-start | bytes 1572872 | tf_op jit(solution)/shard_map/ppermute | solution.py:279
  49.4 7.7 %collective-permute-start.6 = (bf16[512,256]{1,0:T(8,128)(2,1)S(1)}, bf16[512,256]{1,0:T(8,128)(2,1)S(1)}, u32[]{:S(2)}, u32[]{:S(2)}) collective-permute-start(bf16[512,256]{1,0:T(8,128)(2,1)S(1)} %slice.19), channel_id=1, source_target_pairs={{0,192},{64,0},{128,64},{192,128},{1,193},{65,1},{129,65},{193,129... | collective-permute-start | bytes 786440 | tf_op jit(solution)/shard_map/ppermute | solution.py:284
  49.5 7.6 %collective-permute-start.5 = (bf16[512,256]{1,0:T(8,128)(2,1)S(1)}, bf16[512,256]{1,0:T(8,128)(2,1)S(1)}, u32[]{:S(2)}, u32[]{:S(2)}) collective-permute-start(bf16[512,256]{1,0:T(8,128)(2,1)S(1)} %slice.18), channel_id=1, source_target_pairs={{0,64},{64,128},{128,192},{192,0},{1,65},{65,129},{129,193},{193,1... | collective-permute-start | bytes 786440 | tf_op jit(solution)/shard_map/ppermute | solution.py:283
  60.5 4.9 %collective-permute-start.8 = (bf16[512,128]{1,0:T(8,128)(2,1)S(1)}, bf16[512,128]{1,0:T(8,128)(2,1)S(1)}, u32[]{:S(2)}, u32[]{:S(2)}) collective-permute-start(bf16[512,128]{1,0:T(8,128)(2,1)S(1)} %conv_back.4), channel_id=1, source_target_pairs={{3,6},{7,2},{11,14},{15,10},{19,22},{23,18},{27,30},{31,26},{35,38... | collective-permute-start | bytes 393224 | tf_op jit(solution)/shard_map/ppermute | solution.py:348
  61.2 4.3 %collective-permute-start.7 = (bf16[512,128]{1,0:T(8,128)(2,1)S(1)}, bf16[512,128]{1,0:T(8,128)(2,1)S(1)}, u32[]{:S(2)}, u32[]{:S(2)}) collective-permute-start(bf16[512,128]{1,0:T(8,128)(2,1)S(1)} %conv_back.4), channel_id=1, source_target_pairs={{3,2},{7,6},{11,10},{15,14},{19,18},{23,22},{27,26},{31,30},{35,34... | collective-permute-start | bytes 393224 | tf_op jit(solution)/shard_map/ppermute | solution.py:351
  61.8 9.6 %collective-permute-start.15 = (bf16[256,256]{1,0:T(8,128)(2,1)}, bf16[256,256]{1,0:T(8,128)(2,1)}, u32[]{:S(2)}, u32[]{:S(2)}) collective-permute-start(bf16[256,256]{1,0:T(8,128)(2,1)} %norm_forward.1.own), channel_id=1, source_target_pairs={{0,192},{64,0},{128,64},{192,128},{1,193},{65,1},{129,65},{193,129... | collective-permute-start | bytes 393224 | tf_op jit(solution)/shard_map/ppermute | solution.py:280
  63.0 9.3 %collective-permute-start.14 = (bf16[256,256]{1,0:T(8,128)(2,1)}, bf16[256,256]{1,0:T(8,128)(2,1)}, u32[]{:S(2)}, u32[]{:S(2)}) collective-permute-start(bf16[256,256]{1,0:T(8,128)(2,1)} %norm_forward.1.own), channel_id=1, source_target_pairs={{0,64},{64,128},{128,192},{192,0},{1,65},{65,129},{129,193},{193,1... | collective-permute-start | bytes 393224 | tf_op jit(solution)/shard_map/ppermute | solution.py:279
  65.4 3.4 %copy-start.8 = (bf16[512,128]{1,0:T(8,128)(2,1)}, bf16[512,128]{1,0:T(8,128)(2,1)S(1)}, u32[]{:S(2)}) copy-start(bf16[512,128]{1,0:T(8,128)(2,1)S(1)} %collective-permute-done.8.cross) | copy-start | bytes 393220
  65.4 4.7 %copy-start.9 = (bf16[512,128]{1,0:T(8,128)(2,1)}, bf16[512,128]{1,0:T(8,128)(2,1)S(1)}, u32[]{:S(2)}) copy-start(bf16[512,128]{1,0:T(8,128)(2,1)S(1)} %collective-permute-done.7.same) | copy-start | bytes 393220
  68.8 7.6 %collective-permute-start.10 = (bf16[512,128]{1,0:T(8,128)(2,1)S(1)}, bf16[512,128]{1,0:T(8,128)(2,1)}, u32[]{:S(2)}, u32[]{:S(2)}) collective-permute-start(bf16[512,128]{1,0:T(8,128)(2,1)S(1)} %conv_back.5), channel_id=1, source_target_pairs={{2,5},{6,1},{10,13},{14,9},{18,21},{22,17},{26,29},{30,25},{34,37}... | collective-permute-start | bytes 393224 | tf_op jit(solution)/shard_map/ppermute | solution.py:348
  70.2 6.3 %collective-permute-start.9 = (bf16[512,128]{1,0:T(8,128)(2,1)S(1)}, bf16[512,128]{1,0:T(8,128)(2,1)}, u32[]{:S(2)}, u32[]{:S(2)}) collective-permute-start(bf16[512,128]{1,0:T(8,128)(2,1)S(1)} %conv_back.5), channel_id=1, source_target_pairs={{2,1},{6,5},{10,9},{14,13},{18,17},{22,21},{26,25},{30,29},{34,33}... | collective-permute-start | bytes 393224 | tf_op jit(solution)/shard_map/ppermute | solution.py:351
  71.5 16.6 %copy-start.13 = (bf16[2,4,32,256]{3,2,0,1:T(8,128)(2,1)S(1)}, bf16[2,4,32,256]{3,2,0,1:T(8,128)(2,1)}, u32[]{:S(2)}) copy-start(bf16[2,4,32,256]{3,2,0,1:T(8,128)(2,1)} %copy-done.12) | copy-start | bytes 393220
  72.3 15.9 %collective-permute-start.17 = (bf16[128,256]{1,0:T(8,128)(2,1)S(1)}, bf16[128,256]{1,0:T(8,128)(2,1)S(1)}, u32[]{:S(2)}, u32[]{:S(2)}) collective-permute-start(bf16[128,256]{1,0:T(8,128)(2,1)S(1)} %bitcast.102), channel_id=1, source_target_pairs={{0,192},{64,0},{128,64},{192,128},{1,193},{65,1},{129,65},{193,129... | collective-permute-start | bytes 196616 | tf_op jit(solution)/shard_map/ppermute | solution.py:284
  73.2 15.0 %collective-permute-start.16 = (bf16[128,256]{1,0:T(8,128)(2,1)S(1)}, bf16[128,256]{1,0:T(8,128)(2,1)S(1)}, u32[]{:S(2)}, u32[]{:S(2)}) collective-permute-start(bf16[128,256]{1,0:T(8,128)(2,1)S(1)} %bitcast.103), channel_id=1, source_target_pairs={{0,64},{64,128},{128,192},{192,0},{1,65},{65,129},{129,193},{193,1... | collective-permute-start | bytes 196616 | tf_op jit(solution)/shard_map/ppermute | solution.py:283
  80.3 14.3 %copy-start.3 = (bf16[512,128]{1,0:T(8,128)(2,1)}, bf16[512,128]{1,0:T(8,128)(2,1)S(1)}, u32[]{:S(2)}) copy-start(bf16[512,128]{1,0:T(8,128)(2,1)S(1)} %conv_back.6) | copy-start | bytes 393220
  80.3 7.8 %collective-permute-start.12 = (bf16[512,128]{1,0:T(8,128)(2,1)S(1)}, bf16[512,128]{1,0:T(8,128)(2,1)S(1)}, u32[]{:S(2)}, u32[]{:S(2)}) collective-permute-start(bf16[512,128]{1,0:T(8,128)(2,1)S(1)} %conv_back.6), channel_id=1, source_target_pairs={{1,4},{5,0},{9,12},{13,8},{17,20},{21,16},{25,28},{29,24},{33,36},... | collective-permute-start | bytes 393224 | tf_op jit(solution)/shard_map/ppermute | solution.py:348
  81.6 6.5 %collective-permute-start.11 = (bf16[512,128]{1,0:T(8,128)(2,1)S(1)}, bf16[512,128]{1,0:T(8,128)(2,1)S(1)}, u32[]{:S(2)}, u32[]{:S(2)}) collective-permute-start(bf16[512,128]{1,0:T(8,128)(2,1)S(1)} %conv_back.6), channel_id=1, source_target_pairs={{1,0},{5,4},{9,8},{13,12},{17,16},{21,20},{25,24},{29,28},{33,32},... | collective-permute-start | bytes 393224 | tf_op jit(solution)/shard_map/ppermute | solution.py:351
  88.1 6.5 %copy-start.4 = (bf16[512,128]{1,0:T(8,128)(2,1)}, bf16[512,128]{1,0:T(8,128)(2,1)S(1)}, u32[]{:S(2)}) copy-start(bf16[512,128]{1,0:T(8,128)(2,1)S(1)} %collective-permute-done.12.cross) | copy-start | bytes 393220
  88.1 6.5 %copy-start.6 = (bf16[512,128]{1,0:T(8,128)(2,1)}, bf16[512,128]{1,0:T(8,128)(2,1)S(1)}, u32[]{:S(2)}) copy-start(bf16[512,128]{1,0:T(8,128)(2,1)S(1)} %collective-permute-done.11.same) | copy-start | bytes 393220
  88.2 6.3 %collective-permute-start.19 = (bf16[256,256]{1,0:T(8,128)(2,1)S(1)}, bf16[256,256]{1,0:T(8,128)(2,1)S(1)}, u32[]{:S(2)}, u32[]{:S(2)}) collective-permute-start(bf16[256,256]{1,0:T(8,128)(2,1)S(1)} %maximum_select_fusion.own), channel_id=1, source_target_pairs={{0,192},{64,0},{128,64},{192,128},{1,193},{65,1},{129,65},{193,129... | collective-permute-start | bytes 393224 | tf_op jit(solution)/shard_map/ppermute | solution.py:280
  88.3 6.2 %collective-permute-start.18 = (bf16[256,256]{1,0:T(8,128)(2,1)S(1)}, bf16[256,256]{1,0:T(8,128)(2,1)S(1)}, u32[]{:S(2)}, u32[]{:S(2)}) collective-permute-start(bf16[256,256]{1,0:T(8,128)(2,1)S(1)} %maximum_select_fusion.own), channel_id=1, source_target_pairs={{0,64},{64,128},{128,192},{192,0},{1,65},{65,129},{129,193},{193,1... | collective-permute-start | bytes 393224 | tf_op jit(solution)/shard_map/ppermute | solution.py:279
  94.5 5.8 %collective-permute-start.21 = (bf16[128,256]{1,0:T(8,128)(2,1)S(1)}, bf16[128,256]{1,0:T(8,128)(2,1)S(1)}, u32[]{:S(2)}, u32[]{:S(2)}) collective-permute-start(bf16[128,256]{1,0:T(8,128)(2,1)S(1)} %bitcast.104), channel_id=1, source_target_pairs={{0,192},{64,0},{128,64},{192,128},{1,193},{65,1},{129,65},{193,129... | collective-permute-start | bytes 196616 | tf_op jit(solution)/shard_map/ppermute | solution.py:284
  94.6 5.8 %collective-permute-start.20 = (bf16[128,256]{1,0:T(8,128)(2,1)S(1)}, bf16[128,256]{1,0:T(8,128)(2,1)S(1)}, u32[]{:S(2)}, u32[]{:S(2)}) collective-permute-start(bf16[128,256]{1,0:T(8,128)(2,1)S(1)} %bitcast.105), channel_id=1, source_target_pairs={{0,64},{64,128},{128,192},{192,0},{1,65},{65,129},{129,193},{193,1... | collective-permute-start | bytes 196616 | tf_op jit(solution)/shard_map/ppermute | solution.py:283
  102.9 29.7 %all-to-all-start.1 = ((bf16[16,108,256]{2,1,0:T(8,128)(2,1)}), bf16[16,108,256]{2,1,0:T(8,128)(2,1)}, u32[]{:S(2)}, u32[]{:S(2)}) async-start(bf16[16,108,256]{2,1,0:T(8,128)(2,1)} %copy-done.2), calls=%async_computation.1 | async-start | bytes 1835008 | tf_op jit(solution)/shard_map/all_to_all | solution.py:356
  112.7 6.6 %collective-permute-start.13 = (bf16[4,2,32,128]{3,2,1,0:T(8,128)(2,1)S(1)}, bf16[4,2,32,128]{3,2,1,0:T(8,128)(2,1)S(1)}, u32[]{:S(2)}, u32[]{:S(2)}) collective-permute-start(bf16[4,2,32,128]{3,2,1,0:T(8,128)(2,1)S(1)} %dynamic-slice_bitcast_fusion), channel_id=1, source_target_pairs={{0,4},{4,0},{1,5},{5,1},{2,6},{6,2},{3,7},{7,3},{8,12},{12,8},{9,1... | collective-permute-start | bytes 196616 | tf_op jit(solution)/shard_map/ppermute | solution.py:360
  (6 other events, 4.9 us)

commit v3 on v2

--- a/solution.py
+++ b/solution.py
@@ -1,3 +1,5 @@
+import functools
+
 import jax
 import jax.numpy as jnp
 import numpy as np
@@ -20,6 +22,7 @@
 PAIR = NYH * PART
 CHUNK = NZ * PAIR
 HC = C // NYH
+WIDE = 2 * NX * M * HW
 SLOTS = NZ * HC
 CLIPS = NX * NZ * NYH
 GRANT = 24 << 20
@@ -31,15 +34,15 @@
 HBM = pl.BlockSpec(memory_space=pltpu.HBM)
 
 
-def shift_matrices():
-    s = np.zeros((9, HC, HC), np.float32)
+def shift_matrices(size):
+    s = np.zeros((9, size, size), np.float32)
     for kh in range(3):
         for kw in range(3):
             for h in range(H):
                 for w in range(W):
                     h2, w2 = h - kh + 1, w - kw + 1
                     if 0 <= h2 < H and 0 <= w2 < W:
-                        for f in range(HC // HW):
+                        for f in range(size // HW):
                             s[kh * 3 + kw, f * HW + h * W + w, f * HW + h2 * W + w2] = 1
     return s
 
@@ -128,7 +131,13 @@
     )(flags, mine, theirs, gain, shift)
 
 
-def conv_kernel(
+def conv_kernel(target, flags, *refs):
+    @pl.when(flags[2] == target)
+    def _():
+        conv_body(flags, *refs)
+
+
+def conv_body(
     flags, same, cross, s_ref, own, left, right, far_a, far_b, fac_ref,
     out_ref, kbuf, fac, gs, krows, sem,
 ):
@@ -190,10 +199,10 @@
     out_ref[...] = result.astype(BF)
 
 
-def conv_back(flags, g, s, pieces, fac):
+def conv_back(target, flags, g, s, pieces, fac):
     rows = NYH * POS
     return pl.pallas_call(
-        conv_kernel,
+        functools.partial(conv_kernel, target),
         out_shape=jax.ShapeDtypeStruct((rows, HC), BF),
         in_specs=[SMEM] + [VMEM] * 3 + [HBM] * 6,
         out_specs=VMEM,
@@ -210,64 +219,79 @@
     )(flags, *g, s, *pieces, fac)
 
 
-def columns_kernel(flags, own, left, right, far_a, far_b, s_ref, at_ref, turned):
-    blocks = ((own, 0), (own, 1), (left, 0), (left, 1), (right, 0), (right, 1), (far_a, None), (far_b, None))
-    for t in range(2):
-        turned[t] = jnp.zeros((C, C), BF)
+def rows_at(t, blocks):
+    own, left, right, far_a, far_b = blocks
+    pair, clip = NYH * M * HW, M * HW
+    return [ref[pl.ds(t * pair, pair), :] for ref in (own, left, right)] + [
+        ref[pl.ds(t * clip, clip), :] for ref in (far_a, far_b)
+    ]
+
+
+def weight_kernel(
+    flags, own, left, right, far_a, far_b, g_own, g_left, g_right, g_far_a, g_far_b, s_ref,
+    out_ref, a_own, a_left, a_right, a_far_a, a_far_b, shifts, turned, at, gbuf, sem,
+):
+    yh = flags[1]
+    acts = (a_own, a_left, a_right, a_far_a, a_far_b)
+    copies = [
+        pltpu.make_async_copy(src, dst, sem.at[i])
+        for i, (src, dst) in enumerate(
+            zip((own, left, right, far_a, far_b, s_ref), acts + (shifts,))
+        )
+    ]
+    for copy in copies:
+        copy.start()
     for t in range(F):
-        rows = [
-            ref[pl.ds(t * HW if m is None else time_major(m, t), HW), :] for ref, m in blocks
-        ]
-        turned[t + 2] = jnp.concatenate(rows, axis=0).astype(F32).T.astype(BF)
+        gbuf[pl.ds(t * WIDE, WIDE), :] = jnp.concatenate(
+            rows_at(t, (g_own, g_left, g_right, g_far_a, g_far_b)), axis=0
+        )
+    turned[pl.ds(0, 2)] = jnp.zeros((2, C, WIDE), BF)
+    for copy in copies:
+        copy.wait()
+    for t in range(F):
+        rows = jnp.concatenate(rows_at(t, acts), axis=0)
+        turned[t + 2] = rows.astype(F32).T.astype(BF)
     first = lax.div(flags[0] * (CHUNK // 64), 4)
     for k in range(8):
         tap = jnp.minimum(first + k, 26)
         kt = lax.div(tap, 9)
-        j = lax.rem(tap, 9)
-        moved = s_ref[j]
+        moved = shifts[lax.rem(tap, 9)]
         for t in range(F):
-            for r in range(C // HC):
-                at_ref[pl.ds(k * C, C), pl.ds(t * C + r * HC, HC)] = jnp.dot(
-                    turned[t + kt, :, pl.ds(r * HC, HC)], moved, preferred_element_type=F32
+            for r in range(WIDE // C):
+                at[pl.ds(k * C, C), pl.ds(t * WIDE + r * C, C)] = jnp.dot(
+                    turned[t + kt, :, pl.ds(r * C, C)], moved, preferred_element_type=F32
                 ).astype(BF)
-
-
-def columns(flags, acts, s):
-    return pl.pallas_call(
-        columns_kernel,
-        out_shape=jax.ShapeDtypeStruct((8 * C, F * C), BF),
-        in_specs=[SMEM] + [VMEM] * 6,
-        out_specs=VMEM,
-        scratch_shapes=[pltpu.VMEM((F + 2, C, C), BF)],
-        compiler_params=pltpu.CompilerParams(vmem_limit_bytes=GRANT),
-        name="act_columns",
-    )(flags, *acts, s)
-
-
-def weight_kernel(flags, at_ref, own, left, right, far_a, far_b, out_ref, gbuf):
     offset = lax.rem(flags[0] * (CHUNK // 64), 4) * 64
-    blocks = ((own, 0), (own, 1), (left, 0), (left, 1), (right, 0), (right, 1), (far_a, None), (far_b, None))
-    for t in range(F):
-        for b, (ref, m) in enumerate(blocks):
-            gbuf[pl.ds(t * C + b * HW, HW), :] = ref[pl.ds(t * HW if m is None else time_major(m, t), HW), :]
-    for i in range(CHUNK // (2 * PAIR)):
-        rows = at_ref[pl.ds(pl.multiple_of(offset + i * 2 * PAIR, 16), 2 * PAIR), :]
-        total = jnp.dot(rows, gbuf[...], preferred_element_type=F32) * (1.0 / CLIPS)
-        for k in range(4):
-            out_ref[4 * i + k] = total[k * PART : (k + 1) * PART].astype(BF)
-
-
-def weight_back(flags, at, grads):
+    for z in range(NZ):
+        skip = [(z * PAIR + k * PART) % 16 for k in range(NYH)]
+        start = offset + jnp.where(yh == 0, z * PAIR - skip[0], z * PAIR + PART - skip[1])
+        total = jnp.dot(
+            at[pl.ds(pl.multiple_of(start, 16), HC), :], gbuf[...], preferred_element_type=F32
+        ) * (1.0 / CLIPS)
+        out_ref[z] = jnp.where(
+            yh == 0, total[skip[0] : skip[0] + PART], total[skip[1] : skip[1] + PART]
+        ).astype(BF)
+
+
+def weight_back(flags, acts, grads, s):
+    pieces = [pltpu.VMEM(v.shape, BF) for v in acts]
     return pl.pallas_call(
         weight_kernel,
-        out_shape=jax.ShapeDtypeStruct((NZ * NYH, PART, C), BF),
-        in_specs=[SMEM] + [VMEM] * 6,
+        out_shape=jax.ShapeDtypeStruct((NZ, PART, C), BF),
+        in_specs=[SMEM] + [HBM] * 5 + [VMEM] * 5 + [HBM],
         out_specs=VMEM,
-        scratch_shapes=[pltpu.VMEM((F * C, C), BF)],
+        scratch_shapes=pieces
+        + [
+            pltpu.VMEM((9, C, C), BF),
+            pltpu.VMEM((F + 2, C, WIDE), BF),
+            pltpu.VMEM((8 * C, F * WIDE), BF),
+            pltpu.VMEM((F * WIDE, C), BF),
+            pltpu.SemaphoreType.DMA((6,)),
+        ],
         compiler_params=pltpu.CompilerParams(vmem_limit_bytes=GRANT),
         cost_estimate=pl.CostEstimate(flops=2 * CHUNK * F * C * C, bytes_accessed=6 << 20, transcendentals=0),
         name="weight_back",
-    )(flags, at, *grads)
+    )(flags, *acts, *grads, s)
 
 
 def ring(axis, step):
@@ -286,20 +310,21 @@
     return blocks if between is None else (blocks, between)
 
 
-def halves_of_clip():
-    def pick(m):
-        return lambda b: b.reshape(F, M, HW, C)[:, m].reshape(F * HW, C)
+def clips_of_pair():
+    def pick(k):
+        return lambda b: b.reshape(F, NYH, M * HW, C)[:, k].reshape(POS, C)
 
     return pick(0), pick(1)
 
 
 def local(section_inputs, top_grad, norm_gain, norm_shift, conv_weight):
-    s = jnp.asarray(shift_matrices(), BF)
+    s = jnp.asarray(shift_matrices(HC), BF)
+    wide_s = jnp.asarray(shift_matrices(C), BF)
     x_at = lax.axis_index("x")
     yh = lax.axis_index("yh")
     dp = (x_at * NZ + lax.axis_index("z")) * NYH + yh
     section = lax.axis_index("yl") * 2 + lax.axis_index("c")
-    flags = jnp.stack([x_at, yh]).astype(jnp.int32)
+    flags = jnp.stack([x_at, yh, section]).astype(jnp.int32)
     swap = ring("yh", 1)
 
     def mine(value, axis):
@@ -329,36 +354,38 @@
     top = top_grad.reshape(M, F, HW, C).transpose(1, 0, 2, 3).reshape(F, 1, M * HW, C)
     both = in_order(top, lax.ppermute(top, "yh", swap), 1).reshape(NYH * POS, C)
     arrived = (mine(both, 1), theirs(both, 1))
-    kernel_rows, (arrived, fac) = gather_x(
-        chunk, lambda b: b[: SLOTS // 2], lambda b: b[SLOTS // 2 :], (arrived, fac)
-    )
-    own_g = top.reshape(POS, C)
+    act = act.reshape(F, 1, M * HW, C)
+    act = in_order(act, lax.ppermute(act, "yh", swap), 1).reshape(NYH * POS, C)
+    kernel_rows, (arrived, fac, act) = gather_x(
+        chunk, lambda b: b[: SLOTS // 2], lambda b: b[SLOTS // 2 :], (arrived, fac, act)
+    )
+    pair_g = both
     pair_dx = None
     for k in range(4):
         if k > 0:
-            two = [lax.dynamic_index_in_dim(v.reshape(F, NYH, M * HW, HC), yh, 1, False) for v in arrived]
-            own_g = jnp.where(section == 3 - k, in_order(*two, -1).reshape(POS, C), own_g)
-        sent = conv_back(flags, arrived, s, kernel_rows, fac)
+            pair_g = jnp.where(section == 3 - k, in_order(*arrived, 1), pair_g)
+        sent = conv_back(3 - k, flags, arrived, s, kernel_rows, fac)
         if k == 0:
             sent, act = lax.optimization_barrier((sent, act))
-            acts = gather_x(act, *halves_of_clip())
+            acts = gather_x(act, *clips_of_pair())
         pair_dx = sent if k == 0 else jnp.where(section == 3 - k, sent, pair_dx)
         if k < 3:
             src, dst = 3 - k, 2 - k
+            same = lax.ppermute(sent, ("yl", "c"), [(src, dst)])
             cross = lax.ppermute(
                 sent, ("yh", "yl", "c"), [(y * N_PIPE + src, (1 - y) * N_PIPE + dst) for y in range(NYH)]
             )
-            arrived = (lax.ppermute(sent, ("yl", "c"), [(src, dst)]), cross)
-
-    own_g, acts = lax.optimization_barrier((own_g, acts))
-    at = columns(flags, acts, s)
-    partial = weight_back(flags, at, gather_x(own_g, *halves_of_clip()))
-    weight_part = jnp.sum(lax.all_to_all(partial, ("z", "yh"), 0, 0, tiled=True).astype(F32), axis=0)
+            arrived = (same, cross)
 
     pair_dx = pair_dx.reshape(F, NYH, M, HW, HC)
     kept = lax.dynamic_index_in_dim(pair_dx, yh, 1, False)
-    got = lax.ppermute(lax.dynamic_index_in_dim(pair_dx, 1 - yh, 1, False), "yh", swap)
+    given = lax.dynamic_index_in_dim(pair_dx, 1 - yh, 1, False)
+    grads, (kept, given) = gather_x(pair_g, *clips_of_pair(), (kept, given))
+    got = lax.ppermute(given, "yh", swap)
     dx = in_order(kept, got, -1).transpose(1, 0, 2, 3).reshape(section_inputs.shape)
+
+    partial = weight_back(flags, acts, grads, wide_s)
+    weight_part = jnp.sum(lax.all_to_all(partial, "z", 0, 0, tiled=True).astype(F32), axis=0)
     return dx, weight_part[None]
 
 

time: 136 us -> 125 us (0.919)
  waiting for transfers between devices: 48.1 us -> 57 us
  Pallas kernels: 20.7 us -> 14.4 us
  starting transfers between devices: 49.6 us -> 43.4 us
  local copies, waits for them, and re-layouts: 11.6 us -> 6.27 us
    ppermute x3, waiting for transfers between devices: 0.01 us -> 11.4 us  [gather_x(): left = lax.ppermute(block, 'x', ring('x', 1))]
    ppermute x3, waiting for transfers between devices: 12.5 us -> 2.76 us  [gather_x(): right = lax.ppermute(block, 'x', ring('x', -1))]
    ppermute x4 -> x5, waiting for transfers between devices: 3.46 us -> 13.1 us  [the longest x3 9.38 us: local(): same = lax.ppermute(sent, ('yl', 'c'), [(src, dst)])]
    ppermute x3, starting transfers between devices: 9.74 us -> 1.59 us  [gather_x(): far_a = lax.ppermute(first_half(left), 'x', ring('x', 1))]
    ppermute x3, starting transfers between devices: 8 us -> 1.1 us  [gather_x(): left = lax.ppermute(block, 'x', ring('x', 1))]
    ppermute x3, waiting for transfers between devices: 0.01 us -> 6.87 us  [gather_x(): far_a = lax.ppermute(first_half(left), 'x', ring('x', 1))]
    all_to_all x1, waiting for transfers between devices: 12.5 us -> 5.85 us  [local(): lax.all_to_all(partial, 'z', 0, 0, tiled=True).astype(F32)]
    pallas_call x6 -> x5, Pallas kernels: 18.1 us -> 12.4 us  [the longest x4 6.45 us: conv_back(): pl.pallas_call(functools.partial(conv_kernel, target), out_shape=jax.Shap...]
  transfers between devices with their start and end apart: 24 -> 25, of which waited for: 7 -> 14; matrix products, arithmetic and copies ran while one was open for 5% -> 3% of each run, Pallas kernels for 12% -> 6%
where the time goes in v3:
time: 125 us
  waiting for transfers between devices  57 us (46%)
  starting transfers between devices  43.4 us (35%)
  Pallas kernels  14.4 us (12%)
  local copies, waits for them, and re-layouts  6.27 us (5%)
  other arithmetic  2.57 us (2%)
    ppermute x3, waiting for transfers between devices, gather_x(): left = lax.ppermute(block, 'x', ring('x', 1))  11.4 us
    ppermute x3, waiting for transfers between devices, local(): same = lax.ppermute(sent, ('yl', 'c'), [(src, dst)])  9.38 us
    all_to_all x1, starting transfers between devices, local(): lax.all_to_all(jnp.broadcast_to(window[None], (NZ, HC, C)), 'z', 0, 0, ti...  8.47 us
    all_to_all x1, waiting for transfers between devices, local(): lax.all_to_all(jnp.broadcast_to(window[None], (NZ, HC, C)), 'z', 0, 0, ti...  7.15 us
    ppermute x3, waiting for transfers between devices, gather_x(): far_a = lax.ppermute(first_half(left), 'x', ring('x', 1))  6.87 us
    pallas_call x4, Pallas kernels, conv_back(): pl.pallas_call(functools.partial(conv_kernel, target), out_shape=jax.Shap...  6.45 us
    pallas_call x1, Pallas kernels, weight_back(): pl.pallas_call(weight_kernel, out_shape=jax.ShapeDtypeStruct((NZ, PART, C...  5.99 us
    all_to_all x1, waiting for transfers between devices, local(): lax.all_to_all(partial, 'z', 0, 0, tiled=True).astype(F32)  5.85 us
  transfers between devices with their start and end apart: 25, of which 14 were waited for; matrix products, arithmetic and copies ran while one was open for 3% of the time, Pallas kernels for 6%

profile of v3, /device:TPU:6, one launch (start us, length us, event | category | flops | bytes accessed | tf_op | source)
XLA Modules:
  0.0 124.8 jit_solution(13974745957443880073)
XLA Ops:
  1.7 3.3 %collective-permute-start = (bf16[128,256]{1,0:T(8,128)(2,1)S(1)}, bf16[128,256]{1,0:T(8,128)(2,1)S(1)}, u32[]{:S(2)}, u32[]{:S(2)}) collective-permute-start(bf16[128,256]{1,0:T(8,128)(2,1)S(1)} %constant_dynamic-slice_fusion.6), channel_id=1, source_target_pairs={{0,4},{4,0},{1,5},{5,1},{2,6},{6,2},{3,7},{7,3},{8,12},{12,8},{9,1... | collective-permute-start | bytes 196616 | tf_op jit(solution)/shard_map/ppermute | solution.py:342
  8.9 8.5 %all-to-all-start = ((bf16[8,128,256]{2,1,0:T(8,128)(2,1)}), bf16[8,128,256]{2,1,0:T(8,128)(2,1)S(1)}, u32[]{:S(2)}, u32[]{:S(2)}) async-start(bf16[8,128,256]{2,1,0:T(8,128)(2,1)} %broadcast_in_dim.4), calls=%async_computation | async-start | bytes 1048576 | tf_op jit(solution)/shard_map/all_to_all | solution.py:346
  17.4 2.7 %collective-permute-start.4 = (bf16[256,128]{1,0:T(8,128)(2,1)S(1)}, bf16[256,128]{1,0:T(8,128)(2,1)S(1)}, u32[]{:S(2)}, u32[]{:S(2)}) collective-permute-start(bf16[256,128]{1,0:T(8,128)(2,1)S(1)} %get-tuple-element.48), channel_id=1, source_target_pairs={{0,4},{4,0},{1,5},{5,1},{2,6},{6,2},{3,7},{7,3},{8,12},{12,8},{9,1... | collective-permute-start | bytes 196616 | tf_op jit(solution)/shard_map/ppermute | solution.py:350
  21.2 2.7 %collective-permute-start.5 = (bf16[4,1,64,256]{3,2,1,0:T(8,128)(2,1)S(1)}, bf16[4,1,64,256]{3,2,1,0:T(8,128)(2,1)S(1)}, u32[]{:S(2)}, u32[]{:S(2)}) collective-permute-start(bf16[4,1,64,256]{3,2,1,0:T(8,128)(2,1)S(1)} %bitcast.64), channel_id=1, source_target_pairs={{0,4},{4,0},{1,5},{5,1},{2,6},{6,2},{3,7},{7,3},{8,12},{12,8},{9,1... | collective-permute-start | bytes 393224 | tf_op jit(solution)/shard_map/ppermute | solution.py:358
  25.1 2.3 %collective-permute-done.3 = bf16[4,1,64,256]{3,2,1,0:T(8,128)(2,1)S(1)} collective-permute-done((bf16[4,1,64,256]{3,2,1,0:T(8,128)(2,1)S(1)}, bf16[4,1,64,256]{3,2,1,0:T(8,128)(2,1)S(1)}, u32[]{:S(2)}, u32[]{:S(2)}) %collective-permute-start.3) | collective-permute-done | bytes 131104 | tf_op jit(solution)/shard_map/ppermute | solution.py:355
  27.5 7.1 %all-to-all-done = bf16[8,128,256]{2,1,0:T(8,128)(2,1)S(1)} async-done(((bf16[8,128,256]{2,1,0:T(8,128)(2,1)}), bf16[8,128,256]{2,1,0:T(8,128)(2,1)S(1)}, u32[]{:S(2)}, u32[]{:S(2)}) %all-to-all-start) | async-done | bytes 524320 | tf_op jit(solution)/shard_map/all_to_all | solution.py:346
  35.1 1.5 %collective-permute-start.2 = (bf16[1024,256]{1,0:T(8,128)(2,1)S(1)}, bf16[1024,256]{1,0:T(8,128)(2,1)S(1)}, u32[]{:S(2)}, u32[]{:S(2)}) collective-permute-start(bf16[1024,256]{1,0:T(8,128)(2,1)S(1)} %bitcast.52), channel_id=1, source_target_pairs={{0,192},{64,0},{128,64},{192,128},{1,193},{65,1},{129,65},{193,129... | collective-permute-start | bytes 1572872 | tf_op jit(solution)/shard_map/ppermute | solution.py:304
  37.5 10.1 %collective-permute-done.1.refs_4_ = bf16[1024,256]{1,0:T(8,128)(2,1)S(1)} collective-permute-done((bf16[1024,256]{1,0:T(8,128)(2,1)S(1)}, bf16[1024,256]{1,0:T(8,128)(2,1)S(1)}, u32[]{:S(2)}, u32[]{:S(2)}) %collective-permute-start.1) | collective-permute-done | bytes 524320 | tf_op jit(solution)/shard_map/ppermute | solution.py:303
  47.5 1.4 %collective-permute-done.2.refs_5_ = bf16[1024,256]{1,0:T(8,128)(2,1)S(1)} collective-permute-done((bf16[1024,256]{1,0:T(8,128)(2,1)S(1)}, bf16[1024,256]{1,0:T(8,128)(2,1)S(1)}, u32[]{:S(2)}, u32[]{:S(2)}) %collective-permute-start.2) | collective-permute-done | bytes 524320 | tf_op jit(solution)/shard_map/ppermute | solution.py:304
  49.3 1.8 %collective-permute-start.7 = (bf16[512,256]{1,0:T(8,128)(2,1)S(1)}, bf16[512,256]{1,0:T(8,128)(2,1)S(1)}, u32[]{:S(2)}, u32[]{:S(2)}) collective-permute-start(bf16[512,256]{1,0:T(8,128)(2,1)S(1)} %slice.19), channel_id=1, source_target_pairs={{0,192},{64,0},{128,64},{192,128},{1,193},{65,1},{129,65},{193,129... | collective-permute-start | bytes 786440 | tf_op jit(solution)/shard_map/ppermute | solution.py:308
  51.2 4.2 %collective-permute-done.6.refs_6_ = bf16[512,256]{1,0:T(8,128)(2,1)S(1)} collective-permute-done((bf16[512,256]{1,0:T(8,128)(2,1)S(1)}, bf16[512,256]{1,0:T(8,128)(2,1)S(1)}, u32[]{:S(2)}, u32[]{:S(2)}) %collective-permute-start.6) | collective-permute-done | bytes 262176 | tf_op jit(solution)/shard_map/ppermute | solution.py:307
  55.4 1.6 %collective-permute-done.7.refs_7_ = bf16[512,256]{1,0:T(8,128)(2,1)S(1)} collective-permute-done((bf16[512,256]{1,0:T(8,128)(2,1)S(1)}, bf16[512,256]{1,0:T(8,128)(2,1)S(1)}, u32[]{:S(2)}, u32[]{:S(2)}) %collective-permute-start.7) | collective-permute-done | bytes 262176 | tf_op jit(solution)/shard_map/ppermute | solution.py:308
  58.3 1.3 %collective-permute-start.8 = (bf16[512,128]{1,0:T(8,128)(2,1)}, bf16[512,128]{1,0:T(8,128)(2,1)}, u32[]{:S(2)}, u32[]{:S(2)}) collective-permute-start(bf16[512,128]{1,0:T(8,128)(2,1)} %conv_back.4), channel_id=1, source_target_pairs={{3,2},{7,6},{11,10},{15,14},{19,18},{23,22},{27,26},{31,30},{35,34... | collective-permute-start | bytes 393224 | tf_op jit(solution)/shard_map/ppermute | solution.py:374
  59.6 1.3 %collective-permute-start.9 = (bf16[512,128]{1,0:T(8,128)(2,1)}, bf16[512,128]{1,0:T(8,128)(2,1)}, u32[]{:S(2)}, u32[]{:S(2)}) collective-permute-start(bf16[512,128]{1,0:T(8,128)(2,1)} %conv_back.4), channel_id=1, source_target_pairs={{3,6},{7,2},{11,14},{15,10},{19,22},{23,18},{27,30},{31,26},{35,38... | collective-permute-start | bytes 393224 | tf_op jit(solution)/shard_map/ppermute | solution.py:375
  61.2 1.7 %collective-permute-start.18 = (bf16[512,256]{1,0:T(8,128)(2,1)S(1)}, bf16[512,256]{1,0:T(8,128)(2,1)S(1)}, u32[]{:S(2)}, u32[]{:S(2)}) collective-permute-start(bf16[512,256]{1,0:T(8,128)(2,1)S(1)} %bitcast.58), channel_id=1, source_target_pairs={{0,192},{64,0},{128,64},{192,128},{1,193},{65,1},{129,65},{193,129... | collective-permute-start | bytes 786440 | tf_op jit(solution)/shard_map/ppermute | solution.py:304
  66.5 1.3 %collective-permute-done.17.left = bf16[512,256]{1,0:T(8,128)(2,1)S(1)} collective-permute-done((bf16[512,256]{1,0:T(8,128)(2,1)S(1)}, bf16[512,256]{1,0:T(8,128)(2,1)S(1)}, u32[]{:S(2)}, u32[]{:S(2)}) %collective-permute-start.17) | collective-permute-done | bytes 262176 | tf_op jit(solution)/shard_map/ppermute | solution.py:303
  68.9 1.3 %collective-permute-start.20 = (bf16[256,256]{1,0:T(8,128)(2,1)S(1)}, bf16[256,256]{1,0:T(8,128)(2,1)S(1)}, u32[]{:S(2)}, u32[]{:S(2)}) collective-permute-start(bf16[256,256]{1,0:T(8,128)(2,1)S(1)} %bitcast.72), channel_id=1, source_target_pairs={{0,192},{64,0},{128,64},{192,128},{1,193},{65,1},{129,65},{193,129... | collective-permute-start | bytes 393224 | tf_op jit(solution)/shard_map/ppermute | solution.py:308
  70.8 1.4 %collective-permute-start.12 = (bf16[512,128]{1,0:T(8,128)(2,1)S(1)}, bf16[512,128]{1,0:T(8,128)(2,1)S(1)}, u32[]{:S(2)}, u32[]{:S(2)}) collective-permute-start(bf16[512,128]{1,0:T(8,128)(2,1)S(1)} %conv_back.6), channel_id=1, source_target_pairs={{1,0},{5,4},{9,8},{13,12},{17,16},{21,20},{25,24},{29,28},{33,32},... | collective-permute-start | bytes 393224 | tf_op jit(solution)/shard_map/ppermute | solution.py:374
  72.2 1.3 %collective-permute-start.13 = (bf16[512,128]{1,0:T(8,128)(2,1)S(1)}, bf16[512,128]{1,0:T(8,128)(2,1)S(1)}, u32[]{:S(2)}, u32[]{:S(2)}) collective-permute-start(bf16[512,128]{1,0:T(8,128)(2,1)S(1)} %conv_back.6), channel_id=1, source_target_pairs={{1,4},{5,0},{9,12},{13,8},{17,20},{21,16},{25,28},{29,24},{33,36},... | collective-permute-start | bytes 393224 | tf_op jit(solution)/shard_map/ppermute | solution.py:375
  73.5 9.4 %collective-permute-done.12.refs_0_ = bf16[512,128]{1,0:T(8,128)(2,1)S(1)} collective-permute-done((bf16[512,128]{1,0:T(8,128)(2,1)S(1)}, bf16[512,128]{1,0:T(8,128)(2,1)S(1)}, u32[]{:S(2)}, u32[]{:S(2)}) %collective-permute-start.12) | collective-permute-done | bytes 131104 | tf_op jit(solution)/shard_map/ppermute | solution.py:374
  82.9 4.2 %collective-permute-done.13.refs_1_ = bf16[512,128]{1,0:T(8,128)(2,1)S(1)} collective-permute-done((bf16[512,128]{1,0:T(8,128)(2,1)S(1)}, bf16[512,128]{1,0:T(8,128)(2,1)S(1)}, u32[]{:S(2)}, u32[]{:S(2)}) %collective-permute-start.13) | collective-permute-done | bytes 131104 | tf_op jit(solution)/shard_map/ppermute | solution.py:375
  87.7 1.8 %collective-permute-start.15 = (bf16[512,256]{1,0:T(8,128)(2,1)S(1)}, bf16[512,256]{1,0:T(8,128)(2,1)S(1)}, u32[]{:S(2)}, u32[]{:S(2)}) collective-permute-start(bf16[512,256]{1,0:T(8,128)(2,1)S(1)} %maximum_select_fusion.g_own), channel_id=1, source_target_pairs={{0,192},{64,0},{128,64},{192,128},{1,193},{65,1},{129,65},{193,129... | collective-permute-start | bytes 786440 | tf_op jit(solution)/shard_map/ppermute | solution.py:304
  89.5 3.4 %conv_back.7 = bf16[512,128]{1,0:T(8,128)(2,1)S(1)} custom-call(s32[3]{0:T(128)S(1)} %pad_add_fusion.flags, bf16[512,128]{1,0:T(8,128)(2,1)S(1)} %collective-permute-done.12.refs_0_, bf16[512,128]{1,0:T(8,128)(2,1)S(1)} %collective-permute-done.13.refs_1_, bf16[9,128,128]{2,1,0:T(8,128)(2,1)S(1)} %copy-done.1, bf16[1024,256]{1,0:T(8,128)(2,1)S(1)} %bitcast.56, ...), custom_call_target="tpu_custom_call" | custom-call | flops 905969664 | bytes 1769472 | tf_op jit(solution)/shard_map/conv_back/pallas_call | solution.py:204
  93.9 1.3 %collective-permute-done.15.g_right = bf16[512,256]{1,0:T(8,128)(2,1)S(1)} collective-permute-done((bf16[512,256]{1,0:T(8,128)(2,1)S(1)}, bf16[512,256]{1,0:T(8,128)(2,1)S(1)}, u32[]{:S(2)}, u32[]{:S(2)}) %collective-permute-start.15) | collective-permute-done | bytes 262176 | tf_op jit(solution)/shard_map/ppermute | solution.py:304
  95.5 2.2 %collective-permute-start.22 = (bf16[256,256]{1,0:T(8,128)(2,1)S(1)}, bf16[256,256]{1,0:T(8,128)(2,1)S(1)}, u32[]{:S(2)}, u32[]{:S(2)}) collective-permute-start(bf16[256,256]{1,0:T(8,128)(2,1)S(1)} %bitcast.74), channel_id=1, source_target_pairs={{0,192},{64,0},{128,64},{192,128},{1,193},{65,1},{129,65},{193,129... | collective-permute-start | bytes 393224 | tf_op jit(solution)/shard_map/ppermute | solution.py:308
  97.7 2.6 %collective-permute-done.21.g_far_a = bf16[256,256]{1,0:T(8,128)(2,1)S(1)} collective-permute-done((bf16[256,256]{1,0:T(8,128)(2,1)S(1)}, bf16[256,256]{1,0:T(8,128)(2,1)S(1)}, u32[]{:S(2)}, u32[]{:S(2)}) %collective-permute-start.21) | collective-permute-done | bytes 131104 | tf_op jit(solution)/shard_map/ppermute | solution.py:307
  100.3 1.7 %collective-permute-done.22.g_far_b = bf16[256,256]{1,0:T(8,128)(2,1)S(1)} collective-permute-done((bf16[256,256]{1,0:T(8,128)(2,1)S(1)}, bf16[256,256]{1,0:T(8,128)(2,1)S(1)}, u32[]{:S(2)}, u32[]{:S(2)}) %collective-permute-start.22) | collective-permute-done | bytes 131104 | tf_op jit(solution)/shard_map/ppermute | solution.py:308
  102.0 6.0 %weight_back.1 = bf16[8,108,256]{2,1,0:T(8,128)(2,1)} custom-call(s32[3]{0:T(128)S(1)} %pad_add_fusion.flags, bf16[512,256]{1,0:T(8,128)(2,1)S(1)} %bitcast.59, bf16[512,256]{1,0:T(8,128)(2,1)S(1)} %collective-permute-done.17.left, bf16[512,256]{1,0:T(8,128)(2,1)S(1)} %collective-permute-done.18.right, bf16[256,256]{1,0:T(8,128)(2,1)S(1)} %collective-permute-done.19.far_a, ...), custom_call_target="tpu_custom_call" | custom-call | flops 905969664 | bytes 6291456 | tf_op jit(solution)/shard_map/weight_back/pallas_call | solution.py:278
  108.0 3.5 %all-to-all-start.1 = ((bf16[8,108,256]{2,1,0:T(8,128)(2,1)}), bf16[8,108,256]{2,1,0:T(8,128)(2,1)S(1)}, u32[]{:S(2)}, u32[]{:S(2)}) async-start(bf16[8,108,256]{2,1,0:T(8,128)(2,1)} %weight_back.1), calls=%async_computation.1 | async-start | bytes 917504 | tf_op jit(solution)/shard_map/all_to_all | solution.py:388
  111.5 2.1 %collective-permute-start.16 = (bf16[4,2,32,128]{3,2,1,0:T(8,128)(2,1)S(1)}, bf16[4,2,32,128]{3,2,1,0:T(8,128)(2,1)S(1)}, u32[]{:S(2)}, u32[]{:S(2)}) collective-permute-start(bf16[4,2,32,128]{3,2,1,0:T(8,128)(2,1)S(1)} %get-tuple-element.26), channel_id=1, source_target_pairs={{0,4},{4,0},{1,5},{5,1},{2,6},{6,2},{3,7},{7,3},{8,12},{12,8},{9,1... | collective-permute-start | bytes 196616 | tf_op jit(solution)/shard_map/ppermute | solution.py:384
  113.6 3.7 %collective-permute-done.16 = bf16[4,2,32,128]{3,2,1,0:T(8,128)(2,1)S(1)} collective-permute-done((bf16[4,2,32,128]{3,2,1,0:T(8,128)(2,1)S(1)}, bf16[4,2,32,128]{3,2,1,0:T(8,128)(2,1)S(1)}, u32[]{:S(2)}, u32[]{:S(2)}) %collective-permute-start.16) | collective-permute-done | bytes 65568 | tf_op jit(solution)/shard_map/ppermute | solution.py:384
  118.2 5.9 %all-to-all-done.1 = bf16[8,108,256]{2,1,0:T(8,128)(2,1)S(1)} async-done(((bf16[8,108,256]{2,1,0:T(8,128)(2,1)}), bf16[8,108,256]{2,1,0:T(8,128)(2,1)S(1)}, u32[]{:S(2)}, u32[]{:S(2)}) %all-to-all-start.1) | async-done | bytes 442400 | tf_op jit(solution)/shard_map/all_to_all | solution.py:388
  (80 shorter events, 19.1 us)
Async XLA Ops:
  0.6 0.8 copy-start
  1.7 6.4 %collective-permute-start = (bf16[128,256]{1,0:T(8,128)(2,1)S(1)}, bf16[128,256]{1,0:T(8,128)(2,1)S(1)}, u32[]{:S(2)}, u32[]{:S(2)}) collective-permute-start(bf16[128,256]{1,0:T(8,128)(2,1)S(1)} %constant_dynamic-slice_fusion.6), channel_id=1, source_target_pairs={{0,4},{4,0},{1,5},{5,1},{2,6},{6,2},{3,7},{7,3},{8,12},{12,8},{9,1... | collective-permute-start | bytes 196616 | tf_op jit(solution)/shard_map/ppermute | solution.py:342
  7.2 12.9 %copy-start.9 = (bf16[1,2,4,8,4,256]{5,4,3,2,1,0:T(4,128)(2,1)S(1)}, bf16[1,2,4,8,4,256]{5,4,3,2,1,0:T(4,128)(2,1)}, u32[]{:S(2)}) copy-start(bf16[1,2,4,8,4,256]{5,4,3,2,1,0:T(4,128)(2,1)} %param.8) | copy-start | bytes 393220
  8.1 13.1 %copy-start.4 = (f32[1,256]{1,0:T(1,128)S(1)}, f32[1,256]{1,0:T(1,128)}, u32[]{:S(2)}) copy-start(f32[1,256]{1,0:T(1,128)} %shift_ref.1) | copy-start | bytes 3076
  8.1 13.1 %copy-start.6 = (f32[1,256]{1,0:T(1,128)S(1)}, f32[1,256]{1,0:T(1,128)}, u32[]{:S(2)}) copy-start(f32[1,256]{1,0:T(1,128)} %gain_ref.1) | copy-start | bytes 3076
  8.9 25.7 %all-to-all-start = ((bf16[8,128,256]{2,1,0:T(8,128)(2,1)}), bf16[8,128,256]{2,1,0:T(8,128)(2,1)S(1)}, u32[]{:S(2)}, u32[]{:S(2)}) async-start(bf16[8,128,256]{2,1,0:T(8,128)(2,1)} %broadcast_in_dim.4), calls=%async_computation | async-start | bytes 1048576 | tf_op jit(solution)/shard_map/all_to_all | solution.py:346
  17.4 6.6 %collective-permute-start.4 = (bf16[256,128]{1,0:T(8,128)(2,1)S(1)}, bf16[256,128]{1,0:T(8,128)(2,1)S(1)}, u32[]{:S(2)}, u32[]{:S(2)}) collective-permute-start(bf16[256,128]{1,0:T(8,128)(2,1)S(1)} %get-tuple-element.48), channel_id=1, source_target_pairs={{0,4},{4,0},{1,5},{5,1},{2,6},{6,2},{3,7},{7,3},{8,12},{12,8},{9,1... | collective-permute-start | bytes 196616 | tf_op jit(solution)/shard_map/ppermute | solution.py:350
  20.2 7.2 %collective-permute-start.3 = (bf16[4,1,64,256]{3,2,1,0:T(8,128)(2,1)S(1)}, bf16[4,1,64,256]{3,2,1,0:T(8,128)(2,1)S(1)}, u32[]{:S(2)}, u32[]{:S(2)}) collective-permute-start(bf16[4,1,64,256]{3,2,1,0:T(8,128)(2,1)S(1)} %bitcast.67), channel_id=1, source_target_pairs={{0,4},{4,0},{1,5},{5,1},{2,6},{6,2},{3,7},{7,3},{8,12},{12,8},{9,1... | collective-permute-start | bytes 393224 | tf_op jit(solution)/shard_map/ppermute | solution.py:355
  21.2 16.2 %collective-permute-start.5 = (bf16[4,1,64,256]{3,2,1,0:T(8,128)(2,1)S(1)}, bf16[4,1,64,256]{3,2,1,0:T(8,128)(2,1)S(1)}, u32[]{:S(2)}, u32[]{:S(2)}) collective-permute-start(bf16[4,1,64,256]{3,2,1,0:T(8,128)(2,1)S(1)} %bitcast.64), channel_id=1, source_target_pairs={{0,4},{4,0},{1,5},{5,1},{2,6},{6,2},{3,7},{7,3},{8,12},{12,8},{9,1... | collective-permute-start | bytes 393224 | tf_op jit(solution)/shard_map/ppermute | solution.py:358
  34.6 12.9 %collective-permute-start.1 = (bf16[1024,256]{1,0:T(8,128)(2,1)S(1)}, bf16[1024,256]{1,0:T(8,128)(2,1)S(1)}, u32[]{:S(2)}, u32[]{:S(2)}) collective-permute-start(bf16[1024,256]{1,0:T(8,128)(2,1)S(1)} %bitcast.51), channel_id=1, source_target_pairs={{0,64},{64,128},{128,192},{192,0},{1,65},{65,129},{129,193},{193,1... | collective-permute-start | bytes 1572872 | tf_op jit(solution)/shard_map/ppermute | solution.py:303
  35.1 13.9 %collective-permute-start.2 = (bf16[1024,256]{1,0:T(8,128)(2,1)S(1)}, bf16[1024,256]{1,0:T(8,128)(2,1)S(1)}, u32[]{:S(2)}, u32[]{:S(2)}) collective-permute-start(bf16[1024,256]{1,0:T(8,128)(2,1)S(1)} %bitcast.52), channel_id=1, source_target_pairs={{0,192},{64,0},{128,64},{192,128},{1,193},{65,1},{129,65},{193,129... | collective-permute-start | bytes 1572872 | tf_op jit(solution)/shard_map/ppermute | solution.py:304
  37.4 19.6 %copy-start.1 = (bf16[9,128,128]{2,1,0:T(8,128)(2,1)S(1)}, bf16[9,128,128]{2,1,0:T(8,128)(2,1)}, u32[]{:S(2)}) copy-start(bf16[9,128,128]{2,1,0:T(8,128)(2,1)} %constant.51.clone.refs_2_) | copy-start | bytes 884740
  49.0 6.4 %collective-permute-start.6 = (bf16[512,256]{1,0:T(8,128)(2,1)S(1)}, bf16[512,256]{1,0:T(8,128)(2,1)S(1)}, u32[]{:S(2)}, u32[]{:S(2)}) collective-permute-start(bf16[512,256]{1,0:T(8,128)(2,1)S(1)} %slice.18), channel_id=1, source_target_pairs={{0,64},{64,128},{128,192},{192,0},{1,65},{65,129},{129,193},{193,1... | collective-permute-start | bytes 786440 | tf_op jit(solution)/shard_map/ppermute | solution.py:307
  49.3 7.7 %collective-permute-start.7 = (bf16[512,256]{1,0:T(8,128)(2,1)S(1)}, bf16[512,256]{1,0:T(8,128)(2,1)S(1)}, u32[]{:S(2)}, u32[]{:S(2)}) collective-permute-start(bf16[512,256]{1,0:T(8,128)(2,1)S(1)} %slice.19), channel_id=1, source_target_pairs={{0,192},{64,0},{128,64},{192,128},{1,193},{65,1},{129,65},{193,129... | collective-permute-start | bytes 786440 | tf_op jit(solution)/shard_map/ppermute | solution.py:308
  58.3 4.7 %collective-permute-start.8 = (bf16[512,128]{1,0:T(8,128)(2,1)}, bf16[512,128]{1,0:T(8,128)(2,1)}, u32[]{:S(2)}, u32[]{:S(2)}) collective-permute-start(bf16[512,128]{1,0:T(8,128)(2,1)} %conv_back.4), channel_id=1, source_target_pairs={{3,2},{7,6},{11,10},{15,14},{19,18},{23,22},{27,26},{31,30},{35,34... | collective-permute-start | bytes 393224 | tf_op jit(solution)/shard_map/ppermute | solution.py:374
  59.6 3.3 %collective-permute-start.9 = (bf16[512,128]{1,0:T(8,128)(2,1)}, bf16[512,128]{1,0:T(8,128)(2,1)}, u32[]{:S(2)}, u32[]{:S(2)}) collective-permute-start(bf16[512,128]{1,0:T(8,128)(2,1)} %conv_back.4), channel_id=1, source_target_pairs={{3,6},{7,2},{11,14},{15,10},{19,22},{23,18},{27,30},{31,26},{35,38... | collective-permute-start | bytes 393224 | tf_op jit(solution)/shard_map/ppermute | solution.py:375
  60.9 6.9 %collective-permute-start.17 = (bf16[512,256]{1,0:T(8,128)(2,1)S(1)}, bf16[512,256]{1,0:T(8,128)(2,1)S(1)}, u32[]{:S(2)}, u32[]{:S(2)}) collective-permute-start(bf16[512,256]{1,0:T(8,128)(2,1)S(1)} %bitcast.57), channel_id=1, source_target_pairs={{0,64},{64,128},{128,192},{192,0},{1,65},{65,129},{129,193},{193,1... | collective-permute-start | bytes 786440 | tf_op jit(solution)/shard_map/ppermute | solution.py:303
  61.2 7.7 %collective-permute-start.18 = (bf16[512,256]{1,0:T(8,128)(2,1)S(1)}, bf16[512,256]{1,0:T(8,128)(2,1)S(1)}, u32[]{:S(2)}, u32[]{:S(2)}) collective-permute-start(bf16[512,256]{1,0:T(8,128)(2,1)S(1)} %bitcast.58), channel_id=1, source_target_pairs={{0,192},{64,0},{128,64},{192,128},{1,193},{65,1},{129,65},{193,129... | collective-permute-start | bytes 786440 | tf_op jit(solution)/shard_map/ppermute | solution.py:304
  64.2 6.0 %collective-permute-start.10 = (bf16[512,128]{1,0:T(8,128)(2,1)S(1)}, bf16[512,128]{1,0:T(8,128)(2,1)S(1)}, u32[]{:S(2)}, u32[]{:S(2)}) collective-permute-start(bf16[512,128]{1,0:T(8,128)(2,1)S(1)} %conv_back.5), channel_id=1, source_target_pairs={{2,1},{6,5},{10,9},{14,13},{18,17},{22,21},{26,25},{30,29},{34,33}... | collective-permute-start | bytes 393224 | tf_op jit(solution)/shard_map/ppermute | solution.py:374
  64.8 5.3 %collective-permute-start.11 = (bf16[512,128]{1,0:T(8,128)(2,1)S(1)}, bf16[512,128]{1,0:T(8,128)(2,1)S(1)}, u32[]{:S(2)}, u32[]{:S(2)}) collective-permute-start(bf16[512,128]{1,0:T(8,128)(2,1)S(1)} %conv_back.5), channel_id=1, source_target_pairs={{2,5},{6,1},{10,13},{14,9},{18,21},{22,17},{26,29},{30,25},{34,37}... | collective-permute-start | bytes 393224 | tf_op jit(solution)/shard_map/ppermute | solution.py:375
  67.8 29.9 %collective-permute-start.19 = (bf16[256,256]{1,0:T(8,128)(2,1)S(1)}, bf16[256,256]{1,0:T(8,128)(2,1)S(1)}, u32[]{:S(2)}, u32[]{:S(2)}) collective-permute-start(bf16[256,256]{1,0:T(8,128)(2,1)S(1)} %bitcast.71), channel_id=1, source_target_pairs={{0,64},{64,128},{128,192},{192,0},{1,65},{65,129},{129,193},{193,1... | collective-permute-start | bytes 393224 | tf_op jit(solution)/shard_map/ppermute | solution.py:307
  68.9 28.9 %collective-permute-start.20 = (bf16[256,256]{1,0:T(8,128)(2,1)S(1)}, bf16[256,256]{1,0:T(8,128)(2,1)S(1)}, u32[]{:S(2)}, u32[]{:S(2)}) collective-permute-start(bf16[256,256]{1,0:T(8,128)(2,1)S(1)} %bitcast.72), channel_id=1, source_target_pairs={{0,192},{64,0},{128,64},{192,128},{1,193},{65,1},{129,65},{193,129... | collective-permute-start | bytes 393224 | tf_op jit(solution)/shard_map/ppermute | solution.py:308
  70.7 16.4 %copy-start.8 = (bf16[4,2,64,256]{3,2,1,0:T(8,128)(2,1)S(1)}, bf16[4,2,64,256]{3,2,1,0:T(8,128)(2,1)}, u32[]{:S(2)}) copy-start(bf16[4,2,64,256]{3,2,1,0:T(8,128)(2,1)} %copy-done.7) | copy-start | bytes 786436
  70.8 12.1 %collective-permute-start.12 = (bf16[512,128]{1,0:T(8,128)(2,1)S(1)}, bf16[512,128]{1,0:T(8,128)(2,1)S(1)}, u32[]{:S(2)}, u32[]{:S(2)}) collective-permute-start(bf16[512,128]{1,0:T(8,128)(2,1)S(1)} %conv_back.6), channel_id=1, source_target_pairs={{1,0},{5,4},{9,8},{13,12},{17,16},{21,20},{25,24},{29,28},{33,32},... | collective-permute-start | bytes 393224 | tf_op jit(solution)/shard_map/ppermute | solution.py:374
  72.2 14.9 %collective-permute-start.13 = (bf16[512,128]{1,0:T(8,128)(2,1)S(1)}, bf16[512,128]{1,0:T(8,128)(2,1)S(1)}, u32[]{:S(2)}, u32[]{:S(2)}) collective-permute-start(bf16[512,128]{1,0:T(8,128)(2,1)S(1)} %conv_back.6), channel_id=1, source_target_pairs={{1,4},{5,0},{9,12},{13,8},{17,20},{21,16},{25,28},{29,24},{33,36},... | collective-permute-start | bytes 393224 | tf_op jit(solution)/shard_map/ppermute | solution.py:375
  87.4 6.6 %collective-permute-start.14 = (bf16[512,256]{1,0:T(8,128)(2,1)S(1)}, bf16[512,256]{1,0:T(8,128)(2,1)S(1)}, u32[]{:S(2)}, u32[]{:S(2)}) collective-permute-start(bf16[512,256]{1,0:T(8,128)(2,1)S(1)} %maximum_select_fusion.g_own), channel_id=1, source_target_pairs={{0,64},{64,128},{128,192},{192,0},{1,65},{65,129},{129,193},{193,1... | collective-permute-start | bytes 786440 | tf_op jit(solution)/shard_map/ppermute | solution.py:303
  87.7 7.6 %collective-permute-start.15 = (bf16[512,256]{1,0:T(8,128)(2,1)S(1)}, bf16[512,256]{1,0:T(8,128)(2,1)S(1)}, u32[]{:S(2)}, u32[]{:S(2)}) collective-permute-start(bf16[512,256]{1,0:T(8,128)(2,1)S(1)} %maximum_select_fusion.g_own), channel_id=1, source_target_pairs={{0,192},{64,0},{128,64},{192,128},{1,193},{65,1},{129,65},{193,129... | collective-permute-start | bytes 786440 | tf_op jit(solution)/shard_map/ppermute | solution.py:304
  92.8 9.2 %copy-start.2 = (bf16[9,256,256]{2,1,0:T(8,128)(2,1)S(1)}, bf16[9,256,256]{2,1,0:T(8,128)(2,1)}, u32[]{:S(2)}) copy-start(bf16[9,256,256]{2,1,0:T(8,128)(2,1)} %constant.52.clone.s_ref) | copy-start | bytes 3538948
  95.3 5.0 %collective-permute-start.21 = (bf16[256,256]{1,0:T(8,128)(2,1)S(1)}, bf16[256,256]{1,0:T(8,128)(2,1)S(1)}, u32[]{:S(2)}, u32[]{:S(2)}) collective-permute-start(bf16[256,256]{1,0:T(8,128)(2,1)S(1)} %bitcast.73), channel_id=1, source_target_pairs={{0,64},{64,128},{128,192},{192,0},{1,65},{65,129},{129,193},{193,1... | collective-permute-start | bytes 393224 | tf_op jit(solution)/shard_map/ppermute | solution.py:307
  95.5 6.5 %collective-permute-start.22 = (bf16[256,256]{1,0:T(8,128)(2,1)S(1)}, bf16[256,256]{1,0:T(8,128)(2,1)S(1)}, u32[]{:S(2)}, u32[]{:S(2)}) collective-permute-start(bf16[256,256]{1,0:T(8,128)(2,1)S(1)} %bitcast.74), channel_id=1, source_target_pairs={{0,192},{64,0},{128,64},{192,128},{1,193},{65,1},{129,65},{193,129... | collective-permute-start | bytes 393224 | tf_op jit(solution)/shard_map/ppermute | solution.py:308
  108.0 16.0 %all-to-all-start.1 = ((bf16[8,108,256]{2,1,0:T(8,128)(2,1)}), bf16[8,108,256]{2,1,0:T(8,128)(2,1)S(1)}, u32[]{:S(2)}, u32[]{:S(2)}) async-start(bf16[8,108,256]{2,1,0:T(8,128)(2,1)} %weight_back.1), calls=%async_computation.1 | async-start | bytes 917504 | tf_op jit(solution)/shard_map/all_to_all | solution.py:388
  111.5 5.9 %collective-permute-start.16 = (bf16[4,2,32,128]{3,2,1,0:T(8,128)(2,1)S(1)}, bf16[4,2,32,128]{3,2,1,0:T(8,128)(2,1)S(1)}, u32[]{:S(2)}, u32[]{:S(2)}) collective-permute-start(bf16[4,2,32,128]{3,2,1,0:T(8,128)(2,1)S(1)} %get-tuple-element.26), channel_id=1, source_target_pairs={{0,4},{4,0},{1,5},{5,1},{2,6},{6,2},{3,7},{7,3},{8,12},{12,8},{9,1... | collective-permute-start | bytes 196616 | tf_op jit(solution)/shard_map/ppermute | solution.py:384
  (3 other events, 2.1 us)

commit v4 on v3

--- a/solution.py
+++ b/solution.py
@@ -22,7 +22,6 @@
 PAIR = NYH * PART
 CHUNK = NZ * PAIR
 HC = C // NYH
-WIDE = 2 * NX * M * HW
 SLOTS = NZ * HC
 CLIPS = NX * NZ * NYH
 GRANT = 24 << 20
@@ -219,47 +218,39 @@
     )(flags, *g, s, *pieces, fac)
 
 
-def rows_at(t, blocks):
-    own, left, right, far_a, far_b = blocks
-    pair, clip = NYH * M * HW, M * HW
-    return [ref[pl.ds(t * pair, pair), :] for ref in (own, left, right)] + [
-        ref[pl.ds(t * clip, clip), :] for ref in (far_a, far_b)
-    ]
-
-
-def weight_kernel(
-    flags, own, left, right, far_a, far_b, g_own, g_left, g_right, g_far_a, g_far_b, s_ref,
-    out_ref, a_own, a_left, a_right, a_far_a, a_far_b, shifts, turned, at, gbuf, sem,
-):
+def weight_kernel(count, tail, *refs):
+    flags, acts, grads, (s_ref, *before, out_ref) = (
+        refs[0], refs[1 : 1 + count], refs[1 + count : 1 + 2 * count], refs[1 + 2 * count : -4 - count]
+    )
+    held, (turned, at, gbuf, sem) = refs[-4 - count : -4], refs[-4:]
     yh = flags[1]
-    acts = (a_own, a_left, a_right, a_far_a, a_far_b)
-    copies = [
-        pltpu.make_async_copy(src, dst, sem.at[i])
-        for i, (src, dst) in enumerate(
-            zip((own, left, right, far_a, far_b, s_ref), acts + (shifts,))
-        )
-    ]
+    copies = [pltpu.make_async_copy(src, dst, sem.at[i]) for i, (src, dst) in enumerate(zip(acts, held))]
     for copy in copies:
         copy.start()
+    wide = gbuf.shape[0] // F
+
+    def frame(blocks, t):
+        rows = blocks[0].shape[0] // F
+        return jnp.concatenate([ref[pl.ds(t * rows, rows), :] for ref in blocks], axis=0)
+
     for t in range(F):
-        gbuf[pl.ds(t * WIDE, WIDE), :] = jnp.concatenate(
-            rows_at(t, (g_own, g_left, g_right, g_far_a, g_far_b)), axis=0
-        )
-    turned[pl.ds(0, 2)] = jnp.zeros((2, C, WIDE), BF)
+        gbuf[pl.ds(t * wide, wide), :] = frame(grads, t)
+    turned[pl.ds(0, 2)] = jnp.zeros((2, C, wide), BF)
     for copy in copies:
         copy.wait()
     for t in range(F):
-        rows = jnp.concatenate(rows_at(t, acts), axis=0)
-        turned[t + 2] = rows.astype(F32).T.astype(BF)
+        turned[t + 2] = frame(held, t).astype(F32).T.astype(BF)
     first = lax.div(flags[0] * (CHUNK // 64), 4)
     for k in range(8):
         tap = jnp.minimum(first + k, 26)
         kt = lax.div(tap, 9)
-        moved = shifts[lax.rem(tap, 9)]
+        j = lax.rem(tap, 9)
         for t in range(F):
-            for r in range(WIDE // C):
-                at[pl.ds(k * C, C), pl.ds(t * WIDE + r * C, C)] = jnp.dot(
-                    turned[t + kt, :, pl.ds(r * C, C)], moved, preferred_element_type=F32
+            for at_lane in range(0, wide, C):
+                size = min(C, wide - at_lane)
+                moved = s_ref[j, :size, :size]
+                at[pl.ds(k * C, C), pl.ds(t * wide + at_lane, size)] = jnp.dot(
+                    turned[t + kt, :, pl.ds(at_lane, size)], moved, preferred_element_type=F32
                 ).astype(BF)
     offset = lax.rem(flags[0] * (CHUNK // 64), 4) * 64
     for z in range(NZ):
@@ -267,31 +258,36 @@
         start = offset + jnp.where(yh == 0, z * PAIR - skip[0], z * PAIR + PART - skip[1])
         total = jnp.dot(
             at[pl.ds(pl.multiple_of(start, 16), HC), :], gbuf[...], preferred_element_type=F32
-        ) * (1.0 / CLIPS)
-        out_ref[z] = jnp.where(
-            yh == 0, total[skip[0] : skip[0] + PART], total[skip[1] : skip[1] + PART]
-        ).astype(BF)
-
-
-def weight_back(flags, acts, grads, s):
-    pieces = [pltpu.VMEM(v.shape, BF) for v in acts]
+        )
+        if before:
+            total = total + before[0][z]
+        if tail:
+            total = total * (1.0 / CLIPS)
+            total = jnp.where(yh == 0, total[skip[0] : skip[0] + PART], total[skip[1] : skip[1] + PART])
+        out_ref[z] = total.astype(out_ref.dtype)
+
+
+def weight_back(flags, acts, grads, s, before=None):
+    tail = before is not None
+    wide = sum(v.shape[0] // F for v in acts)
     return pl.pallas_call(
-        weight_kernel,
-        out_shape=jax.ShapeDtypeStruct((NZ, PART, C), BF),
-        in_specs=[SMEM] + [HBM] * 5 + [VMEM] * 5 + [HBM],
+        functools.partial(weight_kernel, len(acts), tail),
+        out_shape=jax.ShapeDtypeStruct((NZ, PART if tail else HC, C), BF if tail else F32),
+        in_specs=[SMEM] + [HBM] * len(acts) + [VMEM] * len(grads) + [VMEM] * (1 + tail),
         out_specs=VMEM,
-        scratch_shapes=pieces
+        scratch_shapes=[pltpu.VMEM(v.shape, BF) for v in acts]
         + [
-            pltpu.VMEM((9, C, C), BF),
-            pltpu.VMEM((F + 2, C, WIDE), BF),
-            pltpu.VMEM((8 * C, F * WIDE), BF),
-            pltpu.VMEM((F * WIDE, C), BF),
-            pltpu.SemaphoreType.DMA((6,)),
+            pltpu.VMEM((F + 2, C, wide), BF),
+            pltpu.VMEM((8 * C, F * wide), BF),
+            pltpu.VMEM((F * wide, C), BF),
+            pltpu.SemaphoreType.DMA((len(acts),)),
         ],
         compiler_params=pltpu.CompilerParams(vmem_limit_bytes=GRANT),
-        cost_estimate=pl.CostEstimate(flops=2 * CHUNK * F * C * C, bytes_accessed=6 << 20, transcendentals=0),
-        name="weight_back",
-    )(flags, *acts, *grads, s)
+        cost_estimate=pl.CostEstimate(
+            flops=8 * CHUNK * wide * C, bytes_accessed=4 << 20, transcendentals=0
+        ),
+        name="weight_last" if tail else "weight_first",
+    )(flags, *acts, *grads, s, *([before] if tail else []))
 
 
 def ring(axis, step):
@@ -384,7 +380,8 @@
     got = lax.ppermute(given, "yh", swap)
     dx = in_order(kept, got, -1).transpose(1, 0, 2, 3).reshape(section_inputs.shape)
 
-    partial = weight_back(flags, acts, grads, wide_s)
+    partial = weight_back(flags, acts[:3], grads[:3], wide_s)
+    partial = weight_back(flags, acts[3:], grads[3:], wide_s, partial)
     weight_part = jnp.sum(lax.all_to_all(partial, "z", 0, 0, tiled=True).astype(F32), axis=0)
     return dx, weight_part[None]
 

time: 125 us -> 122 us (0.976)
  waiting for transfers between devices: 57 us -> 54.7 us
  starting transfers between devices: 43.4 us -> 42 us
    ppermute x3, waiting for transfers between devices: 6.87 us -> 4.25 us  [gather_x(): far_a = lax.ppermute(first_half(left), 'x', ring('x', 1))]
    ppermute x3, waiting for transfers between devices: 11.4 us -> 13.1 us  [gather_x(): left = lax.ppermute(block, 'x', ring('x', 1))]
    pallas_call x1 -> x2, Pallas kernels: 5.99 us -> 6.67 us  [weight_back(): pl.pallas_call(functools.partial(weight_kernel, len(acts), tail), out_sha...]
    unnamed x21 -> x23, local copies, waits for them, and re-layouts: 3.56 us -> 3.58 us
  transfers between devices with their start and end apart: 25 -> 25, of which waited for: 14 -> 14; matrix products, arithmetic and copies ran while one was open for 3% -> 3% of each run, Pallas kernels for 6% -> 9%
where the time goes in v4:
time: 122 us; the launch traced here: 121 us
  waiting for transfers between devices  54.7 us (45%)
  starting transfers between devices  42 us (34%)
  Pallas kernels  14.7 us (12%)
  local copies, waits for them, and re-layouts  6.3 us (5%)
  other arithmetic  2.34 us (2%)
    ppermute x3, waiting for transfers between devices, gather_x(): left = lax.ppermute(block, 'x', ring('x', 1))  13.1 us
    ppermute x3, waiting for transfers between devices, local(): same = lax.ppermute(sent, ('yl', 'c'), [(src, dst)])  9.09 us
    all_to_all x1, starting transfers between devices, local(): lax.all_to_all(jnp.broadcast_to(window[None], (NZ, HC, C)), 'z', 0, 0, ti...  8.47 us
    all_to_all x1, waiting for transfers between devices, local(): lax.all_to_all(jnp.broadcast_to(window[None], (NZ, HC, C)), 'z', 0, 0, ti...  7.15 us
    pallas_call x2, Pallas kernels, weight_back(): pl.pallas_call(functools.partial(weight_kernel, len(acts), tail), out_sha...  6.67 us
    pallas_call x4, Pallas kernels, conv_back(): pl.pallas_call(functools.partial(conv_kernel, target), out_shape=jax.Shap...  6.03 us
    all_to_all x1, waiting for transfers between devices, local(): lax.all_to_all(partial, 'z', 0, 0, tiled=True).astype(F32)  5.85 us
    ppermute x3, starting transfers between devices, gather_x(): far_b = lax.ppermute(second_half(right), 'x', ring('x', -1))  5.45 us
  transfers between devices with their start and end apart: 25, of which 14 were waited for; matrix products, arithmetic and copies ran while one was open for 3% of the time, Pallas kernels for 9%

profile of v4, /device:TPU:6, one launch (start us, length us, event | category | flops | bytes accessed | tf_op | source)
XLA Modules:
  0.0 121.3 jit_solution(4561543894198367515)
XLA Ops:
  1.7 3.3 %collective-permute-start = (bf16[128,256]{1,0:T(8,128)(2,1)S(1)}, bf16[128,256]{1,0:T(8,128)(2,1)S(1)}, u32[]{:S(2)}, u32[]{:S(2)}) collective-permute-start(bf16[128,256]{1,0:T(8,128)(2,1)S(1)} %constant_dynamic-slice_fusion.6), channel_id=1, source_target_pairs={{0,4},{4,0},{1,5},{5,1},{2,6},{6,2},{3,7},{7,3},{8,12},{12,8},{9,1... | collective-permute-start | bytes 196616 | tf_op jit(solution)/shard_map/ppermute | solution.py:338
  8.9 8.5 %all-to-all-start = ((bf16[8,128,256]{2,1,0:T(8,128)(2,1)}), bf16[8,128,256]{2,1,0:T(8,128)(2,1)S(1)}, u32[]{:S(2)}, u32[]{:S(2)}) async-start(bf16[8,128,256]{2,1,0:T(8,128)(2,1)} %broadcast_in_dim.4), calls=%async_computation | async-start | bytes 1048576 | tf_op jit(solution)/shard_map/all_to_all | solution.py:342
  17.4 2.7 %collective-permute-start.4 = (bf16[256,128]{1,0:T(8,128)(2,1)S(1)}, bf16[256,128]{1,0:T(8,128)(2,1)S(1)}, u32[]{:S(2)}, u32[]{:S(2)}) collective-permute-start(bf16[256,128]{1,0:T(8,128)(2,1)S(1)} %get-tuple-element.48), channel_id=1, source_target_pairs={{0,4},{4,0},{1,5},{5,1},{2,6},{6,2},{3,7},{7,3},{8,12},{12,8},{9,1... | collective-permute-start | bytes 196616 | tf_op jit(solution)/shard_map/ppermute | solution.py:346
  21.3 2.7 %collective-permute-start.5 = (bf16[4,1,64,256]{3,2,1,0:T(8,128)(2,1)S(1)}, bf16[4,1,64,256]{3,2,1,0:T(8,128)(2,1)S(1)}, u32[]{:S(2)}, u32[]{:S(2)}) collective-permute-start(bf16[4,1,64,256]{3,2,1,0:T(8,128)(2,1)S(1)} %bitcast.57), channel_id=1, source_target_pairs={{0,4},{4,0},{1,5},{5,1},{2,6},{6,2},{3,7},{7,3},{8,12},{12,8},{9,1... | collective-permute-start | bytes 393224 | tf_op jit(solution)/shard_map/ppermute | solution.py:354
  24.0 1.2 norm_factors.1.refs_8_
  25.1 2.3 %collective-permute-done.3 = bf16[4,1,64,256]{3,2,1,0:T(8,128)(2,1)S(1)} collective-permute-done((bf16[4,1,64,256]{3,2,1,0:T(8,128)(2,1)S(1)}, bf16[4,1,64,256]{3,2,1,0:T(8,128)(2,1)S(1)}, u32[]{:S(2)}, u32[]{:S(2)}) %collective-permute-start.3) | collective-permute-done | bytes 131104 | tf_op jit(solution)/shard_map/ppermute | solution.py:351
  27.5 7.1 %all-to-all-done = bf16[8,128,256]{2,1,0:T(8,128)(2,1)S(1)} async-done(((bf16[8,128,256]{2,1,0:T(8,128)(2,1)}), bf16[8,128,256]{2,1,0:T(8,128)(2,1)S(1)}, u32[]{:S(2)}, u32[]{:S(2)}) %all-to-all-start) | async-done | bytes 524320 | tf_op jit(solution)/shard_map/all_to_all | solution.py:342
  35.1 1.5 %collective-permute-start.2 = (bf16[1024,256]{1,0:T(8,128)(2,1)S(1)}, bf16[1024,256]{1,0:T(8,128)(2,1)S(1)}, u32[]{:S(2)}, u32[]{:S(2)}) collective-permute-start(bf16[1024,256]{1,0:T(8,128)(2,1)S(1)} %bitcast.52), channel_id=1, source_target_pairs={{0,192},{64,0},{128,64},{192,128},{1,193},{65,1},{129,65},{193,129... | collective-permute-start | bytes 1572872 | tf_op jit(solution)/shard_map/ppermute | solution.py:300
  38.2 9.3 %collective-permute-done.1.refs_4_ = bf16[1024,256]{1,0:T(8,128)(2,1)S(1)} collective-permute-done((bf16[1024,256]{1,0:T(8,128)(2,1)S(1)}, bf16[1024,256]{1,0:T(8,128)(2,1)S(1)}, u32[]{:S(2)}, u32[]{:S(2)}) %collective-permute-start.1) | collective-permute-done | bytes 524320 | tf_op jit(solution)/shard_map/ppermute | solution.py:299
  47.5 1.4 %collective-permute-done.2.refs_5_ = bf16[1024,256]{1,0:T(8,128)(2,1)S(1)} collective-permute-done((bf16[1024,256]{1,0:T(8,128)(2,1)S(1)}, bf16[1024,256]{1,0:T(8,128)(2,1)S(1)}, u32[]{:S(2)}, u32[]{:S(2)}) %collective-permute-start.2) | collective-permute-done | bytes 524320 | tf_op jit(solution)/shard_map/ppermute | solution.py:300
  49.3 1.8 %collective-permute-start.7 = (bf16[512,256]{1,0:T(8,128)(2,1)S(1)}, bf16[512,256]{1,0:T(8,128)(2,1)S(1)}, u32[]{:S(2)}, u32[]{:S(2)}) collective-permute-start(bf16[512,256]{1,0:T(8,128)(2,1)S(1)} %slice.19), channel_id=1, source_target_pairs={{0,192},{64,0},{128,64},{192,128},{1,193},{65,1},{129,65},{193,129... | collective-permute-start | bytes 786440 | tf_op jit(solution)/shard_map/ppermute | solution.py:304
  51.2 4.2 %collective-permute-done.6.refs_6_ = bf16[512,256]{1,0:T(8,128)(2,1)S(1)} collective-permute-done((bf16[512,256]{1,0:T(8,128)(2,1)S(1)}, bf16[512,256]{1,0:T(8,128)(2,1)S(1)}, u32[]{:S(2)}, u32[]{:S(2)}) %collective-permute-start.6) | collective-permute-done | bytes 262176 | tf_op jit(solution)/shard_map/ppermute | solution.py:303
  55.4 1.6 %collective-permute-done.7.refs_7_ = bf16[512,256]{1,0:T(8,128)(2,1)S(1)} collective-permute-done((bf16[512,256]{1,0:T(8,128)(2,1)S(1)}, bf16[512,256]{1,0:T(8,128)(2,1)S(1)}, u32[]{:S(2)}, u32[]{:S(2)}) %collective-permute-start.7) | collective-permute-done | bytes 262176 | tf_op jit(solution)/shard_map/ppermute | solution.py:304
  57.0 1.3 %conv_back.4 = bf16[512,128]{1,0:T(8,128)(2,1)} custom-call(s32[3]{0:T(128)S(1)} %pad_add_fusion.flags.refs_0_, bf16[512,128]{1,0:T(8,128)(2,1)S(1)} %get-tuple-element.18.refs_0_, bf16[512,128]{1,0:T(8,128)(2,1)S(1)} %get-tuple-element.19.refs_1_, bf16[9,128,128]{2,1,0:T(8,128)(2,1)S(1)} %copy-done.1, bf16[1024,256]{1,0:T(8,128)(2,1)S(1)} %bitcast.53, ...), custom_call_target="tpu_custom_call" | custom-call | flops 905969664 | bytes 1769472 | tf_op jit(solution)/shard_map/conv_back/pallas_call | solution.py:203
  60.0 1.7 %collective-permute-start.19 = (bf16[512,256]{1,0:T(8,128)(2,1)}, bf16[512,256]{1,0:T(8,128)(2,1)S(1)}, u32[]{:S(2)}, u32[]{:S(2)}) collective-permute-start(bf16[512,256]{1,0:T(8,128)(2,1)} %bitcast.60), channel_id=1, source_target_pairs={{0,192},{64,0},{128,64},{192,128},{1,193},{65,1},{129,65},{193,129... | collective-permute-start | bytes 786440 | tf_op jit(solution)/shard_map/ppermute | solution.py:300
  63.9 3.8 %collective-permute-done.17.refs_2_ = bf16[512,256]{1,0:T(8,128)(2,1)S(1)} collective-permute-done((bf16[512,256]{1,0:T(8,128)(2,1)}, bf16[512,256]{1,0:T(8,128)(2,1)S(1)}, u32[]{:S(2)}, u32[]{:S(2)}) %collective-permute-start.17) | collective-permute-done | bytes 262176 | tf_op jit(solution)/shard_map/ppermute | solution.py:299
  68.4 1.5 %collective-permute-start.20 = (bf16[256,256]{1,0:T(8,128)(2,1)S(1)}, bf16[256,256]{1,0:T(8,128)(2,1)S(1)}, u32[]{:S(2)}, u32[]{:S(2)}) collective-permute-start(bf16[256,256]{1,0:T(8,128)(2,1)S(1)} %bitcast.72), channel_id=1, source_target_pairs={{0,192},{64,0},{128,64},{192,128},{1,193},{65,1},{129,65},{193,129... | collective-permute-start | bytes 393224 | tf_op jit(solution)/shard_map/ppermute | solution.py:304
  70.5 1.4 %collective-permute-start.12 = (bf16[512,128]{1,0:T(8,128)(2,1)S(1)}, bf16[512,128]{1,0:T(8,128)(2,1)S(1)}, u32[]{:S(2)}, u32[]{:S(2)}) collective-permute-start(bf16[512,128]{1,0:T(8,128)(2,1)S(1)} %conv_back.6), channel_id=1, source_target_pairs={{1,0},{5,4},{9,8},{13,12},{17,16},{21,20},{25,24},{29,28},{33,32},... | collective-permute-start | bytes 393224 | tf_op jit(solution)/shard_map/ppermute | solution.py:370
  72.0 1.3 %collective-permute-start.13 = (bf16[512,128]{1,0:T(8,128)(2,1)S(1)}, bf16[512,128]{1,0:T(8,128)(2,1)S(1)}, u32[]{:S(2)}, u32[]{:S(2)}) collective-permute-start(bf16[512,128]{1,0:T(8,128)(2,1)S(1)} %conv_back.6), channel_id=1, source_target_pairs={{1,4},{5,0},{9,12},{13,8},{17,20},{21,16},{25,28},{29,24},{33,36},... | collective-permute-start | bytes 393224 | tf_op jit(solution)/shard_map/ppermute | solution.py:371
  73.3 9.1 %collective-permute-done.12.refs_0_ = bf16[512,128]{1,0:T(8,128)(2,1)S(1)} collective-permute-done((bf16[512,128]{1,0:T(8,128)(2,1)S(1)}, bf16[512,128]{1,0:T(8,128)(2,1)S(1)}, u32[]{:S(2)}, u32[]{:S(2)}) %collective-permute-start.12) | collective-permute-done | bytes 131104 | tf_op jit(solution)/shard_map/ppermute | solution.py:370
  82.4 4.2 %collective-permute-done.13.refs_1_ = bf16[512,128]{1,0:T(8,128)(2,1)S(1)} collective-permute-done((bf16[512,128]{1,0:T(8,128)(2,1)S(1)}, bf16[512,128]{1,0:T(8,128)(2,1)S(1)}, u32[]{:S(2)}, u32[]{:S(2)}) %collective-permute-start.13) | collective-permute-done | bytes 131104 | tf_op jit(solution)/shard_map/ppermute | solution.py:371
  87.2 1.8 %collective-permute-start.15 = (bf16[512,256]{1,0:T(8,128)(2,1)S(1)}, bf16[512,256]{1,0:T(8,128)(2,1)S(1)}, u32[]{:S(2)}, u32[]{:S(2)}) collective-permute-start(bf16[512,256]{1,0:T(8,128)(2,1)S(1)} %maximum_select_fusion.refs_4_), channel_id=1, source_target_pairs={{0,192},{64,0},{128,64},{192,128},{1,193},{65,1},{129,65},{193,129... | collective-permute-start | bytes 786440 | tf_op jit(solution)/shard_map/ppermute | solution.py:300
  89.0 3.4 %conv_back.7 = bf16[512,128]{1,0:T(8,128)(2,1)S(1)} custom-call(s32[3]{0:T(128)S(1)} %pad_add_fusion.flags.refs_0_, bf16[512,128]{1,0:T(8,128)(2,1)S(1)} %collective-permute-done.12.refs_0_, bf16[512,128]{1,0:T(8,128)(2,1)S(1)} %collective-permute-done.13.refs_1_, bf16[9,128,128]{2,1,0:T(8,128)(2,1)S(1)} %copy-done.1, bf16[1024,256]{1,0:T(8,128)(2,1)S(1)} %bitcast.56, ...), custom_call_target="tpu_custom_call" | custom-call | flops 905969664 | bytes 1769472 | tf_op jit(solution)/shard_map/conv_back/pallas_call | solution.py:203
  92.4 1.1 select_select_fusion
  93.5 1.3 %collective-permute-done.15.refs_6_ = bf16[512,256]{1,0:T(8,128)(2,1)S(1)} collective-permute-done((bf16[512,256]{1,0:T(8,128)(2,1)S(1)}, bf16[512,256]{1,0:T(8,128)(2,1)S(1)}, u32[]{:S(2)}, u32[]{:S(2)}) %collective-permute-start.15) | collective-permute-done | bytes 262176 | tf_op jit(solution)/shard_map/ppermute | solution.py:300
  95.1 2.1 %collective-permute-start.22 = (bf16[256,256]{1,0:T(8,128)(2,1)S(1)}, bf16[256,256]{1,0:T(8,128)(2,1)S(1)}, u32[]{:S(2)}, u32[]{:S(2)}) collective-permute-start(bf16[256,256]{1,0:T(8,128)(2,1)S(1)} %bitcast.74), channel_id=1, source_target_pairs={{0,192},{64,0},{128,64},{192,128},{1,193},{65,1},{129,65},{193,129... | collective-permute-start | bytes 393224 | tf_op jit(solution)/shard_map/ppermute | solution.py:304
  97.2 3.7 %weight_first.1.refs_6_ = f32[8,128,256]{2,1,0:T(8,128)S(1)} custom-call(s32[3]{0:T(128)S(1)} %pad_add_fusion.flags.refs_0_, bf16[512,256]{1,0:T(8,128)(2,1)S(1)} %bitcast.61, bf16[512,256]{1,0:T(8,128)(2,1)S(1)} %collective-permute-done.17.refs_2_, bf16[512,256]{1,0:T(8,128)(2,1)S(1)} %collective-permute-done.19.refs_3_, ...), custom_call_target="tpu_custom_call" | custom-call | flops 1358954496 | bytes 4194304 | tf_op jit(solution)/shard_map/weight_first/pallas_call | solution.py:273
  101.5 2.9 %weight_last.1 = bf16[8,108,256]{2,1,0:T(8,128)(2,1)} custom-call(s32[3]{0:T(128)S(1)} %pad_add_fusion.flags.refs_0_, bf16[256,256]{1,0:T(8,128)(2,1)S(1)} %collective-permute-done.18.refs_1_, bf16[256,256]{1,0:T(8,128)(2,1)S(1)} %collective-permute-done.20.refs_2_, bf16[256,256]{1,0:T(8,128)(2,1)S(1)} %collective-permute-done.21.refs_3_, ...), custom_call_target="tpu_custom_call" | custom-call | flops 452984832 | bytes 4194304 | tf_op jit(solution)/shard_map/weight_last/pallas_call | solution.py:273
  104.5 3.5 %all-to-all-start.1 = ((bf16[8,108,256]{2,1,0:T(8,128)(2,1)}), bf16[8,108,256]{2,1,0:T(8,128)(2,1)S(1)}, u32[]{:S(2)}, u32[]{:S(2)}) async-start(bf16[8,108,256]{2,1,0:T(8,128)(2,1)} %weight_last.1), calls=%async_computation.1 | async-start | bytes 917504 | tf_op jit(solution)/shard_map/all_to_all | solution.py:385
  108.0 2.1 %collective-permute-start.16 = (bf16[4,2,32,128]{3,2,1,0:T(8,128)(2,1)S(1)}, bf16[4,2,32,128]{3,2,1,0:T(8,128)(2,1)S(1)}, u32[]{:S(2)}, u32[]{:S(2)}) collective-permute-start(bf16[4,2,32,128]{3,2,1,0:T(8,128)(2,1)S(1)} %get-tuple-element.26), channel_id=1, source_target_pairs={{0,4},{4,0},{1,5},{5,1},{2,6},{6,2},{3,7},{7,3},{8,12},{12,8},{9,1... | collective-permute-start | bytes 196616 | tf_op jit(solution)/shard_map/ppermute | solution.py:380
  110.1 3.7 %collective-permute-done.16 = bf16[4,2,32,128]{3,2,1,0:T(8,128)(2,1)S(1)} collective-permute-done((bf16[4,2,32,128]{3,2,1,0:T(8,128)(2,1)S(1)}, bf16[4,2,32,128]{3,2,1,0:T(8,128)(2,1)S(1)}, u32[]{:S(2)}, u32[]{:S(2)}) %collective-permute-start.16) | collective-permute-done | bytes 65568 | tf_op jit(solution)/shard_map/ppermute | solution.py:380
  114.6 5.9 %all-to-all-done.1 = bf16[8,108,256]{2,1,0:T(8,128)(2,1)S(1)} async-done(((bf16[8,108,256]{2,1,0:T(8,128)(2,1)}), bf16[8,108,256]{2,1,0:T(8,128)(2,1)S(1)}, u32[]{:S(2)}, u32[]{:S(2)}) %all-to-all-start.1) | async-done | bytes 442400 | tf_op jit(solution)/shard_map/all_to_all | solution.py:385
  (83 shorter events, 16.6 us)
Async XLA Ops:
  1.7 6.4 %collective-permute-start = (bf16[128,256]{1,0:T(8,128)(2,1)S(1)}, bf16[128,256]{1,0:T(8,128)(2,1)S(1)}, u32[]{:S(2)}, u32[]{:S(2)}) collective-permute-start(bf16[128,256]{1,0:T(8,128)(2,1)S(1)} %constant_dynamic-slice_fusion.6), channel_id=1, source_target_pairs={{0,4},{4,0},{1,5},{5,1},{2,6},{6,2},{3,7},{7,3},{8,12},{12,8},{9,1... | collective-permute-start | bytes 196616 | tf_op jit(solution)/shard_map/ppermute | solution.py:338
  7.2 12.9 %copy-start.10 = (bf16[1,2,4,8,4,256]{5,4,3,2,1,0:T(4,128)(2,1)S(1)}, bf16[1,2,4,8,4,256]{5,4,3,2,1,0:T(4,128)(2,1)}, u32[]{:S(2)}) copy-start(bf16[1,2,4,8,4,256]{5,4,3,2,1,0:T(4,128)(2,1)} %param.8) | copy-start | bytes 393220
  8.1 13.1 %copy-start.5 = (f32[1,256]{1,0:T(1,128)S(1)}, f32[1,256]{1,0:T(1,128)}, u32[]{:S(2)}) copy-start(f32[1,256]{1,0:T(1,128)} %shift_ref.1) | copy-start | bytes 3076
  8.1 13.1 %copy-start.7 = (f32[1,256]{1,0:T(1,128)S(1)}, f32[1,256]{1,0:T(1,128)}, u32[]{:S(2)}) copy-start(f32[1,256]{1,0:T(1,128)} %gain_ref.1) | copy-start | bytes 3076
  8.9 25.7 %all-to-all-start = ((bf16[8,128,256]{2,1,0:T(8,128)(2,1)}), bf16[8,128,256]{2,1,0:T(8,128)(2,1)S(1)}, u32[]{:S(2)}, u32[]{:S(2)}) async-start(bf16[8,128,256]{2,1,0:T(8,128)(2,1)} %broadcast_in_dim.4), calls=%async_computation | async-start | bytes 1048576 | tf_op jit(solution)/shard_map/all_to_all | solution.py:342
  17.4 6.6 %collective-permute-start.4 = (bf16[256,128]{1,0:T(8,128)(2,1)S(1)}, bf16[256,128]{1,0:T(8,128)(2,1)S(1)}, u32[]{:S(2)}, u32[]{:S(2)}) collective-permute-start(bf16[256,128]{1,0:T(8,128)(2,1)S(1)} %get-tuple-element.48), channel_id=1, source_target_pairs={{0,4},{4,0},{1,5},{5,1},{2,6},{6,2},{3,7},{7,3},{8,12},{12,8},{9,1... | collective-permute-start | bytes 196616 | tf_op jit(solution)/shard_map/ppermute | solution.py:346
  20.2 7.2 %collective-permute-start.3 = (bf16[4,1,64,256]{3,2,1,0:T(8,128)(2,1)S(1)}, bf16[4,1,64,256]{3,2,1,0:T(8,128)(2,1)S(1)}, u32[]{:S(2)}, u32[]{:S(2)}) collective-permute-start(bf16[4,1,64,256]{3,2,1,0:T(8,128)(2,1)S(1)} %bitcast.67), channel_id=1, source_target_pairs={{0,4},{4,0},{1,5},{5,1},{2,6},{6,2},{3,7},{7,3},{8,12},{12,8},{9,1... | collective-permute-start | bytes 393224 | tf_op jit(solution)/shard_map/ppermute | solution.py:351
  21.3 16.2 %collective-permute-start.5 = (bf16[4,1,64,256]{3,2,1,0:T(8,128)(2,1)S(1)}, bf16[4,1,64,256]{3,2,1,0:T(8,128)(2,1)S(1)}, u32[]{:S(2)}, u32[]{:S(2)}) collective-permute-start(bf16[4,1,64,256]{3,2,1,0:T(8,128)(2,1)S(1)} %bitcast.57), channel_id=1, source_target_pairs={{0,4},{4,0},{1,5},{5,1},{2,6},{6,2},{3,7},{7,3},{8,12},{12,8},{9,1... | collective-permute-start | bytes 393224 | tf_op jit(solution)/shard_map/ppermute | solution.py:354
  34.6 12.9 %collective-permute-start.1 = (bf16[1024,256]{1,0:T(8,128)(2,1)S(1)}, bf16[1024,256]{1,0:T(8,128)(2,1)S(1)}, u32[]{:S(2)}, u32[]{:S(2)}) collective-permute-start(bf16[1024,256]{1,0:T(8,128)(2,1)S(1)} %bitcast.51), channel_id=1, source_target_pairs={{0,64},{64,128},{128,192},{192,0},{1,65},{65,129},{129,193},{193,1... | collective-permute-start | bytes 1572872 | tf_op jit(solution)/shard_map/ppermute | solution.py:299
  35.1 13.9 %collective-permute-start.2 = (bf16[1024,256]{1,0:T(8,128)(2,1)S(1)}, bf16[1024,256]{1,0:T(8,128)(2,1)S(1)}, u32[]{:S(2)}, u32[]{:S(2)}) collective-permute-start(bf16[1024,256]{1,0:T(8,128)(2,1)S(1)} %bitcast.52), channel_id=1, source_target_pairs={{0,192},{64,0},{128,64},{192,128},{1,193},{65,1},{129,65},{193,129... | collective-permute-start | bytes 1572872 | tf_op jit(solution)/shard_map/ppermute | solution.py:300
  37.4 19.6 %copy-start.1 = (bf16[9,128,128]{2,1,0:T(8,128)(2,1)S(1)}, bf16[9,128,128]{2,1,0:T(8,128)(2,1)}, u32[]{:S(2)}) copy-start(bf16[9,128,128]{2,1,0:T(8,128)(2,1)} %constant.51.clone.refs_2_) | copy-start | bytes 884740
  49.0 6.4 %collective-permute-start.6 = (bf16[512,256]{1,0:T(8,128)(2,1)S(1)}, bf16[512,256]{1,0:T(8,128)(2,1)S(1)}, u32[]{:S(2)}, u32[]{:S(2)}) collective-permute-start(bf16[512,256]{1,0:T(8,128)(2,1)S(1)} %slice.18), channel_id=1, source_target_pairs={{0,64},{64,128},{128,192},{192,0},{1,65},{65,129},{129,193},{193,1... | collective-permute-start | bytes 786440 | tf_op jit(solution)/shard_map/ppermute | solution.py:303
  49.3 7.7 %collective-permute-start.7 = (bf16[512,256]{1,0:T(8,128)(2,1)S(1)}, bf16[512,256]{1,0:T(8,128)(2,1)S(1)}, u32[]{:S(2)}, u32[]{:S(2)}) collective-permute-start(bf16[512,256]{1,0:T(8,128)(2,1)S(1)} %slice.19), channel_id=1, source_target_pairs={{0,192},{64,0},{128,64},{192,128},{1,193},{65,1},{129,65},{193,129... | collective-permute-start | bytes 786440 | tf_op jit(solution)/shard_map/ppermute | solution.py:304
  58.3 3.5 %collective-permute-start.8 = (bf16[512,128]{1,0:T(8,128)(2,1)}, bf16[512,128]{1,0:T(8,128)(2,1)S(1)}, u32[]{:S(2)}, u32[]{:S(2)}) collective-permute-start(bf16[512,128]{1,0:T(8,128)(2,1)} %conv_back.4), channel_id=1, source_target_pairs={{3,2},{7,6},{11,10},{15,14},{19,18},{23,22},{27,26},{31,30},{35,34... | collective-permute-start | bytes 393224 | tf_op jit(solution)/shard_map/ppermute | solution.py:370
  59.0 2.8 %collective-permute-start.9 = (bf16[512,128]{1,0:T(8,128)(2,1)}, bf16[512,128]{1,0:T(8,128)(2,1)S(1)}, u32[]{:S(2)}, u32[]{:S(2)}) collective-permute-start(bf16[512,128]{1,0:T(8,128)(2,1)} %conv_back.4), channel_id=1, source_target_pairs={{3,6},{7,2},{11,14},{15,10},{19,22},{23,18},{27,30},{31,26},{35,38... | collective-permute-start | bytes 393224 | tf_op jit(solution)/shard_map/ppermute | solution.py:371
  59.6 8.1 %collective-permute-start.17 = (bf16[512,256]{1,0:T(8,128)(2,1)}, bf16[512,256]{1,0:T(8,128)(2,1)S(1)}, u32[]{:S(2)}, u32[]{:S(2)}) collective-permute-start(bf16[512,256]{1,0:T(8,128)(2,1)} %bitcast.59), channel_id=1, source_target_pairs={{0,64},{64,128},{128,192},{192,0},{1,65},{65,129},{129,193},{193,1... | collective-permute-start | bytes 786440 | tf_op jit(solution)/shard_map/ppermute | solution.py:299
  60.0 8.4 %collective-permute-start.19 = (bf16[512,256]{1,0:T(8,128)(2,1)}, bf16[512,256]{1,0:T(8,128)(2,1)S(1)}, u32[]{:S(2)}, u32[]{:S(2)}) collective-permute-start(bf16[512,256]{1,0:T(8,128)(2,1)} %bitcast.60), channel_id=1, source_target_pairs={{0,192},{64,0},{128,64},{192,128},{1,193},{65,1},{129,65},{193,129... | collective-permute-start | bytes 786440 | tf_op jit(solution)/shard_map/ppermute | solution.py:300
  62.5 7.4 %collective-permute-start.10 = (bf16[512,128]{1,0:T(8,128)(2,1)S(1)}, bf16[512,128]{1,0:T(8,128)(2,1)S(1)}, u32[]{:S(2)}, u32[]{:S(2)}) collective-permute-start(bf16[512,128]{1,0:T(8,128)(2,1)S(1)} %conv_back.5), channel_id=1, source_target_pairs={{2,1},{6,5},{10,9},{14,13},{18,17},{22,21},{26,25},{30,29},{34,33}... | collective-permute-start | bytes 393224 | tf_op jit(solution)/shard_map/ppermute | solution.py:370
  63.2 6.7 %collective-permute-start.11 = (bf16[512,128]{1,0:T(8,128)(2,1)S(1)}, bf16[512,128]{1,0:T(8,128)(2,1)S(1)}, u32[]{:S(2)}, u32[]{:S(2)}) collective-permute-start(bf16[512,128]{1,0:T(8,128)(2,1)S(1)} %conv_back.5), channel_id=1, source_target_pairs={{2,5},{6,1},{10,13},{14,9},{18,21},{22,17},{26,29},{30,25},{34,37}... | collective-permute-start | bytes 393224 | tf_op jit(solution)/shard_map/ppermute | solution.py:371
  67.7 33.2 %collective-permute-start.18 = (bf16[256,256]{1,0:T(8,128)(2,1)S(1)}, bf16[256,256]{1,0:T(8,128)(2,1)S(1)}, u32[]{:S(2)}, u32[]{:S(2)}) collective-permute-start(bf16[256,256]{1,0:T(8,128)(2,1)S(1)} %bitcast.71), channel_id=1, source_target_pairs={{0,64},{64,128},{128,192},{192,0},{1,65},{65,129},{129,193},{193,1... | collective-permute-start | bytes 393224 | tf_op jit(solution)/shard_map/ppermute | solution.py:303
  68.4 32.5 %collective-permute-start.20 = (bf16[256,256]{1,0:T(8,128)(2,1)S(1)}, bf16[256,256]{1,0:T(8,128)(2,1)S(1)}, u32[]{:S(2)}, u32[]{:S(2)}) collective-permute-start(bf16[256,256]{1,0:T(8,128)(2,1)S(1)} %bitcast.72), channel_id=1, source_target_pairs={{0,192},{64,0},{128,64},{192,128},{1,193},{65,1},{129,65},{193,129... | collective-permute-start | bytes 393224 | tf_op jit(solution)/shard_map/ppermute | solution.py:304
  70.5 16.1 %copy-start.9 = (bf16[4,2,64,256]{3,2,1,0:T(8,128)(2,1)S(1)}, bf16[4,2,64,256]{3,2,1,0:T(8,128)(2,1)}, u32[]{:S(2)}) copy-start(bf16[4,2,64,256]{3,2,1,0:T(8,128)(2,1)} %copy-done.8) | copy-start | bytes 786436
  70.5 11.9 %collective-permute-start.12 = (bf16[512,128]{1,0:T(8,128)(2,1)S(1)}, bf16[512,128]{1,0:T(8,128)(2,1)S(1)}, u32[]{:S(2)}, u32[]{:S(2)}) collective-permute-start(bf16[512,128]{1,0:T(8,128)(2,1)S(1)} %conv_back.6), channel_id=1, source_target_pairs={{1,0},{5,4},{9,8},{13,12},{17,16},{21,20},{25,24},{29,28},{33,32},... | collective-permute-start | bytes 393224 | tf_op jit(solution)/shard_map/ppermute | solution.py:370
  72.0 14.7 %collective-permute-start.13 = (bf16[512,128]{1,0:T(8,128)(2,1)S(1)}, bf16[512,128]{1,0:T(8,128)(2,1)S(1)}, u32[]{:S(2)}, u32[]{:S(2)}) collective-permute-start(bf16[512,128]{1,0:T(8,128)(2,1)S(1)} %conv_back.6), channel_id=1, source_target_pairs={{1,4},{5,0},{9,12},{13,8},{17,20},{21,16},{25,28},{29,24},{33,36},... | collective-permute-start | bytes 393224 | tf_op jit(solution)/shard_map/ppermute | solution.py:371
  86.8 6.6 %collective-permute-start.14 = (bf16[512,256]{1,0:T(8,128)(2,1)S(1)}, bf16[512,256]{1,0:T(8,128)(2,1)S(1)}, u32[]{:S(2)}, u32[]{:S(2)}) collective-permute-start(bf16[512,256]{1,0:T(8,128)(2,1)S(1)} %maximum_select_fusion.refs_4_), channel_id=1, source_target_pairs={{0,64},{64,128},{128,192},{192,0},{1,65},{65,129},{129,193},{193,1... | collective-permute-start | bytes 786440 | tf_op jit(solution)/shard_map/ppermute | solution.py:299
  87.2 7.6 %collective-permute-start.15 = (bf16[512,256]{1,0:T(8,128)(2,1)S(1)}, bf16[512,256]{1,0:T(8,128)(2,1)S(1)}, u32[]{:S(2)}, u32[]{:S(2)}) collective-permute-start(bf16[512,256]{1,0:T(8,128)(2,1)S(1)} %maximum_select_fusion.refs_4_), channel_id=1, source_target_pairs={{0,192},{64,0},{128,64},{192,128},{1,193},{65,1},{129,65},{193,129... | collective-permute-start | bytes 786440 | tf_op jit(solution)/shard_map/ppermute | solution.py:300
  92.3 4.9 %copy-start.2 = (bf16[9,256,256]{2,1,0:T(8,128)(2,1)S(1)}, bf16[9,256,256]{2,1,0:T(8,128)(2,1)}, u32[]{:S(2)}) copy-start(bf16[9,256,256]{2,1,0:T(8,128)(2,1)} %constant.52.clone.refs_7_.refs_5_) | copy-start | bytes 3538948
  92.4 4.9 %copy-start.3 = (bf16[4,2,64,256]{3,2,1,0:T(8,128)(2,1)S(1)}, bf16[4,2,64,256]{3,2,1,0:T(8,128)(2,1)}, u32[]{:S(2)}) copy-start(bf16[4,2,64,256]{3,2,1,0:T(8,128)(2,1)} %pad_maximum_fusion.1) | copy-start | bytes 786436
  94.8 6.2 %collective-permute-start.21 = (bf16[256,256]{1,0:T(8,128)(2,1)S(1)}, bf16[256,256]{1,0:T(8,128)(2,1)S(1)}, u32[]{:S(2)}, u32[]{:S(2)}) collective-permute-start(bf16[256,256]{1,0:T(8,128)(2,1)S(1)} %bitcast.73), channel_id=1, source_target_pairs={{0,64},{64,128},{128,192},{192,0},{1,65},{65,129},{129,193},{193,1... | collective-permute-start | bytes 393224 | tf_op jit(solution)/shard_map/ppermute | solution.py:303
  95.1 6.5 %collective-permute-start.22 = (bf16[256,256]{1,0:T(8,128)(2,1)S(1)}, bf16[256,256]{1,0:T(8,128)(2,1)S(1)}, u32[]{:S(2)}, u32[]{:S(2)}) collective-permute-start(bf16[256,256]{1,0:T(8,128)(2,1)S(1)} %bitcast.74), channel_id=1, source_target_pairs={{0,192},{64,0},{128,64},{192,128},{1,193},{65,1},{129,65},{193,129... | collective-permute-start | bytes 393224 | tf_op jit(solution)/shard_map/ppermute | solution.py:304
  104.5 16.0 %all-to-all-start.1 = ((bf16[8,108,256]{2,1,0:T(8,128)(2,1)}), bf16[8,108,256]{2,1,0:T(8,128)(2,1)S(1)}, u32[]{:S(2)}, u32[]{:S(2)}) async-start(bf16[8,108,256]{2,1,0:T(8,128)(2,1)} %weight_last.1), calls=%async_computation.1 | async-start | bytes 917504 | tf_op jit(solution)/shard_map/all_to_all | solution.py:385
  108.0 5.9 %collective-permute-start.16 = (bf16[4,2,32,128]{3,2,1,0:T(8,128)(2,1)S(1)}, bf16[4,2,32,128]{3,2,1,0:T(8,128)(2,1)S(1)}, u32[]{:S(2)}, u32[]{:S(2)}) collective-permute-start(bf16[4,2,32,128]{3,2,1,0:T(8,128)(2,1)S(1)} %get-tuple-element.26), channel_id=1, source_target_pairs={{0,4},{4,0},{1,5},{5,1},{2,6},{6,2},{3,7},{7,3},{8,12},{12,8},{9,1... | collective-permute-start | bytes 196616 | tf_op jit(solution)/shard_map/ppermute | solution.py:380
  (4 other events, 2.9 us)

commit v5 on v4

--- a/solution.py
+++ b/solution.py
@@ -137,8 +137,8 @@
 
 
 def conv_body(
-    flags, same, cross, s_ref, own, left, right, far_a, far_b, fac_ref,
-    out_ref, kbuf, fac, gs, krows, sem,
+    flags, cross, same, s_ref, own, left, right, far_a, far_b, fac,
+    out_ref, kbuf, gs, krows,
 ):
     x = flags[0]
     yh = flags[1]
@@ -150,13 +150,8 @@
         (far_a, lax.rem(x + 2, NX) * SLOTS, SLOTS // 2),
         (far_b, lax.rem(x + 2, NX) * SLOTS + SLOTS // 2, SLOTS // 2),
     )
-    later = [
-        pltpu.make_async_copy(ref, kbuf.at[pl.ds(pl.multiple_of(at, HC), size), :], sem.at[i])
-        for i, (ref, at, size) in enumerate(pieces)
-    ]
-    last = pltpu.make_async_copy(fac_ref, fac, sem.at[5])
-    for copy in later + [last]:
-        copy.start()
+    for ref, at, size in pieces:
+        kbuf[pl.ds(pl.multiple_of(at, HC), size), :] = ref[...]
     kept, got = same[...], cross[...]
     g = jnp.concatenate([jnp.where(yh == 0, kept, got), jnp.where(yh == 0, got, kept)], axis=1)
     for j in range(9):
@@ -164,8 +159,6 @@
             gs[pl.ds(r * HC, HC), pl.ds(j * C, C)] = jnp.dot(
                 s_ref[j], g[r * HC : (r + 1) * HC], preferred_element_type=F32
             ).astype(BF)
-    for copy in later:
-        copy.wait()
     slot = lax.broadcasted_iota(jnp.int32, (HC, C), 0)
     for kt in range(3):
         for j in range(9):
@@ -186,7 +179,6 @@
         ahead = (2 - kt) * frame
         part = product[ahead:, kt * HC : (kt + 1) * HC]
         grad_act = grad_act + jnp.concatenate([part, jnp.zeros((ahead, HC), F32)], axis=0)
-    last.wait()
     xhat = fac[0]
     grad_hat = grad_act * fac[1]
     sums = jnp.concatenate(
@@ -203,14 +195,12 @@
     return pl.pallas_call(
         functools.partial(conv_kernel, target),
         out_shape=jax.ShapeDtypeStruct((rows, HC), BF),
-        in_specs=[SMEM] + [VMEM] * 3 + [HBM] * 6,
+        in_specs=[SMEM] + [VMEM] * 9,
         out_specs=VMEM,
         scratch_shapes=[
             pltpu.VMEM((NX * SLOTS, C), BF),
-            pltpu.VMEM((3, rows, HC), F32),
             pltpu.VMEM((rows, 9 * C), BF),
             pltpu.VMEM((3 * HC, 9 * C), BF),
-            pltpu.SemaphoreType.DMA((6,)),
         ],
         compiler_params=pltpu.CompilerParams(vmem_limit_bytes=GRANT),
         cost_estimate=pl.CostEstimate(flops=2 * POS * ROWS * C, bytes_accessed=ROWS * C, transcendentals=0),
@@ -223,6 +213,8 @@
         refs[0], refs[1 : 1 + count], refs[1 + count : 1 + 2 * count], refs[1 + 2 * count : -4 - count]
     )
     held, (turned, at, gbuf, sem) = refs[-4 - count : -4], refs[-4:]
+    if tail:
+        held, acts = acts, ()
     yh = flags[1]
     copies = [pltpu.make_async_copy(src, dst, sem.at[i]) for i, (src, dst) in enumerate(zip(acts, held))]
     for copy in copies:
@@ -273,7 +265,7 @@
     return pl.pallas_call(
         functools.partial(weight_kernel, len(acts), tail),
         out_shape=jax.ShapeDtypeStruct((NZ, PART if tail else HC, C), BF if tail else F32),
-        in_specs=[SMEM] + [HBM] * len(acts) + [VMEM] * len(grads) + [VMEM] * (1 + tail),
+        in_specs=[SMEM] + [VMEM if tail else HBM] * len(acts) + [VMEM] * len(grads) + [VMEM] * (1 + tail),
         out_specs=VMEM,
         scratch_shapes=[pltpu.VMEM(v.shape, BF) for v in acts]
         + [
@@ -335,10 +327,11 @@
     channel = lax.rem(dp * PART + lax.broadcasted_iota(jnp.int32, (C, PART), 1), C)
     place = (channel == lax.broadcasted_iota(jnp.int32, (C, PART), 0)).astype(BF)
     slots = jnp.dot(place, conv_weight[0], preferred_element_type=F32).astype(BF)
-    window = mine(slots, 0) + lax.ppermute(theirs(slots, 0), "yh", swap)
+    other = lax.ppermute(theirs(slots, 0), "yh", swap)
     x_in = section_inputs.reshape(POS, C)
     act = forward(x_in, norm_gain, norm_shift)
-    window, act = lax.optimization_barrier((window, act))
+    other, act = lax.optimization_barrier((other, act))
+    window = mine(slots, 0) + other
     chunk = lax.all_to_all(
         jnp.broadcast_to(window[None], (NZ, HC, C)), "z", 0, 0, tiled=True
     ).reshape(SLOTS, C)
@@ -359,8 +352,10 @@
     pair_dx = None
     for k in range(4):
         if k > 0:
-            pair_g = jnp.where(section == 3 - k, in_order(*arrived, 1), pair_g)
-        sent = conv_back(3 - k, flags, arrived, s, kernel_rows, fac)
+            same, cross = arrived
+            both = [jnp.where(yh == 1, cross, same), jnp.where(yh == 1, same, cross)]
+            pair_g = jnp.where(section == 3 - k, jnp.concatenate(both, axis=1), pair_g)
+        sent = conv_back(3 - k, flags, arrived[::-1], s, kernel_rows, fac)
         if k == 0:
             sent, act = lax.optimization_barrier((sent, act))
             acts = gather_x(act, *clips_of_pair())
@@ -382,8 +377,8 @@
 
     partial = weight_back(flags, acts[:3], grads[:3], wide_s)
     partial = weight_back(flags, acts[3:], grads[3:], wide_s, partial)
-    weight_part = jnp.sum(lax.all_to_all(partial, "z", 0, 0, tiled=True).astype(F32), axis=0)
-    return dx, weight_part[None]
+    parts = lax.all_to_all(partial, "z", 0, 0, tiled=True).reshape(NZ, 1, PART, C)
+    return dx, jnp.sum(parts.astype(F32), axis=0)
 
 
 def solution(mesh):

time: 122 us -> 118 us (0.967)
  waiting for transfers between devices: 54.7 us -> 52.1 us
    ppermute x3, waiting for transfers between devices: 9.09 us -> 0.01 us  [local(): same = lax.ppermute(sent, ('yl', 'c'), [(src, dst)])]
    ppermute x3, waiting for transfers between devices: 4.24 us -> 9.98 us  [local(): lax.ppermute(sent, ('yh', 'yl', 'c'), [(y * N_PIPE + src, (1 - y) * N_PIP...]
  transfers between devices with their start and end apart: 25 -> 25, of which waited for: 14 -> 14; matrix products, arithmetic and copies ran while one was open for 3% -> 3% of each run, Pallas kernels for 9% -> 8%
where the time goes in v5:
time: 118 us; the launch traced here: 117 us
  waiting for transfers between devices  52.1 us (44%)
  starting transfers between devices  41.7 us (35%)
  Pallas kernels  13.7 us (12%)
  local copies, waits for them, and re-layouts  6.3 us (5%)
  other arithmetic  2.34 us (2%)
    ppermute x3, waiting for transfers between devices, gather_x(): left = lax.ppermute(block, 'x', ring('x', 1))  13.5 us
    ppermute x3, waiting for transfers between devices, local(): lax.ppermute(sent, ('yh', 'yl', 'c'), [(y * N_PIPE + src, (1 - y) * N_PIP...  9.98 us
    all_to_all x1, starting transfers between devices, local(): lax.all_to_all(jnp.broadcast_to(window[None], (NZ, HC, C)), 'z', 0, 0, ti...  8.47 us
    all_to_all x1, waiting for transfers between devices, local(): lax.all_to_all(jnp.broadcast_to(window[None], (NZ, HC, C)), 'z', 0, 0, ti...  7.15 us
    pallas_call x2, Pallas kernels, weight_back(): pl.pallas_call(functools.partial(weight_kernel, len(acts), tail), out_sha...  6.29 us
    all_to_all x1, waiting for transfers between devices, local(): lax.all_to_all(partial, 'z', 0, 0, tiled=True).reshape(NZ, 1, PART, C)  5.88 us
    pallas_call x4, Pallas kernels, conv_back(): pl.pallas_call(functools.partial(conv_kernel, target), out_shape=jax.Shap...  5.49 us
    ppermute x3, starting transfers between devices, gather_x(): far_b = lax.ppermute(second_half(right), 'x', ring('x', -1))  5.49 us
  transfers between devices with their start and end apart: 25, of which 14 were waited for; matrix products, arithmetic and copies ran while one was open for 3% of the time, Pallas kernels for 8%

profile of v5, /device:TPU:6, one launch (start us, length us, event | category | flops | bytes accessed | tf_op | source)
XLA Modules:
  0.0 117.4 jit_solution(527631574882343271)
XLA Ops:
  1.7 3.3 %collective-permute-start = (bf16[128,256]{1,0:T(8,128)(2,1)S(1)}, bf16[128,256]{1,0:T(8,128)(2,1)S(1)}, u32[]{:S(2)}, u32[]{:S(2)}) collective-permute-start(bf16[128,256]{1,0:T(8,128)(2,1)S(1)} %constant_dynamic-slice_fusion.6), channel_id=1, source_target_pairs={{0,4},{4,0},{1,5},{5,1},{2,6},{6,2},{3,7},{7,3},{8,12},{12,8},{9,1... | collective-permute-start | bytes 196616 | tf_op jit(solution)/shard_map/ppermute | solution.py:330
  8.9 8.5 %all-to-all-start = ((bf16[8,128,256]{2,1,0:T(8,128)(2,1)}), bf16[8,128,256]{2,1,0:T(8,128)(2,1)S(1)}, u32[]{:S(2)}, u32[]{:S(2)}) async-start(bf16[8,128,256]{2,1,0:T(8,128)(2,1)} %broadcast_in_dim.2), calls=%async_computation | async-start | bytes 1048576 | tf_op jit(solution)/shard_map/all_to_all | solution.py:335
  17.4 2.7 %collective-permute-start.4 = (bf16[256,128]{1,0:T(8,128)(2,1)S(1)}, bf16[256,128]{1,0:T(8,128)(2,1)S(1)}, u32[]{:S(2)}, u32[]{:S(2)}) collective-permute-start(bf16[256,128]{1,0:T(8,128)(2,1)S(1)} %get-tuple-element.48), channel_id=1, source_target_pairs={{0,4},{4,0},{1,5},{5,1},{2,6},{6,2},{3,7},{7,3},{8,12},{12,8},{9,1... | collective-permute-start | bytes 196616 | tf_op jit(solution)/shard_map/ppermute | solution.py:339
  20.2 1.0 collective-permute-start.3
  21.3 2.7 %collective-permute-start.5 = (bf16[4,1,64,256]{3,2,1,0:T(8,128)(2,1)S(1)}, bf16[4,1,64,256]{3,2,1,0:T(8,128)(2,1)S(1)}, u32[]{:S(2)}, u32[]{:S(2)}) collective-permute-start(bf16[4,1,64,256]{3,2,1,0:T(8,128)(2,1)S(1)} %bitcast.57), channel_id=1, source_target_pairs={{0,4},{4,0},{1,5},{5,1},{2,6},{6,2},{3,7},{7,3},{8,12},{12,8},{9,1... | collective-permute-start | bytes 393224 | tf_op jit(solution)/shard_map/ppermute | solution.py:347
  24.0 1.2 %norm_factors.1.refs_8_ = f32[3,512,128]{2,1,0:T(8,128)S(1)} custom-call(s32[3]{0:T(128)S(1)} %pad_add_fusion.flags.refs_0_, bf16[256,128]{1,0:T(8,128)(2,1)S(1)} %get-tuple-element.49.mine, bf16[256,128]{1,0:T(8,128)(2,1)S(1)} %collective-permute-done.4.theirs, f32[1,128]{1,0:T(1,128)S(1)} %get-tuple-element.53.gain_ref, ...), custom_call_target="tpu_custom_call" | custom-call | tf_op jit(solution)/shard_map/norm_factors/pallas_call | solution.py:122
  25.1 2.3 %collective-permute-done.3 = bf16[4,1,64,256]{3,2,1,0:T(8,128)(2,1)S(1)} collective-permute-done((bf16[4,1,64,256]{3,2,1,0:T(8,128)(2,1)S(1)}, bf16[4,1,64,256]{3,2,1,0:T(8,128)(2,1)S(1)}, u32[]{:S(2)}, u32[]{:S(2)}) %collective-permute-start.3) | collective-permute-done | bytes 131104 | tf_op jit(solution)/shard_map/ppermute | solution.py:344
  27.5 7.1 %all-to-all-done = bf16[8,128,256]{2,1,0:T(8,128)(2,1)S(1)} async-done(((bf16[8,128,256]{2,1,0:T(8,128)(2,1)}), bf16[8,128,256]{2,1,0:T(8,128)(2,1)S(1)}, u32[]{:S(2)}, u32[]{:S(2)}) %all-to-all-start) | async-done | bytes 524320 | tf_op jit(solution)/shard_map/all_to_all | solution.py:335
  35.1 1.5 %collective-permute-start.2 = (bf16[1024,256]{1,0:T(8,128)(2,1)S(1)}, bf16[1024,256]{1,0:T(8,128)(2,1)S(1)}, u32[]{:S(2)}, u32[]{:S(2)}) collective-permute-start(bf16[1024,256]{1,0:T(8,128)(2,1)S(1)} %bitcast.52), channel_id=1, source_target_pairs={{0,192},{64,0},{128,64},{192,128},{1,193},{65,1},{129,65},{193,129... | collective-permute-start | bytes 1572872 | tf_op jit(solution)/shard_map/ppermute | solution.py:292
  38.2 9.3 %collective-permute-done.1.refs_4_ = bf16[1024,256]{1,0:T(8,128)(2,1)S(1)} collective-permute-done((bf16[1024,256]{1,0:T(8,128)(2,1)S(1)}, bf16[1024,256]{1,0:T(8,128)(2,1)S(1)}, u32[]{:S(2)}, u32[]{:S(2)}) %collective-permute-start.1) | collective-permute-done | bytes 524320 | tf_op jit(solution)/shard_map/ppermute | solution.py:291
  47.5 1.4 %collective-permute-done.2.refs_5_ = bf16[1024,256]{1,0:T(8,128)(2,1)S(1)} collective-permute-done((bf16[1024,256]{1,0:T(8,128)(2,1)S(1)}, bf16[1024,256]{1,0:T(8,128)(2,1)S(1)}, u32[]{:S(2)}, u32[]{:S(2)}) %collective-permute-start.2) | collective-permute-done | bytes 524320 | tf_op jit(solution)/shard_map/ppermute | solution.py:292
  49.3 1.8 %collective-permute-start.7 = (bf16[512,256]{1,0:T(8,128)(2,1)S(1)}, bf16[512,256]{1,0:T(8,128)(2,1)S(1)}, u32[]{:S(2)}, u32[]{:S(2)}) collective-permute-start(bf16[512,256]{1,0:T(8,128)(2,1)S(1)} %slice.19), channel_id=1, source_target_pairs={{0,192},{64,0},{128,64},{192,128},{1,193},{65,1},{129,65},{193,129... | collective-permute-start | bytes 786440 | tf_op jit(solution)/shard_map/ppermute | solution.py:296
  51.2 4.2 %collective-permute-done.6.refs_6_ = bf16[512,256]{1,0:T(8,128)(2,1)S(1)} collective-permute-done((bf16[512,256]{1,0:T(8,128)(2,1)S(1)}, bf16[512,256]{1,0:T(8,128)(2,1)S(1)}, u32[]{:S(2)}, u32[]{:S(2)}) %collective-permute-start.6) | collective-permute-done | bytes 262176 | tf_op jit(solution)/shard_map/ppermute | solution.py:295
  55.4 1.6 %collective-permute-done.7.refs_7_ = bf16[512,256]{1,0:T(8,128)(2,1)S(1)} collective-permute-done((bf16[512,256]{1,0:T(8,128)(2,1)S(1)}, bf16[512,256]{1,0:T(8,128)(2,1)S(1)}, u32[]{:S(2)}, u32[]{:S(2)}) %collective-permute-start.7) | collective-permute-done | bytes 262176 | tf_op jit(solution)/shard_map/ppermute | solution.py:296
  57.0 1.2 %conv_back.4 = bf16[512,128]{1,0:T(8,128)(2,1)} custom-call(s32[3]{0:T(128)S(1)} %pad_add_fusion.flags.refs_0_, bf16[512,128]{1,0:T(8,128)(2,1)S(1)} %get-tuple-element.18.refs_0_, bf16[512,128]{1,0:T(8,128)(2,1)S(1)} %get-tuple-element.19.refs_1_, bf16[9,128,128]{2,1,0:T(8,128)(2,1)S(1)} %copy-done.1, bf16[1024,256]{1,0:T(8,128)(2,1)S(1)} %bitcast.53, ...), custom_call_target="tpu_custom_call" | custom-call | flops 905969664 | bytes 1769472 | tf_op jit(solution)/shard_map/conv_back/pallas_call | solution.py:195
  59.9 1.7 %collective-permute-start.19 = (bf16[512,256]{1,0:T(8,128)(2,1)}, bf16[512,256]{1,0:T(8,128)(2,1)S(1)}, u32[]{:S(2)}, u32[]{:S(2)}) collective-permute-start(bf16[512,256]{1,0:T(8,128)(2,1)} %bitcast.60), channel_id=1, source_target_pairs={{0,192},{64,0},{128,64},{192,128},{1,193},{65,1},{129,65},{193,129... | collective-permute-start | bytes 786440 | tf_op jit(solution)/shard_map/ppermute | solution.py:292
  63.8 3.8 %collective-permute-done.17.refs_2_ = bf16[512,256]{1,0:T(8,128)(2,1)S(1)} collective-permute-done((bf16[512,256]{1,0:T(8,128)(2,1)}, bf16[512,256]{1,0:T(8,128)(2,1)S(1)}, u32[]{:S(2)}, u32[]{:S(2)}) %collective-permute-start.17) | collective-permute-done | bytes 262176 | tf_op jit(solution)/shard_map/ppermute | solution.py:291
  68.3 1.5 %collective-permute-start.20 = (bf16[256,256]{1,0:T(8,128)(2,1)S(1)}, bf16[256,256]{1,0:T(8,128)(2,1)S(1)}, u32[]{:S(2)}, u32[]{:S(2)}) collective-permute-start(bf16[256,256]{1,0:T(8,128)(2,1)S(1)} %bitcast.72), channel_id=1, source_target_pairs={{0,192},{64,0},{128,64},{192,128},{1,193},{65,1},{129,65},{193,129... | collective-permute-start | bytes 393224 | tf_op jit(solution)/shard_map/ppermute | solution.py:296
  70.4 1.4 %collective-permute-start.12 = (bf16[512,128]{1,0:T(8,128)(2,1)S(1)}, bf16[512,128]{1,0:T(8,128)(2,1)S(1)}, u32[]{:S(2)}, u32[]{:S(2)}) collective-permute-start(bf16[512,128]{1,0:T(8,128)(2,1)S(1)} %conv_back.6), channel_id=1, source_target_pairs={{1,4},{5,0},{9,12},{13,8},{17,20},{21,16},{25,28},{29,24},{33,36},... | collective-permute-start | bytes 393224 | tf_op jit(solution)/shard_map/ppermute | solution.py:366
  71.9 1.3 %collective-permute-start.13 = (bf16[512,128]{1,0:T(8,128)(2,1)S(1)}, bf16[512,128]{1,0:T(8,128)(2,1)S(1)}, u32[]{:S(2)}, u32[]{:S(2)}) collective-permute-start(bf16[512,128]{1,0:T(8,128)(2,1)S(1)} %conv_back.6), channel_id=1, source_target_pairs={{1,0},{5,4},{9,8},{13,12},{17,16},{21,20},{25,24},{29,28},{33,32},... | collective-permute-start | bytes 393224 | tf_op jit(solution)/shard_map/ppermute | solution.py:365
  73.2 10.0 %collective-permute-done.12.refs_0_ = bf16[512,128]{1,0:T(8,128)(2,1)S(1)} collective-permute-done((bf16[512,128]{1,0:T(8,128)(2,1)S(1)}, bf16[512,128]{1,0:T(8,128)(2,1)S(1)}, u32[]{:S(2)}, u32[]{:S(2)}) %collective-permute-start.12) | collective-permute-done | bytes 131104 | tf_op jit(solution)/shard_map/ppermute | solution.py:366
  83.7 1.8 %collective-permute-start.15 = (bf16[512,256]{1,0:T(8,128)(2,1)S(1)}, bf16[512,256]{1,0:T(8,128)(2,1)S(1)}, u32[]{:S(2)}, u32[]{:S(2)}) collective-permute-start(bf16[512,256]{1,0:T(8,128)(2,1)S(1)} %maximum_select_fusion.refs_4_), channel_id=1, source_target_pairs={{0,192},{64,0},{128,64},{192,128},{1,193},{65,1},{129,65},{193,129... | collective-permute-start | bytes 786440 | tf_op jit(solution)/shard_map/ppermute | solution.py:292
  85.5 3.0 %conv_back.7 = bf16[512,128]{1,0:T(8,128)(2,1)S(1)} custom-call(s32[3]{0:T(128)S(1)} %pad_add_fusion.flags.refs_0_, bf16[512,128]{1,0:T(8,128)(2,1)S(1)} %collective-permute-done.12.refs_0_, bf16[512,128]{1,0:T(8,128)(2,1)S(1)} %collective-permute-done.13.refs_1_, bf16[9,128,128]{2,1,0:T(8,128)(2,1)S(1)} %copy-done.1, bf16[1024,256]{1,0:T(8,128)(2,1)S(1)} %bitcast.56, ...), custom_call_target="tpu_custom_call" | custom-call | flops 905969664 | bytes 1769472 | tf_op jit(solution)/shard_map/conv_back/pallas_call | solution.py:195
  88.5 1.1 select_select_fusion
  90.0 1.3 %collective-permute-done.15.refs_6_ = bf16[512,256]{1,0:T(8,128)(2,1)S(1)} collective-permute-done((bf16[512,256]{1,0:T(8,128)(2,1)S(1)}, bf16[512,256]{1,0:T(8,128)(2,1)S(1)}, u32[]{:S(2)}, u32[]{:S(2)}) %collective-permute-start.15) | collective-permute-done | bytes 262176 | tf_op jit(solution)/shard_map/ppermute | solution.py:292
  91.6 2.2 %collective-permute-start.22 = (bf16[256,256]{1,0:T(8,128)(2,1)S(1)}, bf16[256,256]{1,0:T(8,128)(2,1)S(1)}, u32[]{:S(2)}, u32[]{:S(2)}) collective-permute-start(bf16[256,256]{1,0:T(8,128)(2,1)S(1)} %bitcast.74), channel_id=1, source_target_pairs={{0,192},{64,0},{128,64},{192,128},{1,193},{65,1},{129,65},{193,129... | collective-permute-start | bytes 393224 | tf_op jit(solution)/shard_map/ppermute | solution.py:296
  93.7 3.7 %weight_first.1.refs_6_ = f32[8,128,256]{2,1,0:T(8,128)S(1)} custom-call(s32[3]{0:T(128)S(1)} %pad_add_fusion.flags.refs_0_, bf16[512,256]{1,0:T(8,128)(2,1)S(1)} %bitcast.61, bf16[512,256]{1,0:T(8,128)(2,1)S(1)} %collective-permute-done.17.refs_2_, bf16[512,256]{1,0:T(8,128)(2,1)S(1)} %collective-permute-done.19.refs_3_, ...), custom_call_target="tpu_custom_call" | custom-call | flops 1358954496 | bytes 4194304 | tf_op jit(solution)/shard_map/weight_first/pallas_call | solution.py:265
  98.0 2.6 %weight_last.1 = bf16[8,108,256]{2,1,0:T(8,128)(2,1)} custom-call(s32[3]{0:T(128)S(1)} %pad_add_fusion.flags.refs_0_, bf16[256,256]{1,0:T(8,128)(2,1)S(1)} %collective-permute-done.18.refs_1_, bf16[256,256]{1,0:T(8,128)(2,1)S(1)} %collective-permute-done.20.refs_2_, bf16[256,256]{1,0:T(8,128)(2,1)S(1)} %collective-permute-done.21.refs_3_, ...), custom_call_target="tpu_custom_call" | custom-call | flops 452984832 | bytes 4194304 | tf_op jit(solution)/shard_map/weight_last/pallas_call | solution.py:265
  100.6 3.5 %all-to-all-start.1 = ((bf16[8,108,256]{2,1,0:T(8,128)(2,1)}), bf16[8,108,256]{2,1,0:T(8,128)(2,1)S(1)}, u32[]{:S(2)}, u32[]{:S(2)}) async-start(bf16[8,108,256]{2,1,0:T(8,128)(2,1)} %weight_last.1), calls=%async_computation.1 | async-start | bytes 917504 | tf_op jit(solution)/shard_map/all_to_all | solution.py:380
  104.1 1.8 %collective-permute-start.16 = (bf16[4,2,32,128]{3,2,1,0:T(8,128)(2,1)S(1)}, bf16[4,2,32,128]{3,2,1,0:T(8,128)(2,1)S(1)}, u32[]{:S(2)}, u32[]{:S(2)}) collective-permute-start(bf16[4,2,32,128]{3,2,1,0:T(8,128)(2,1)S(1)} %get-tuple-element.26), channel_id=1, source_target_pairs={{0,4},{4,0},{1,5},{5,1},{2,6},{6,2},{3,7},{7,3},{8,12},{12,8},{9,1... | collective-permute-start | bytes 196616 | tf_op jit(solution)/shard_map/ppermute | solution.py:375
  105.9 4.0 %collective-permute-done.16 = bf16[4,2,32,128]{3,2,1,0:T(8,128)(2,1)S(1)} collective-permute-done((bf16[4,2,32,128]{3,2,1,0:T(8,128)(2,1)S(1)}, bf16[4,2,32,128]{3,2,1,0:T(8,128)(2,1)S(1)}, u32[]{:S(2)}, u32[]{:S(2)}) %collective-permute-start.16) | collective-permute-done | bytes 65568 | tf_op jit(solution)/shard_map/ppermute | solution.py:375
  110.7 5.9 %all-to-all-done.1 = bf16[8,108,256]{2,1,0:T(8,128)(2,1)S(1)} async-done(((bf16[8,108,256]{2,1,0:T(8,128)(2,1)}), bf16[8,108,256]{2,1,0:T(8,128)(2,1)S(1)}, u32[]{:S(2)}, u32[]{:S(2)}) %all-to-all-start.1) | async-done | bytes 442400 | tf_op jit(solution)/shard_map/all_to_all | solution.py:380
  (83 shorter events, 15.9 us)
Async XLA Ops:
  1.7 6.4 %collective-permute-start = (bf16[128,256]{1,0:T(8,128)(2,1)S(1)}, bf16[128,256]{1,0:T(8,128)(2,1)S(1)}, u32[]{:S(2)}, u32[]{:S(2)}) collective-permute-start(bf16[128,256]{1,0:T(8,128)(2,1)S(1)} %constant_dynamic-slice_fusion.6), channel_id=1, source_target_pairs={{0,4},{4,0},{1,5},{5,1},{2,6},{6,2},{3,7},{7,3},{8,12},{12,8},{9,1... | collective-permute-start | bytes 196616 | tf_op jit(solution)/shard_map/ppermute | solution.py:330
  7.2 12.9 %copy-start.10 = (bf16[1,2,4,8,4,256]{5,4,3,2,1,0:T(4,128)(2,1)S(1)}, bf16[1,2,4,8,4,256]{5,4,3,2,1,0:T(4,128)(2,1)}, u32[]{:S(2)}) copy-start(bf16[1,2,4,8,4,256]{5,4,3,2,1,0:T(4,128)(2,1)} %param.8) | copy-start | bytes 393220
  8.1 13.1 %copy-start.5 = (f32[1,256]{1,0:T(1,128)S(1)}, f32[1,256]{1,0:T(1,128)}, u32[]{:S(2)}) copy-start(f32[1,256]{1,0:T(1,128)} %shift_ref.1) | copy-start | bytes 3076
  8.1 13.1 %copy-start.7 = (f32[1,256]{1,0:T(1,128)S(1)}, f32[1,256]{1,0:T(1,128)}, u32[]{:S(2)}) copy-start(f32[1,256]{1,0:T(1,128)} %gain_ref.1) | copy-start | bytes 3076
  8.9 25.7 %all-to-all-start = ((bf16[8,128,256]{2,1,0:T(8,128)(2,1)}), bf16[8,128,256]{2,1,0:T(8,128)(2,1)S(1)}, u32[]{:S(2)}, u32[]{:S(2)}) async-start(bf16[8,128,256]{2,1,0:T(8,128)(2,1)} %broadcast_in_dim.2), calls=%async_computation | async-start | bytes 1048576 | tf_op jit(solution)/shard_map/all_to_all | solution.py:335
  17.4 6.6 %collective-permute-start.4 = (bf16[256,128]{1,0:T(8,128)(2,1)S(1)}, bf16[256,128]{1,0:T(8,128)(2,1)S(1)}, u32[]{:S(2)}, u32[]{:S(2)}) collective-permute-start(bf16[256,128]{1,0:T(8,128)(2,1)S(1)} %get-tuple-element.48), channel_id=1, source_target_pairs={{0,4},{4,0},{1,5},{5,1},{2,6},{6,2},{3,7},{7,3},{8,12},{12,8},{9,1... | collective-permute-start | bytes 196616 | tf_op jit(solution)/shard_map/ppermute | solution.py:339
  20.2 7.2 %collective-permute-start.3 = (bf16[4,1,64,256]{3,2,1,0:T(8,128)(2,1)S(1)}, bf16[4,1,64,256]{3,2,1,0:T(8,128)(2,1)S(1)}, u32[]{:S(2)}, u32[]{:S(2)}) collective-permute-start(bf16[4,1,64,256]{3,2,1,0:T(8,128)(2,1)S(1)} %bitcast.67), channel_id=1, source_target_pairs={{0,4},{4,0},{1,5},{5,1},{2,6},{6,2},{3,7},{7,3},{8,12},{12,8},{9,1... | collective-permute-start | bytes 393224 | tf_op jit(solution)/shard_map/ppermute | solution.py:344
  21.3 16.2 %collective-permute-start.5 = (bf16[4,1,64,256]{3,2,1,0:T(8,128)(2,1)S(1)}, bf16[4,1,64,256]{3,2,1,0:T(8,128)(2,1)S(1)}, u32[]{:S(2)}, u32[]{:S(2)}) collective-permute-start(bf16[4,1,64,256]{3,2,1,0:T(8,128)(2,1)S(1)} %bitcast.57), channel_id=1, source_target_pairs={{0,4},{4,0},{1,5},{5,1},{2,6},{6,2},{3,7},{7,3},{8,12},{12,8},{9,1... | collective-permute-start | bytes 393224 | tf_op jit(solution)/shard_map/ppermute | solution.py:347
  34.6 12.9 %collective-permute-start.1 = (bf16[1024,256]{1,0:T(8,128)(2,1)S(1)}, bf16[1024,256]{1,0:T(8,128)(2,1)S(1)}, u32[]{:S(2)}, u32[]{:S(2)}) collective-permute-start(bf16[1024,256]{1,0:T(8,128)(2,1)S(1)} %bitcast.51), channel_id=1, source_target_pairs={{0,64},{64,128},{128,192},{192,0},{1,65},{65,129},{129,193},{193,1... | collective-permute-start | bytes 1572872 | tf_op jit(solution)/shard_map/ppermute | solution.py:291
  35.1 13.9 %collective-permute-start.2 = (bf16[1024,256]{1,0:T(8,128)(2,1)S(1)}, bf16[1024,256]{1,0:T(8,128)(2,1)S(1)}, u32[]{:S(2)}, u32[]{:S(2)}) collective-permute-start(bf16[1024,256]{1,0:T(8,128)(2,1)S(1)} %bitcast.52), channel_id=1, source_target_pairs={{0,192},{64,0},{128,64},{192,128},{1,193},{65,1},{129,65},{193,129... | collective-permute-start | bytes 1572872 | tf_op jit(solution)/shard_map/ppermute | solution.py:292
  37.4 19.6 %copy-start.1 = (bf16[9,128,128]{2,1,0:T(8,128)(2,1)S(1)}, bf16[9,128,128]{2,1,0:T(8,128)(2,1)}, u32[]{:S(2)}) copy-start(bf16[9,128,128]{2,1,0:T(8,128)(2,1)} %constant.51.clone.refs_2_) | copy-start | bytes 884740
  49.0 6.4 %collective-permute-start.6 = (bf16[512,256]{1,0:T(8,128)(2,1)S(1)}, bf16[512,256]{1,0:T(8,128)(2,1)S(1)}, u32[]{:S(2)}, u32[]{:S(2)}) collective-permute-start(bf16[512,256]{1,0:T(8,128)(2,1)S(1)} %slice.18), channel_id=1, source_target_pairs={{0,64},{64,128},{128,192},{192,0},{1,65},{65,129},{129,193},{193,1... | collective-permute-start | bytes 786440 | tf_op jit(solution)/shard_map/ppermute | solution.py:295
  49.3 7.7 %collective-permute-start.7 = (bf16[512,256]{1,0:T(8,128)(2,1)S(1)}, bf16[512,256]{1,0:T(8,128)(2,1)S(1)}, u32[]{:S(2)}, u32[]{:S(2)}) collective-permute-start(bf16[512,256]{1,0:T(8,128)(2,1)S(1)} %slice.19), channel_id=1, source_target_pairs={{0,192},{64,0},{128,64},{192,128},{1,193},{65,1},{129,65},{193,129... | collective-permute-start | bytes 786440 | tf_op jit(solution)/shard_map/ppermute | solution.py:296
  58.2 3.5 %collective-permute-start.8 = (bf16[512,128]{1,0:T(8,128)(2,1)}, bf16[512,128]{1,0:T(8,128)(2,1)S(1)}, u32[]{:S(2)}, u32[]{:S(2)}) collective-permute-start(bf16[512,128]{1,0:T(8,128)(2,1)} %conv_back.4), channel_id=1, source_target_pairs={{3,6},{7,2},{11,14},{15,10},{19,22},{23,18},{27,30},{31,26},{35,38... | collective-permute-start | bytes 393224 | tf_op jit(solution)/shard_map/ppermute | solution.py:366
  58.9 2.8 %collective-permute-start.9 = (bf16[512,128]{1,0:T(8,128)(2,1)}, bf16[512,128]{1,0:T(8,128)(2,1)S(1)}, u32[]{:S(2)}, u32[]{:S(2)}) collective-permute-start(bf16[512,128]{1,0:T(8,128)(2,1)} %conv_back.4), channel_id=1, source_target_pairs={{3,2},{7,6},{11,10},{15,14},{19,18},{23,22},{27,26},{31,30},{35,34... | collective-permute-start | bytes 393224 | tf_op jit(solution)/shard_map/ppermute | solution.py:365
  59.6 8.1 %collective-permute-start.17 = (bf16[512,256]{1,0:T(8,128)(2,1)}, bf16[512,256]{1,0:T(8,128)(2,1)S(1)}, u32[]{:S(2)}, u32[]{:S(2)}) collective-permute-start(bf16[512,256]{1,0:T(8,128)(2,1)} %bitcast.59), channel_id=1, source_target_pairs={{0,64},{64,128},{128,192},{192,0},{1,65},{65,129},{129,193},{193,1... | collective-permute-start | bytes 786440 | tf_op jit(solution)/shard_map/ppermute | solution.py:291
  59.9 8.4 %collective-permute-start.19 = (bf16[512,256]{1,0:T(8,128)(2,1)}, bf16[512,256]{1,0:T(8,128)(2,1)S(1)}, u32[]{:S(2)}, u32[]{:S(2)}) collective-permute-start(bf16[512,256]{1,0:T(8,128)(2,1)} %bitcast.60), channel_id=1, source_target_pairs={{0,192},{64,0},{128,64},{192,128},{1,193},{65,1},{129,65},{193,129... | collective-permute-start | bytes 786440 | tf_op jit(solution)/shard_map/ppermute | solution.py:292
  62.4 7.4 %collective-permute-start.10 = (bf16[512,128]{1,0:T(8,128)(2,1)S(1)}, bf16[512,128]{1,0:T(8,128)(2,1)S(1)}, u32[]{:S(2)}, u32[]{:S(2)}) collective-permute-start(bf16[512,128]{1,0:T(8,128)(2,1)S(1)} %conv_back.5), channel_id=1, source_target_pairs={{2,5},{6,1},{10,13},{14,9},{18,21},{22,17},{26,29},{30,25},{34,37}... | collective-permute-start | bytes 393224 | tf_op jit(solution)/shard_map/ppermute | solution.py:366
  63.1 6.8 %collective-permute-start.11 = (bf16[512,128]{1,0:T(8,128)(2,1)S(1)}, bf16[512,128]{1,0:T(8,128)(2,1)S(1)}, u32[]{:S(2)}, u32[]{:S(2)}) collective-permute-start(bf16[512,128]{1,0:T(8,128)(2,1)S(1)} %conv_back.5), channel_id=1, source_target_pairs={{2,1},{6,5},{10,9},{14,13},{18,17},{22,21},{26,25},{30,29},{34,33}... | collective-permute-start | bytes 393224 | tf_op jit(solution)/shard_map/ppermute | solution.py:365
  67.6 29.8 %collective-permute-start.18 = (bf16[256,256]{1,0:T(8,128)(2,1)S(1)}, bf16[256,256]{1,0:T(8,128)(2,1)S(1)}, u32[]{:S(2)}, u32[]{:S(2)}) collective-permute-start(bf16[256,256]{1,0:T(8,128)(2,1)S(1)} %bitcast.71), channel_id=1, source_target_pairs={{0,64},{64,128},{128,192},{192,0},{1,65},{65,129},{129,193},{193,1... | collective-permute-start | bytes 393224 | tf_op jit(solution)/shard_map/ppermute | solution.py:295
  68.3 29.1 %collective-permute-start.20 = (bf16[256,256]{1,0:T(8,128)(2,1)S(1)}, bf16[256,256]{1,0:T(8,128)(2,1)S(1)}, u32[]{:S(2)}, u32[]{:S(2)}) collective-permute-start(bf16[256,256]{1,0:T(8,128)(2,1)S(1)} %bitcast.72), channel_id=1, source_target_pairs={{0,192},{64,0},{128,64},{192,128},{1,193},{65,1},{129,65},{193,129... | collective-permute-start | bytes 393224 | tf_op jit(solution)/shard_map/ppermute | solution.py:296
  70.4 12.8 %copy-start.9 = (bf16[4,2,64,256]{3,2,1,0:T(8,128)(2,1)S(1)}, bf16[4,2,64,256]{3,2,1,0:T(8,128)(2,1)}, u32[]{:S(2)}) copy-start(bf16[4,2,64,256]{3,2,1,0:T(8,128)(2,1)} %copy-done.8) | copy-start | bytes 786436
  70.4 12.7 %collective-permute-start.12 = (bf16[512,128]{1,0:T(8,128)(2,1)S(1)}, bf16[512,128]{1,0:T(8,128)(2,1)S(1)}, u32[]{:S(2)}, u32[]{:S(2)}) collective-permute-start(bf16[512,128]{1,0:T(8,128)(2,1)S(1)} %conv_back.6), channel_id=1, source_target_pairs={{1,4},{5,0},{9,12},{13,8},{17,20},{21,16},{25,28},{29,24},{33,36},... | collective-permute-start | bytes 393224 | tf_op jit(solution)/shard_map/ppermute | solution.py:366
  71.9 11.3 %collective-permute-start.13 = (bf16[512,128]{1,0:T(8,128)(2,1)S(1)}, bf16[512,128]{1,0:T(8,128)(2,1)S(1)}, u32[]{:S(2)}, u32[]{:S(2)}) collective-permute-start(bf16[512,128]{1,0:T(8,128)(2,1)S(1)} %conv_back.6), channel_id=1, source_target_pairs={{1,0},{5,4},{9,8},{13,12},{17,16},{21,20},{25,24},{29,28},{33,32},... | collective-permute-start | bytes 393224 | tf_op jit(solution)/shard_map/ppermute | solution.py:365
  83.4 6.6 %collective-permute-start.14 = (bf16[512,256]{1,0:T(8,128)(2,1)S(1)}, bf16[512,256]{1,0:T(8,128)(2,1)S(1)}, u32[]{:S(2)}, u32[]{:S(2)}) collective-permute-start(bf16[512,256]{1,0:T(8,128)(2,1)S(1)} %maximum_select_fusion.refs_4_), channel_id=1, source_target_pairs={{0,64},{64,128},{128,192},{192,0},{1,65},{65,129},{129,193},{193,1... | collective-permute-start | bytes 786440 | tf_op jit(solution)/shard_map/ppermute | solution.py:291
  83.7 7.6 %collective-permute-start.15 = (bf16[512,256]{1,0:T(8,128)(2,1)S(1)}, bf16[512,256]{1,0:T(8,128)(2,1)S(1)}, u32[]{:S(2)}, u32[]{:S(2)}) collective-permute-start(bf16[512,256]{1,0:T(8,128)(2,1)S(1)} %maximum_select_fusion.refs_4_), channel_id=1, source_target_pairs={{0,192},{64,0},{128,64},{192,128},{1,193},{65,1},{129,65},{193,129... | collective-permute-start | bytes 786440 | tf_op jit(solution)/shard_map/ppermute | solution.py:292
  88.5 5.2 %copy-start.2 = (bf16[9,256,256]{2,1,0:T(8,128)(2,1)S(1)}, bf16[9,256,256]{2,1,0:T(8,128)(2,1)}, u32[]{:S(2)}) copy-start(bf16[9,256,256]{2,1,0:T(8,128)(2,1)} %constant.52.clone.refs_7_.refs_5_) | copy-start | bytes 3538948
  88.5 5.2 %copy-start.3 = (bf16[4,2,64,256]{3,2,1,0:T(8,128)(2,1)S(1)}, bf16[4,2,64,256]{3,2,1,0:T(8,128)(2,1)}, u32[]{:S(2)}) copy-start(bf16[4,2,64,256]{3,2,1,0:T(8,128)(2,1)} %pad_maximum_fusion.1) | copy-start | bytes 786436
  91.3 6.2 %collective-permute-start.21 = (bf16[256,256]{1,0:T(8,128)(2,1)S(1)}, bf16[256,256]{1,0:T(8,128)(2,1)S(1)}, u32[]{:S(2)}, u32[]{:S(2)}) collective-permute-start(bf16[256,256]{1,0:T(8,128)(2,1)S(1)} %bitcast.73), channel_id=1, source_target_pairs={{0,64},{64,128},{128,192},{192,0},{1,65},{65,129},{129,193},{193,1... | collective-permute-start | bytes 393224 | tf_op jit(solution)/shard_map/ppermute | solution.py:295
  91.6 6.5 %collective-permute-start.22 = (bf16[256,256]{1,0:T(8,128)(2,1)S(1)}, bf16[256,256]{1,0:T(8,128)(2,1)S(1)}, u32[]{:S(2)}, u32[]{:S(2)}) collective-permute-start(bf16[256,256]{1,0:T(8,128)(2,1)S(1)} %bitcast.74), channel_id=1, source_target_pairs={{0,192},{64,0},{128,64},{192,128},{1,193},{65,1},{129,65},{193,129... | collective-permute-start | bytes 393224 | tf_op jit(solution)/shard_map/ppermute | solution.py:296
  100.6 16.0 %all-to-all-start.1 = ((bf16[8,108,256]{2,1,0:T(8,128)(2,1)}), bf16[8,108,256]{2,1,0:T(8,128)(2,1)S(1)}, u32[]{:S(2)}, u32[]{:S(2)}) async-start(bf16[8,108,256]{2,1,0:T(8,128)(2,1)} %weight_last.1), calls=%async_computation.1 | async-start | bytes 917504 | tf_op jit(solution)/shard_map/all_to_all | solution.py:380
  104.1 5.9 %collective-permute-start.16 = (bf16[4,2,32,128]{3,2,1,0:T(8,128)(2,1)S(1)}, bf16[4,2,32,128]{3,2,1,0:T(8,128)(2,1)S(1)}, u32[]{:S(2)}, u32[]{:S(2)}) collective-permute-start(bf16[4,2,32,128]{3,2,1,0:T(8,128)(2,1)S(1)} %get-tuple-element.26), channel_id=1, source_target_pairs={{0,4},{4,0},{1,5},{5,1},{2,6},{6,2},{3,7},{7,3},{8,12},{12,8},{9,1... | collective-permute-start | bytes 196616 | tf_op jit(solution)/shard_map/ppermute | solution.py:375
  (4 other events, 2.9 us)

commit v6 on v5

--- a/solution.py
+++ b/solution.py
@@ -131,7 +131,7 @@
 
 
 def conv_kernel(target, flags, *refs):
-    @pl.when(flags[2] == target)
+    @pl.when((flags[2] == target) | (target == 0))
     def _():
         conv_body(flags, *refs)
 
@@ -291,7 +291,7 @@
     left = lax.ppermute(block, "x", ring("x", 1))
     right = lax.ppermute(block, "x", ring("x", -1))
     if between is not None:
-        left, right, between = lax.optimization_barrier((left, right, between))
+        left, between = lax.optimization_barrier((left, between))
     far_a = lax.ppermute(first_half(left), "x", ring("x", 1))
     far_b = lax.ppermute(second_half(right), "x", ring("x", -1))
     blocks = (block, left, right, far_a, far_b)
@@ -349,17 +349,17 @@
         chunk, lambda b: b[: SLOTS // 2], lambda b: b[SLOTS // 2 :], (arrived, fac, act)
     )
     pair_g = both
-    pair_dx = None
     for k in range(4):
         if k > 0:
             same, cross = arrived
             both = [jnp.where(yh == 1, cross, same), jnp.where(yh == 1, same, cross)]
             pair_g = jnp.where(section == 3 - k, jnp.concatenate(both, axis=1), pair_g)
+        if k == 3:
+            arrived = (mine(pair_g, 1), theirs(pair_g, 1))
         sent = conv_back(3 - k, flags, arrived[::-1], s, kernel_rows, fac)
         if k == 0:
             sent, act = lax.optimization_barrier((sent, act))
             acts = gather_x(act, *clips_of_pair())
-        pair_dx = sent if k == 0 else jnp.where(section == 3 - k, sent, pair_dx)
         if k < 3:
             src, dst = 3 - k, 2 - k
             same = lax.ppermute(sent, ("yl", "c"), [(src, dst)])
@@ -368,7 +368,7 @@
             )
             arrived = (same, cross)
 
-    pair_dx = pair_dx.reshape(F, NYH, M, HW, HC)
+    pair_dx = sent.reshape(F, NYH, M, HW, HC)
     kept = lax.dynamic_index_in_dim(pair_dx, yh, 1, False)
     given = lax.dynamic_index_in_dim(pair_dx, 1 - yh, 1, False)
     grads, (kept, given) = gather_x(pair_g, *clips_of_pair(), (kept, given))

time: 118 us -> 118 us (level)
    ppermute x3, waiting for transfers between devices: 2.85 us -> 0.23 us  [gather_x(): right = lax.ppermute(block, 'x', ring('x', -1))]
    ppermute x3, waiting for transfers between devices: 2.12 us -> 4.35 us  [gather_x(): far_b = lax.ppermute(second_half(right), 'x', ring('x', -1))]
    ppermute x3, starting transfers between devices: 5.49 us -> 3.63 us  [gather_x(): far_b = lax.ppermute(second_half(right), 'x', ring('x', -1))]
    ppermute x3, starting transfers between devices: 1.18 us -> 2.9 us  [gather_x(): far_a = lax.ppermute(first_half(left), 'x', ring('x', 1))]
    ppermute x3, waiting for transfers between devices: 13.5 us -> 14.8 us  [gather_x(): left = lax.ppermute(block, 'x', ring('x', 1))]
    unnamed x23 -> x19, local copies, waits for them, and re-layouts: 3.58 us -> 3.55 us
  transfers between devices with their start and end apart: 25 -> 25, of which waited for: 14 -> 12; matrix products, arithmetic and copies ran while one was open for 3% -> 3% of each run, Pallas kernels for 8% -> 9%
where the time goes in v6:
time: 118 us; the launch traced here: 117 us
  waiting for transfers between devices  52.7 us (45%)
  starting transfers between devices  41.8 us (35%)
  Pallas kernels  13.7 us (12%)
  local copies, waits for them, and re-layouts  6.28 us (5%)
  other arithmetic  1.27 us (1%)
    ppermute x3, waiting for transfers between devices, gather_x(): left = lax.ppermute(block, 'x', ring('x', 1))  14.8 us
    ppermute x3, waiting for transfers between devices, local(): lax.ppermute(sent, ('yh', 'yl', 'c'), [(y * N_PIPE + src, (1 - y) * N_PIP...  9.98 us
    all_to_all x1, starting transfers between devices, local(): lax.all_to_all(jnp.broadcast_to(window[None], (NZ, HC, C)), 'z', 0, 0, ti...  8.47 us
    all_to_all x1, waiting for transfers between devices, local(): lax.all_to_all(jnp.broadcast_to(window[None], (NZ, HC, C)), 'z', 0, 0, ti...  7.15 us
    pallas_call x2, Pallas kernels, weight_back(): pl.pallas_call(functools.partial(weight_kernel, len(acts), tail), out_sha...  6.29 us
    all_to_all x1, waiting for transfers between devices, local(): lax.all_to_all(partial, 'z', 0, 0, tiled=True).reshape(NZ, 1, PART, C)  5.86 us
    ppermute x3, starting transfers between devices, gather_x(): right = lax.ppermute(block, 'x', ring('x', -1))  5.57 us
    pallas_call x4, Pallas kernels, conv_back(): pl.pallas_call(functools.partial(conv_kernel, target), out_shape=jax.Shap...  5.5 us
  transfers between devices with their start and end apart: 25, of which 12 were waited for; matrix products, arithmetic and copies ran while one was open for 3% of the time, Pallas kernels for 9%

profile of v6, /device:TPU:6, one launch (start us, length us, event | category | flops | bytes accessed | tf_op | source)
XLA Modules:
  0.0 117.1 jit_solution(11513487171653389424)
XLA Ops:
  1.7 3.3 %collective-permute-start = (bf16[128,256]{1,0:T(8,128)(2,1)S(1)}, bf16[128,256]{1,0:T(8,128)(2,1)S(1)}, u32[]{:S(2)}, u32[]{:S(2)}) collective-permute-start(bf16[128,256]{1,0:T(8,128)(2,1)S(1)} %constant_dynamic-slice_fusion.8), channel_id=1, source_target_pairs={{0,4},{4,0},{1,5},{5,1},{2,6},{6,2},{3,7},{7,3},{8,12},{12,8},{9,1... | collective-permute-start | bytes 196616 | tf_op jit(solution)/shard_map/ppermute | solution.py:330
  8.9 8.5 %all-to-all-start = ((bf16[8,128,256]{2,1,0:T(8,128)(2,1)}), bf16[8,128,256]{2,1,0:T(8,128)(2,1)S(1)}, u32[]{:S(2)}, u32[]{:S(2)}) async-start(bf16[8,128,256]{2,1,0:T(8,128)(2,1)} %broadcast_in_dim.2), calls=%async_computation | async-start | bytes 1048576 | tf_op jit(solution)/shard_map/all_to_all | solution.py:335
  17.4 2.7 %collective-permute-start.3 = (bf16[256,128]{1,0:T(8,128)(2,1)S(1)}, bf16[256,128]{1,0:T(8,128)(2,1)S(1)}, u32[]{:S(2)}, u32[]{:S(2)}) collective-permute-start(bf16[256,128]{1,0:T(8,128)(2,1)S(1)} %get-tuple-element.46), channel_id=1, source_target_pairs={{0,4},{4,0},{1,5},{5,1},{2,6},{6,2},{3,7},{7,3},{8,12},{12,8},{9,1... | collective-permute-start | bytes 196616 | tf_op jit(solution)/shard_map/ppermute | solution.py:339
  20.2 1.0 collective-permute-start.2
  21.2 2.7 %collective-permute-start.4 = (bf16[4,1,64,256]{3,2,1,0:T(8,128)(2,1)S(1)}, bf16[4,1,64,256]{3,2,1,0:T(8,128)(2,1)S(1)}, u32[]{:S(2)}, u32[]{:S(2)}) collective-permute-start(bf16[4,1,64,256]{3,2,1,0:T(8,128)(2,1)S(1)} %bitcast.57), channel_id=1, source_target_pairs={{0,4},{4,0},{1,5},{5,1},{2,6},{6,2},{3,7},{7,3},{8,12},{12,8},{9,1... | collective-permute-start | bytes 393224 | tf_op jit(solution)/shard_map/ppermute | solution.py:347
  23.9 1.2 %norm_factors.1.refs_8_ = f32[3,512,128]{2,1,0:T(8,128)S(1)} custom-call(s32[3]{0:T(128)S(1)} %pad_add_fusion.flags.refs_0_, bf16[256,128]{1,0:T(8,128)(2,1)S(1)} %get-tuple-element.47.mine, bf16[256,128]{1,0:T(8,128)(2,1)S(1)} %collective-permute-done.3.theirs, f32[1,128]{1,0:T(1,128)S(1)} %get-tuple-element.51.gain_ref, ...), custom_call_target="tpu_custom_call" | custom-call | tf_op jit(solution)/shard_map/norm_factors/pallas_call | solution.py:122
  25.1 2.3 %collective-permute-done.2 = bf16[4,1,64,256]{3,2,1,0:T(8,128)(2,1)S(1)} collective-permute-done((bf16[4,1,64,256]{3,2,1,0:T(8,128)(2,1)S(1)}, bf16[4,1,64,256]{3,2,1,0:T(8,128)(2,1)S(1)}, u32[]{:S(2)}, u32[]{:S(2)}) %collective-permute-start.2) | collective-permute-done | bytes 131104 | tf_op jit(solution)/shard_map/ppermute | solution.py:344
  27.4 7.1 %all-to-all-done = bf16[8,128,256]{2,1,0:T(8,128)(2,1)S(1)} async-done(((bf16[8,128,256]{2,1,0:T(8,128)(2,1)}), bf16[8,128,256]{2,1,0:T(8,128)(2,1)S(1)}, u32[]{:S(2)}, u32[]{:S(2)}) %all-to-all-start) | async-done | bytes 524320 | tf_op jit(solution)/shard_map/all_to_all | solution.py:335
  35.1 1.5 %collective-permute-start.5 = (bf16[1024,256]{1,0:T(8,128)(2,1)S(1)}, bf16[1024,256]{1,0:T(8,128)(2,1)S(1)}, u32[]{:S(2)}, u32[]{:S(2)}) collective-permute-start(bf16[1024,256]{1,0:T(8,128)(2,1)S(1)} %bitcast.52), channel_id=1, source_target_pairs={{0,192},{64,0},{128,64},{192,128},{1,193},{65,1},{129,65},{193,129... | collective-permute-start | bytes 1572872 | tf_op jit(solution)/shard_map/ppermute | solution.py:292
  38.2 9.3 %collective-permute-done.1.refs_4_ = bf16[1024,256]{1,0:T(8,128)(2,1)S(1)} collective-permute-done((bf16[1024,256]{1,0:T(8,128)(2,1)S(1)}, bf16[1024,256]{1,0:T(8,128)(2,1)S(1)}, u32[]{:S(2)}, u32[]{:S(2)}) %collective-permute-start.1) | collective-permute-done | bytes 524320 | tf_op jit(solution)/shard_map/ppermute | solution.py:291
  47.5 1.8 %collective-permute-start.6 = (bf16[512,256]{1,0:T(8,128)(2,1)S(1)}, bf16[512,256]{1,0:T(8,128)(2,1)S(1)}, u32[]{:S(2)}, u32[]{:S(2)}) collective-permute-start(bf16[512,256]{1,0:T(8,128)(2,1)S(1)} %slice.18), channel_id=1, source_target_pairs={{0,64},{64,128},{128,192},{192,0},{1,65},{65,129},{129,193},{193,1... | collective-permute-start | bytes 786440 | tf_op jit(solution)/shard_map/ppermute | solution.py:295
  49.7 4.3 %collective-permute-done.6.refs_6_ = bf16[512,256]{1,0:T(8,128)(2,1)S(1)} collective-permute-done((bf16[512,256]{1,0:T(8,128)(2,1)S(1)}, bf16[512,256]{1,0:T(8,128)(2,1)S(1)}, u32[]{:S(2)}, u32[]{:S(2)}) %collective-permute-start.6) | collective-permute-done | bytes 262176 | tf_op jit(solution)/shard_map/ppermute | solution.py:295
  54.0 3.0 %collective-permute-done.7.refs_7_ = bf16[512,256]{1,0:T(8,128)(2,1)S(1)} collective-permute-done((bf16[512,256]{1,0:T(8,128)(2,1)S(1)}, bf16[512,256]{1,0:T(8,128)(2,1)S(1)}, u32[]{:S(2)}, u32[]{:S(2)}) %collective-permute-start.7) | collective-permute-done | bytes 262176 | tf_op jit(solution)/shard_map/ppermute | solution.py:296
  57.0 1.2 %conv_back.4 = bf16[512,128]{1,0:T(8,128)(2,1)} custom-call(s32[3]{0:T(128)S(1)} %pad_add_fusion.flags.refs_0_, bf16[512,128]{1,0:T(8,128)(2,1)S(1)} %get-tuple-element.16.refs_0_, bf16[512,128]{1,0:T(8,128)(2,1)S(1)} %get-tuple-element.17.refs_1_, bf16[9,128,128]{2,1,0:T(8,128)(2,1)S(1)} %copy-done.1, bf16[1024,256]{1,0:T(8,128)(2,1)S(1)} %bitcast.53, ...), custom_call_target="tpu_custom_call" | custom-call | flops 905969664 | bytes 1769472 | tf_op jit(solution)/shard_map/conv_back/pallas_call | solution.py:195
  59.6 2.0 %collective-permute-start.18 = (bf16[512,256]{1,0:T(8,128)(2,1)}, bf16[512,256]{1,0:T(8,128)(2,1)S(1)}, u32[]{:S(2)}, u32[]{:S(2)}) collective-permute-start(bf16[512,256]{1,0:T(8,128)(2,1)} %bitcast.61), channel_id=1, source_target_pairs={{0,192},{64,0},{128,64},{192,128},{1,193},{65,1},{129,65},{193,129... | collective-permute-start | bytes 786440 | tf_op jit(solution)/shard_map/ppermute | solution.py:292
  63.8 3.8 %collective-permute-done.16.refs_2_ = bf16[512,256]{1,0:T(8,128)(2,1)S(1)} collective-permute-done((bf16[512,256]{1,0:T(8,128)(2,1)}, bf16[512,256]{1,0:T(8,128)(2,1)S(1)}, u32[]{:S(2)}, u32[]{:S(2)}) %collective-permute-start.16) | collective-permute-done | bytes 262176 | tf_op jit(solution)/shard_map/ppermute | solution.py:291
  67.9 1.9 %collective-permute-start.19 = (bf16[256,256]{1,0:T(8,128)(2,1)S(1)}, bf16[256,256]{1,0:T(8,128)(2,1)S(1)}, u32[]{:S(2)}, u32[]{:S(2)}) collective-permute-start(bf16[256,256]{1,0:T(8,128)(2,1)S(1)} %bitcast.72), channel_id=1, source_target_pairs={{0,192},{64,0},{128,64},{192,128},{1,193},{65,1},{129,65},{193,129... | collective-permute-start | bytes 393224 | tf_op jit(solution)/shard_map/ppermute | solution.py:296
  70.4 1.4 %collective-permute-start.12 = (bf16[512,128]{1,0:T(8,128)(2,1)S(1)}, bf16[512,128]{1,0:T(8,128)(2,1)S(1)}, u32[]{:S(2)}, u32[]{:S(2)}) collective-permute-start(bf16[512,128]{1,0:T(8,128)(2,1)S(1)} %conv_back.6), channel_id=1, source_target_pairs={{1,4},{5,0},{9,12},{13,8},{17,20},{21,16},{25,28},{29,24},{33,36},... | collective-permute-start | bytes 393224 | tf_op jit(solution)/shard_map/ppermute | solution.py:366
  71.8 1.3 %collective-permute-start.13 = (bf16[512,128]{1,0:T(8,128)(2,1)S(1)}, bf16[512,128]{1,0:T(8,128)(2,1)S(1)}, u32[]{:S(2)}, u32[]{:S(2)}) collective-permute-start(bf16[512,128]{1,0:T(8,128)(2,1)S(1)} %conv_back.6), channel_id=1, source_target_pairs={{1,0},{5,4},{9,8},{13,12},{17,16},{21,20},{25,24},{29,28},{33,32},... | collective-permute-start | bytes 393224 | tf_op jit(solution)/shard_map/ppermute | solution.py:365
  73.1 10.0 %collective-permute-done.12 = bf16[512,128]{1,0:T(8,128)(2,1)S(1)} collective-permute-done((bf16[512,128]{1,0:T(8,128)(2,1)S(1)}, bf16[512,128]{1,0:T(8,128)(2,1)S(1)}, u32[]{:S(2)}, u32[]{:S(2)}) %collective-permute-start.12) | collective-permute-done | bytes 131104 | tf_op jit(solution)/shard_map/ppermute | solution.py:366
  83.4 2.0 %collective-permute-start.21 = (bf16[512,256]{1,0:T(8,128)(2,1)S(1)}, bf16[512,256]{1,0:T(8,128)(2,1)S(1)}, u32[]{:S(2)}, u32[]{:S(2)}) collective-permute-start(bf16[512,256]{1,0:T(8,128)(2,1)S(1)} %maximum_select_fusion.refs_4_), channel_id=1, source_target_pairs={{0,192},{64,0},{128,64},{192,128},{1,193},{65,1},{129,65},{193,129... | collective-permute-start | bytes 786440 | tf_op jit(solution)/shard_map/ppermute | solution.py:292
  85.5 3.0 %conv_back.7 = bf16[512,128]{1,0:T(8,128)(2,1)S(1)} custom-call(s32[3]{0:T(128)S(1)} %pad_add_fusion.flags.refs_0_, bf16[512,128]{1,0:T(8,128)(2,1)S(1)} %get-tuple-element.29.refs_0_, bf16[512,128]{1,0:T(8,128)(2,1)S(1)} %get-tuple-element.28.refs_1_, bf16[9,128,128]{2,1,0:T(8,128)(2,1)S(1)} %copy-done.1, bf16[1024,256]{1,0:T(8,128)(2,1)S(1)} %bitcast.56, ...), custom_call_target="tpu_custom_call" | custom-call | flops 905969664 | bytes 1769472 | tf_op jit(solution)/shard_map/conv_back/pallas_call | solution.py:195
  88.5 1.6 %collective-permute-done.14.refs_5_ = bf16[512,256]{1,0:T(8,128)(2,1)S(1)} collective-permute-done((bf16[512,256]{1,0:T(8,128)(2,1)S(1)}, bf16[512,256]{1,0:T(8,128)(2,1)S(1)}, u32[]{:S(2)}, u32[]{:S(2)}) %collective-permute-start.14) | collective-permute-done | bytes 262176 | tf_op jit(solution)/shard_map/ppermute | solution.py:291
  90.2 1.1 collective-permute-start.20
  91.3 1.3 %collective-permute-start.22 = (bf16[256,256]{1,0:T(8,128)(2,1)S(1)}, bf16[256,256]{1,0:T(8,128)(2,1)S(1)}, u32[]{:S(2)}, u32[]{:S(2)}) collective-permute-start(bf16[256,256]{1,0:T(8,128)(2,1)S(1)} %bitcast.74), channel_id=1, source_target_pairs={{0,192},{64,0},{128,64},{192,128},{1,193},{65,1},{129,65},{193,129... | collective-permute-start | bytes 393224 | tf_op jit(solution)/shard_map/ppermute | solution.py:296
  92.6 3.7 %weight_first.1.refs_6_ = f32[8,128,256]{2,1,0:T(8,128)S(1)} custom-call(s32[3]{0:T(128)S(1)} %pad_add_fusion.flags.refs_0_, bf16[512,256]{1,0:T(8,128)(2,1)S(1)} %bitcast.62, bf16[512,256]{1,0:T(8,128)(2,1)S(1)} %collective-permute-done.16.refs_2_, bf16[512,256]{1,0:T(8,128)(2,1)S(1)} %collective-permute-done.18.refs_3_, ...), custom_call_target="tpu_custom_call" | custom-call | flops 1358954496 | bytes 4194304 | tf_op jit(solution)/shard_map/weight_first/pallas_call | solution.py:265
  96.4 1.4 %collective-permute-done.22.refs_4_ = bf16[256,256]{1,0:T(8,128)(2,1)S(1)} collective-permute-done((bf16[256,256]{1,0:T(8,128)(2,1)S(1)}, bf16[256,256]{1,0:T(8,128)(2,1)S(1)}, u32[]{:S(2)}, u32[]{:S(2)}) %collective-permute-start.22) | collective-permute-done | bytes 131104 | tf_op jit(solution)/shard_map/ppermute | solution.py:296
  97.7 2.6 %weight_last.1 = bf16[8,108,256]{2,1,0:T(8,128)(2,1)} custom-call(s32[3]{0:T(128)S(1)} %pad_add_fusion.flags.refs_0_, bf16[256,256]{1,0:T(8,128)(2,1)S(1)} %collective-permute-done.17.refs_1_, bf16[256,256]{1,0:T(8,128)(2,1)S(1)} %collective-permute-done.19.refs_2_, bf16[256,256]{1,0:T(8,128)(2,1)S(1)} %collective-permute-done.20.refs_3_, ...), custom_call_target="tpu_custom_call" | custom-call | flops 452984832 | bytes 4194304 | tf_op jit(solution)/shard_map/weight_last/pallas_call | solution.py:265
  100.3 3.5 %all-to-all-start.1 = ((bf16[8,108,256]{2,1,0:T(8,128)(2,1)}), bf16[8,108,256]{2,1,0:T(8,128)(2,1)S(1)}, u32[]{:S(2)}, u32[]{:S(2)}) async-start(bf16[8,108,256]{2,1,0:T(8,128)(2,1)} %weight_last.1), calls=%async_computation.1 | async-start | bytes 917504 | tf_op jit(solution)/shard_map/all_to_all | solution.py:380
  103.8 2.1 %collective-permute-start.15 = (bf16[4,2,32,128]{3,2,1,0:T(8,128)(2,1)S(1)}, bf16[4,2,32,128]{3,2,1,0:T(8,128)(2,1)S(1)}, u32[]{:S(2)}, u32[]{:S(2)}) collective-permute-start(bf16[4,2,32,128]{3,2,1,0:T(8,128)(2,1)S(1)} %get-tuple-element.23), channel_id=1, source_target_pairs={{0,4},{4,0},{1,5},{5,1},{2,6},{6,2},{3,7},{7,3},{8,12},{12,8},{9,1... | collective-permute-start | bytes 196616 | tf_op jit(solution)/shard_map/ppermute | solution.py:375
  105.9 3.8 %collective-permute-done.15 = bf16[4,2,32,128]{3,2,1,0:T(8,128)(2,1)S(1)} collective-permute-done((bf16[4,2,32,128]{3,2,1,0:T(8,128)(2,1)S(1)}, bf16[4,2,32,128]{3,2,1,0:T(8,128)(2,1)S(1)}, u32[]{:S(2)}, u32[]{:S(2)}) %collective-permute-start.15) | collective-permute-done | bytes 65568 | tf_op jit(solution)/shard_map/ppermute | solution.py:375
  110.4 5.9 %all-to-all-done.1 = bf16[8,108,256]{2,1,0:T(8,128)(2,1)S(1)} async-done(((bf16[8,108,256]{2,1,0:T(8,128)(2,1)}), bf16[8,108,256]{2,1,0:T(8,128)(2,1)S(1)}, u32[]{:S(2)}, u32[]{:S(2)}) %all-to-all-start.1) | async-done | bytes 442400 | tf_op jit(solution)/shard_map/all_to_all | solution.py:380
  (79 shorter events, 13.9 us)
Async XLA Ops:
  0.6 0.8 copy-start
  1.7 6.4 %collective-permute-start = (bf16[128,256]{1,0:T(8,128)(2,1)S(1)}, bf16[128,256]{1,0:T(8,128)(2,1)S(1)}, u32[]{:S(2)}, u32[]{:S(2)}) collective-permute-start(bf16[128,256]{1,0:T(8,128)(2,1)S(1)} %constant_dynamic-slice_fusion.8), channel_id=1, source_target_pairs={{0,4},{4,0},{1,5},{5,1},{2,6},{6,2},{3,7},{7,3},{8,12},{12,8},{9,1... | collective-permute-start | bytes 196616 | tf_op jit(solution)/shard_map/ppermute | solution.py:330
  7.2 12.9 %copy-start.8 = (bf16[1,2,4,8,4,256]{5,4,3,2,1,0:T(4,128)(2,1)S(1)}, bf16[1,2,4,8,4,256]{5,4,3,2,1,0:T(4,128)(2,1)}, u32[]{:S(2)}) copy-start(bf16[1,2,4,8,4,256]{5,4,3,2,1,0:T(4,128)(2,1)} %param.8) | copy-start | bytes 393220
  8.9 25.7 %all-to-all-start = ((bf16[8,128,256]{2,1,0:T(8,128)(2,1)}), bf16[8,128,256]{2,1,0:T(8,128)(2,1)S(1)}, u32[]{:S(2)}, u32[]{:S(2)}) async-start(bf16[8,128,256]{2,1,0:T(8,128)(2,1)} %broadcast_in_dim.2), calls=%async_computation | async-start | bytes 1048576 | tf_op jit(solution)/shard_map/all_to_all | solution.py:335
  17.4 6.6 %collective-permute-start.3 = (bf16[256,128]{1,0:T(8,128)(2,1)S(1)}, bf16[256,128]{1,0:T(8,128)(2,1)S(1)}, u32[]{:S(2)}, u32[]{:S(2)}) collective-permute-start(bf16[256,128]{1,0:T(8,128)(2,1)S(1)} %get-tuple-element.46), channel_id=1, source_target_pairs={{0,4},{4,0},{1,5},{5,1},{2,6},{6,2},{3,7},{7,3},{8,12},{12,8},{9,1... | collective-permute-start | bytes 196616 | tf_op jit(solution)/shard_map/ppermute | solution.py:339
  20.2 7.2 %collective-permute-start.2 = (bf16[4,1,64,256]{3,2,1,0:T(8,128)(2,1)S(1)}, bf16[4,1,64,256]{3,2,1,0:T(8,128)(2,1)S(1)}, u32[]{:S(2)}, u32[]{:S(2)}) collective-permute-start(bf16[4,1,64,256]{3,2,1,0:T(8,128)(2,1)S(1)} %bitcast.68), channel_id=1, source_target_pairs={{0,4},{4,0},{1,5},{5,1},{2,6},{6,2},{3,7},{7,3},{8,12},{12,8},{9,1... | collective-permute-start | bytes 393224 | tf_op jit(solution)/shard_map/ppermute | solution.py:344
  21.2 16.2 %collective-permute-start.4 = (bf16[4,1,64,256]{3,2,1,0:T(8,128)(2,1)S(1)}, bf16[4,1,64,256]{3,2,1,0:T(8,128)(2,1)S(1)}, u32[]{:S(2)}, u32[]{:S(2)}) collective-permute-start(bf16[4,1,64,256]{3,2,1,0:T(8,128)(2,1)S(1)} %bitcast.57), channel_id=1, source_target_pairs={{0,4},{4,0},{1,5},{5,1},{2,6},{6,2},{3,7},{7,3},{8,12},{12,8},{9,1... | collective-permute-start | bytes 393224 | tf_op jit(solution)/shard_map/ppermute | solution.py:347
  34.6 12.9 %collective-permute-start.1 = (bf16[1024,256]{1,0:T(8,128)(2,1)S(1)}, bf16[1024,256]{1,0:T(8,128)(2,1)S(1)}, u32[]{:S(2)}, u32[]{:S(2)}) collective-permute-start(bf16[1024,256]{1,0:T(8,128)(2,1)S(1)} %bitcast.51), channel_id=1, source_target_pairs={{0,64},{64,128},{128,192},{192,0},{1,65},{65,129},{129,193},{193,1... | collective-permute-start | bytes 1572872 | tf_op jit(solution)/shard_map/ppermute | solution.py:291
  35.1 14.2 %collective-permute-start.5 = (bf16[1024,256]{1,0:T(8,128)(2,1)S(1)}, bf16[1024,256]{1,0:T(8,128)(2,1)S(1)}, u32[]{:S(2)}, u32[]{:S(2)}) collective-permute-start(bf16[1024,256]{1,0:T(8,128)(2,1)S(1)} %bitcast.52), channel_id=1, source_target_pairs={{0,192},{64,0},{128,64},{192,128},{1,193},{65,1},{129,65},{193,129... | collective-permute-start | bytes 1572872 | tf_op jit(solution)/shard_map/ppermute | solution.py:292
  36.6 0.7 copy-start.6
  37.4 19.6 %copy-start.1 = (bf16[9,128,128]{2,1,0:T(8,128)(2,1)S(1)}, bf16[9,128,128]{2,1,0:T(8,128)(2,1)}, u32[]{:S(2)}) copy-start(bf16[9,128,128]{2,1,0:T(8,128)(2,1)} %constant.51.clone.refs_2_) | copy-start | bytes 884740
  47.5 6.5 %collective-permute-start.6 = (bf16[512,256]{1,0:T(8,128)(2,1)S(1)}, bf16[512,256]{1,0:T(8,128)(2,1)S(1)}, u32[]{:S(2)}, u32[]{:S(2)}) collective-permute-start(bf16[512,256]{1,0:T(8,128)(2,1)S(1)} %slice.18), channel_id=1, source_target_pairs={{0,64},{64,128},{128,192},{192,0},{1,65},{65,129},{129,193},{193,1... | collective-permute-start | bytes 786440 | tf_op jit(solution)/shard_map/ppermute | solution.py:295
  49.3 7.7 %collective-permute-start.7 = (bf16[512,256]{1,0:T(8,128)(2,1)S(1)}, bf16[512,256]{1,0:T(8,128)(2,1)S(1)}, u32[]{:S(2)}, u32[]{:S(2)}) collective-permute-start(bf16[512,256]{1,0:T(8,128)(2,1)S(1)} %slice.24), channel_id=1, source_target_pairs={{0,192},{64,0},{128,64},{192,128},{1,193},{65,1},{129,65},{193,129... | collective-permute-start | bytes 786440 | tf_op jit(solution)/shard_map/ppermute | solution.py:296
  58.2 3.5 %collective-permute-start.8 = (bf16[512,128]{1,0:T(8,128)(2,1)}, bf16[512,128]{1,0:T(8,128)(2,1)S(1)}, u32[]{:S(2)}, u32[]{:S(2)}) collective-permute-start(bf16[512,128]{1,0:T(8,128)(2,1)} %conv_back.4), channel_id=1, source_target_pairs={{3,6},{7,2},{11,14},{15,10},{19,22},{23,18},{27,30},{31,26},{35,38... | collective-permute-start | bytes 393224 | tf_op jit(solution)/shard_map/ppermute | solution.py:366
  58.8 2.8 %collective-permute-start.9 = (bf16[512,128]{1,0:T(8,128)(2,1)}, bf16[512,128]{1,0:T(8,128)(2,1)S(1)}, u32[]{:S(2)}, u32[]{:S(2)}) collective-permute-start(bf16[512,128]{1,0:T(8,128)(2,1)} %conv_back.4), channel_id=1, source_target_pairs={{3,2},{7,6},{11,10},{15,14},{19,18},{23,22},{27,26},{31,30},{35,34... | collective-permute-start | bytes 393224 | tf_op jit(solution)/shard_map/ppermute | solution.py:365
  59.5 8.1 %collective-permute-start.16 = (bf16[512,256]{1,0:T(8,128)(2,1)}, bf16[512,256]{1,0:T(8,128)(2,1)S(1)}, u32[]{:S(2)}, u32[]{:S(2)}) collective-permute-start(bf16[512,256]{1,0:T(8,128)(2,1)} %bitcast.60), channel_id=1, source_target_pairs={{0,64},{64,128},{128,192},{192,0},{1,65},{65,129},{129,193},{193,1... | collective-permute-start | bytes 786440 | tf_op jit(solution)/shard_map/ppermute | solution.py:291
  59.6 8.3 %collective-permute-start.18 = (bf16[512,256]{1,0:T(8,128)(2,1)}, bf16[512,256]{1,0:T(8,128)(2,1)S(1)}, u32[]{:S(2)}, u32[]{:S(2)}) collective-permute-start(bf16[512,256]{1,0:T(8,128)(2,1)} %bitcast.61), channel_id=1, source_target_pairs={{0,192},{64,0},{128,64},{192,128},{1,193},{65,1},{129,65},{193,129... | collective-permute-start | bytes 786440 | tf_op jit(solution)/shard_map/ppermute | solution.py:292
  62.4 7.4 %collective-permute-start.10 = (bf16[512,128]{1,0:T(8,128)(2,1)S(1)}, bf16[512,128]{1,0:T(8,128)(2,1)S(1)}, u32[]{:S(2)}, u32[]{:S(2)}) collective-permute-start(bf16[512,128]{1,0:T(8,128)(2,1)S(1)} %conv_back.5), channel_id=1, source_target_pairs={{2,5},{6,1},{10,13},{14,9},{18,21},{22,17},{26,29},{30,25},{34,37}... | collective-permute-start | bytes 393224 | tf_op jit(solution)/shard_map/ppermute | solution.py:366
  63.1 6.8 %collective-permute-start.11 = (bf16[512,128]{1,0:T(8,128)(2,1)S(1)}, bf16[512,128]{1,0:T(8,128)(2,1)S(1)}, u32[]{:S(2)}, u32[]{:S(2)}) collective-permute-start(bf16[512,128]{1,0:T(8,128)(2,1)S(1)} %conv_back.5), channel_id=1, source_target_pairs={{2,1},{6,5},{10,9},{14,13},{18,17},{22,21},{26,25},{30,29},{34,33}... | collective-permute-start | bytes 393224 | tf_op jit(solution)/shard_map/ppermute | solution.py:365
  67.6 28.7 %collective-permute-start.17 = (bf16[256,256]{1,0:T(8,128)(2,1)S(1)}, bf16[256,256]{1,0:T(8,128)(2,1)S(1)}, u32[]{:S(2)}, u32[]{:S(2)}) collective-permute-start(bf16[256,256]{1,0:T(8,128)(2,1)S(1)} %bitcast.71), channel_id=1, source_target_pairs={{0,64},{64,128},{128,192},{192,0},{1,65},{65,129},{129,193},{193,1... | collective-permute-start | bytes 393224 | tf_op jit(solution)/shard_map/ppermute | solution.py:295
  67.9 28.4 %collective-permute-start.19 = (bf16[256,256]{1,0:T(8,128)(2,1)S(1)}, bf16[256,256]{1,0:T(8,128)(2,1)S(1)}, u32[]{:S(2)}, u32[]{:S(2)}) collective-permute-start(bf16[256,256]{1,0:T(8,128)(2,1)S(1)} %bitcast.72), channel_id=1, source_target_pairs={{0,192},{64,0},{128,64},{192,128},{1,193},{65,1},{129,65},{193,129... | collective-permute-start | bytes 393224 | tf_op jit(solution)/shard_map/ppermute | solution.py:296
  70.4 12.8 %copy-start.7 = (bf16[4,2,64,256]{3,2,1,0:T(8,128)(2,1)S(1)}, bf16[4,2,64,256]{3,2,1,0:T(8,128)(2,1)}, u32[]{:S(2)}) copy-start(bf16[4,2,64,256]{3,2,1,0:T(8,128)(2,1)} %copy-done.6) | copy-start | bytes 786436
  70.4 12.7 %collective-permute-start.12 = (bf16[512,128]{1,0:T(8,128)(2,1)S(1)}, bf16[512,128]{1,0:T(8,128)(2,1)S(1)}, u32[]{:S(2)}, u32[]{:S(2)}) collective-permute-start(bf16[512,128]{1,0:T(8,128)(2,1)S(1)} %conv_back.6), channel_id=1, source_target_pairs={{1,4},{5,0},{9,12},{13,8},{17,20},{21,16},{25,28},{29,24},{33,36},... | collective-permute-start | bytes 393224 | tf_op jit(solution)/shard_map/ppermute | solution.py:366
  71.8 11.3 %collective-permute-start.13 = (bf16[512,128]{1,0:T(8,128)(2,1)S(1)}, bf16[512,128]{1,0:T(8,128)(2,1)S(1)}, u32[]{:S(2)}, u32[]{:S(2)}) collective-permute-start(bf16[512,128]{1,0:T(8,128)(2,1)S(1)} %conv_back.6), channel_id=1, source_target_pairs={{1,0},{5,4},{9,8},{13,12},{17,16},{21,20},{25,24},{29,28},{33,32},... | collective-permute-start | bytes 393224 | tf_op jit(solution)/shard_map/ppermute | solution.py:365
  83.3 6.8 %collective-permute-start.14 = (bf16[512,256]{1,0:T(8,128)(2,1)S(1)}, bf16[512,256]{1,0:T(8,128)(2,1)S(1)}, u32[]{:S(2)}, u32[]{:S(2)}) collective-permute-start(bf16[512,256]{1,0:T(8,128)(2,1)S(1)} %maximum_select_fusion.refs_4_), channel_id=1, source_target_pairs={{0,64},{64,128},{128,192},{192,0},{1,65},{65,129},{129,193},{193,1... | collective-permute-start | bytes 786440 | tf_op jit(solution)/shard_map/ppermute | solution.py:291
  83.4 7.8 %collective-permute-start.21 = (bf16[512,256]{1,0:T(8,128)(2,1)S(1)}, bf16[512,256]{1,0:T(8,128)(2,1)S(1)}, u32[]{:S(2)}, u32[]{:S(2)}) collective-permute-start(bf16[512,256]{1,0:T(8,128)(2,1)S(1)} %maximum_select_fusion.refs_4_), channel_id=1, source_target_pairs={{0,192},{64,0},{128,64},{192,128},{1,193},{65,1},{129,65},{193,129... | collective-permute-start | bytes 786440 | tf_op jit(solution)/shard_map/ppermute | solution.py:292
  85.5 7.1 %copy-start.2 = (bf16[9,256,256]{2,1,0:T(8,128)(2,1)S(1)}, bf16[9,256,256]{2,1,0:T(8,128)(2,1)}, u32[]{:S(2)}) copy-start(bf16[9,256,256]{2,1,0:T(8,128)(2,1)} %constant.52.clone.refs_7_.refs_5_) | copy-start | bytes 3538948
  85.5 7.1 %copy-start.3 = (bf16[4,2,64,256]{3,2,1,0:T(8,128)(2,1)S(1)}, bf16[4,2,64,256]{3,2,1,0:T(8,128)(2,1)}, u32[]{:S(2)}) copy-start(bf16[4,2,64,256]{3,2,1,0:T(8,128)(2,1)} %pad_maximum_fusion.1) | copy-start | bytes 786436
  90.2 6.2 %collective-permute-start.20 = (bf16[256,256]{1,0:T(8,128)(2,1)S(1)}, bf16[256,256]{1,0:T(8,128)(2,1)S(1)}, u32[]{:S(2)}, u32[]{:S(2)}) collective-permute-start(bf16[256,256]{1,0:T(8,128)(2,1)S(1)} %bitcast.73), channel_id=1, source_target_pairs={{0,64},{64,128},{128,192},{192,0},{1,65},{65,129},{129,193},{193,1... | collective-permute-start | bytes 393224 | tf_op jit(solution)/shard_map/ppermute | solution.py:295
  91.3 6.5 %collective-permute-start.22 = (bf16[256,256]{1,0:T(8,128)(2,1)S(1)}, bf16[256,256]{1,0:T(8,128)(2,1)S(1)}, u32[]{:S(2)}, u32[]{:S(2)}) collective-permute-start(bf16[256,256]{1,0:T(8,128)(2,1)S(1)} %bitcast.74), channel_id=1, source_target_pairs={{0,192},{64,0},{128,64},{192,128},{1,193},{65,1},{129,65},{193,129... | collective-permute-start | bytes 393224 | tf_op jit(solution)/shard_map/ppermute | solution.py:296
  100.3 16.0 %all-to-all-start.1 = ((bf16[8,108,256]{2,1,0:T(8,128)(2,1)}), bf16[8,108,256]{2,1,0:T(8,128)(2,1)S(1)}, u32[]{:S(2)}, u32[]{:S(2)}) async-start(bf16[8,108,256]{2,1,0:T(8,128)(2,1)} %weight_last.1), calls=%async_computation.1 | async-start | bytes 917504 | tf_op jit(solution)/shard_map/all_to_all | solution.py:380
  103.8 5.9 %collective-permute-start.15 = (bf16[4,2,32,128]{3,2,1,0:T(8,128)(2,1)S(1)}, bf16[4,2,32,128]{3,2,1,0:T(8,128)(2,1)S(1)}, u32[]{:S(2)}, u32[]{:S(2)}) collective-permute-start(bf16[4,2,32,128]{3,2,1,0:T(8,128)(2,1)S(1)} %get-tuple-element.23), channel_id=1, source_target_pairs={{0,4},{4,0},{1,5},{5,1},{2,6},{6,2},{3,7},{7,3},{8,12},{12,8},{9,1... | collective-permute-start | bytes 196616 | tf_op jit(solution)/shard_map/ppermute | solution.py:375
  (2 other events, 1.4 us)

commit v7 on v6

--- a/solution.py
+++ b/solution.py
@@ -357,7 +357,7 @@
         if k == 3:
             arrived = (mine(pair_g, 1), theirs(pair_g, 1))
         sent = conv_back(3 - k, flags, arrived[::-1], s, kernel_rows, fac)
-        if k == 0:
+        if k == 1:
             sent, act = lax.optimization_barrier((sent, act))
             acts = gather_x(act, *clips_of_pair())
         if k < 3:

time: 118 us -> 123 us (1.042)
  waiting for transfers between devices: 52.7 us -> 56.6 us
    ppermute x3, starting transfers between devices: 2.9 us -> 5.97 us  [gather_x(): far_a = lax.ppermute(first_half(left), 'x', ring('x', 1))]
    ppermute x3, waiting for transfers between devices: 9.98 us -> 12.8 us  [local(): lax.ppermute(sent, ('yh', 'yl', 'c'), [(y * N_PIPE + src, (1 - y) * N_PIP...]
    ppermute x3, waiting for transfers between devices: 14.8 us -> 12.5 us  [gather_x(): left = lax.ppermute(block, 'x', ring('x', 1))]
    all_to_all x1, waiting for transfers between devices: 5.86 us -> 8.17 us  [local(): lax.all_to_all(partial, 'z', 0, 0, tiled=True).reshape(NZ, 1, PART, C)]
    ppermute x3, starting transfers between devices: 3.63 us -> 1.43 us  [gather_x(): far_b = lax.ppermute(second_half(right), 'x', ring('x', -1))]
    unnamed x19 -> x23, local copies, waits for them, and re-layouts: 3.55 us -> 3.57 us
  transfers between devices with their start and end apart: 25 -> 25, of which waited for: 12 -> 12; matrix products, arithmetic and copies ran while one was open for 3% -> 3% of each run, Pallas kernels for 9% -> 8%
where the time goes in v7:
time: 123 us; the launch traced here: 122 us
  waiting for transfers between devices  56.6 us (46%)
  starting transfers between devices  42.4 us (34%)
  Pallas kernels  13.6 us (11%)
  local copies, waits for them, and re-layouts  6.31 us (5%)
  other arithmetic  1.27 us (1%)
    ppermute x3, waiting for transfers between devices, local(): lax.ppermute(sent, ('yh', 'yl', 'c'), [(y * N_PIPE + src, (1 - y) * N_PIP...  12.8 us
    ppermute x3, waiting for transfers between devices, gather_x(): left = lax.ppermute(block, 'x', ring('x', 1))  12.5 us
    all_to_all x1, starting transfers between devices, local(): lax.all_to_all(jnp.broadcast_to(window[None], (NZ, HC, C)), 'z', 0, 0, ti...  8.47 us
    all_to_all x1, waiting for transfers between devices, local(): lax.all_to_all(partial, 'z', 0, 0, tiled=True).reshape(NZ, 1, PART, C)  8.17 us
    all_to_all x1, waiting for transfers between devices, local(): lax.all_to_all(jnp.broadcast_to(window[None], (NZ, HC, C)), 'z', 0, 0, ti...  7.15 us
    pallas_call x2, Pallas kernels, weight_back(): pl.pallas_call(functools.partial(weight_kernel, len(acts), tail), out_sha...  6.34 us
    ppermute x3, starting transfers between devices, gather_x(): far_a = lax.ppermute(first_half(left), 'x', ring('x', 1))  5.97 us
    ppermute x3, starting transfers between devices, gather_x(): right = lax.ppermute(block, 'x', ring('x', -1))  5.57 us
  transfers between devices with their start and end apart: 25, of which 12 were waited for; matrix products, arithmetic and copies ran while one was open for 3% of the time, Pallas kernels for 8%

profile of v7, /device:TPU:6, one launch (start us, length us, event | category | flops | bytes accessed | tf_op | source)
XLA Modules:
  0.0 121.5 jit_solution(6409460047340486077)
XLA Ops:
  1.7 3.3 %collective-permute-start = (bf16[128,256]{1,0:T(8,128)(2,1)S(1)}, bf16[128,256]{1,0:T(8,128)(2,1)S(1)}, u32[]{:S(2)}, u32[]{:S(2)}) collective-permute-start(bf16[128,256]{1,0:T(8,128)(2,1)S(1)} %constant_dynamic-slice_fusion.8), channel_id=1, source_target_pairs={{0,4},{4,0},{1,5},{5,1},{2,6},{6,2},{3,7},{7,3},{8,12},{12,8},{9,1... | collective-permute-start | bytes 196616 | tf_op jit(solution)/shard_map/ppermute | solution.py:330
  4.9 0.9 reshape.47.x_ref
  8.9 8.5 %all-to-all-start = ((bf16[8,128,256]{2,1,0:T(8,128)(2,1)}), bf16[8,128,256]{2,1,0:T(8,128)(2,1)S(1)}, u32[]{:S(2)}, u32[]{:S(2)}) async-start(bf16[8,128,256]{2,1,0:T(8,128)(2,1)} %broadcast_in_dim.2), calls=%async_computation | async-start | bytes 1048576 | tf_op jit(solution)/shard_map/all_to_all | solution.py:335
  17.4 2.7 %collective-permute-start.3 = (bf16[256,128]{1,0:T(8,128)(2,1)S(1)}, bf16[256,128]{1,0:T(8,128)(2,1)S(1)}, u32[]{:S(2)}, u32[]{:S(2)}) collective-permute-start(bf16[256,128]{1,0:T(8,128)(2,1)S(1)} %get-tuple-element.46), channel_id=1, source_target_pairs={{0,4},{4,0},{1,5},{5,1},{2,6},{6,2},{3,7},{7,3},{8,12},{12,8},{9,1... | collective-permute-start | bytes 196616 | tf_op jit(solution)/shard_map/ppermute | solution.py:339
  20.2 1.0 collective-permute-start.2
  21.3 2.7 %collective-permute-start.4 = (bf16[4,1,64,256]{3,2,1,0:T(8,128)(2,1)S(1)}, bf16[4,1,64,256]{3,2,1,0:T(8,128)(2,1)S(1)}, u32[]{:S(2)}, u32[]{:S(2)}) collective-permute-start(bf16[4,1,64,256]{3,2,1,0:T(8,128)(2,1)S(1)} %bitcast.57), channel_id=1, source_target_pairs={{0,4},{4,0},{1,5},{5,1},{2,6},{6,2},{3,7},{7,3},{8,12},{12,8},{9,1... | collective-permute-start | bytes 393224 | tf_op jit(solution)/shard_map/ppermute | solution.py:347
  24.0 1.2 norm_factors.1.refs_8_
  25.1 2.3 %collective-permute-done.2 = bf16[4,1,64,256]{3,2,1,0:T(8,128)(2,1)S(1)} collective-permute-done((bf16[4,1,64,256]{3,2,1,0:T(8,128)(2,1)S(1)}, bf16[4,1,64,256]{3,2,1,0:T(8,128)(2,1)S(1)}, u32[]{:S(2)}, u32[]{:S(2)}) %collective-permute-start.2) | collective-permute-done | bytes 131104 | tf_op jit(solution)/shard_map/ppermute | solution.py:344
  27.5 7.1 %all-to-all-done = bf16[8,128,256]{2,1,0:T(8,128)(2,1)S(1)} async-done(((bf16[8,128,256]{2,1,0:T(8,128)(2,1)}), bf16[8,128,256]{2,1,0:T(8,128)(2,1)S(1)}, u32[]{:S(2)}, u32[]{:S(2)}) %all-to-all-start) | async-done | bytes 524320 | tf_op jit(solution)/shard_map/all_to_all | solution.py:335
  35.1 1.5 %collective-permute-start.5 = (bf16[1024,256]{1,0:T(8,128)(2,1)S(1)}, bf16[1024,256]{1,0:T(8,128)(2,1)S(1)}, u32[]{:S(2)}, u32[]{:S(2)}) collective-permute-start(bf16[1024,256]{1,0:T(8,128)(2,1)S(1)} %bitcast.52), channel_id=1, source_target_pairs={{0,192},{64,0},{128,64},{192,128},{1,193},{65,1},{129,65},{193,129... | collective-permute-start | bytes 1572872 | tf_op jit(solution)/shard_map/ppermute | solution.py:292
  38.2 9.3 %collective-permute-done.1.refs_4_ = bf16[1024,256]{1,0:T(8,128)(2,1)S(1)} collective-permute-done((bf16[1024,256]{1,0:T(8,128)(2,1)S(1)}, bf16[1024,256]{1,0:T(8,128)(2,1)S(1)}, u32[]{:S(2)}, u32[]{:S(2)}) %collective-permute-start.1) | collective-permute-done | bytes 524320 | tf_op jit(solution)/shard_map/ppermute | solution.py:291
  47.6 1.8 %collective-permute-start.6 = (bf16[512,256]{1,0:T(8,128)(2,1)S(1)}, bf16[512,256]{1,0:T(8,128)(2,1)S(1)}, u32[]{:S(2)}, u32[]{:S(2)}) collective-permute-start(bf16[512,256]{1,0:T(8,128)(2,1)S(1)} %slice.18), channel_id=1, source_target_pairs={{0,64},{64,128},{128,192},{192,0},{1,65},{65,129},{129,193},{193,1... | collective-permute-start | bytes 786440 | tf_op jit(solution)/shard_map/ppermute | solution.py:295
  49.8 4.3 %collective-permute-done.6.refs_6_ = bf16[512,256]{1,0:T(8,128)(2,1)S(1)} collective-permute-done((bf16[512,256]{1,0:T(8,128)(2,1)S(1)}, bf16[512,256]{1,0:T(8,128)(2,1)S(1)}, u32[]{:S(2)}, u32[]{:S(2)}) %collective-permute-start.6) | collective-permute-done | bytes 262176 | tf_op jit(solution)/shard_map/ppermute | solution.py:295
  54.0 3.0 %collective-permute-done.7.refs_7_ = bf16[512,256]{1,0:T(8,128)(2,1)S(1)} collective-permute-done((bf16[512,256]{1,0:T(8,128)(2,1)S(1)}, bf16[512,256]{1,0:T(8,128)(2,1)S(1)}, u32[]{:S(2)}, u32[]{:S(2)}) %collective-permute-start.7) | collective-permute-done | bytes 262176 | tf_op jit(solution)/shard_map/ppermute | solution.py:296
  57.0 1.2 conv_back.4
  61.6 2.0 %collective-permute-start.18 = (bf16[512,256]{1,0:T(8,128)(2,1)S(1)}, bf16[512,256]{1,0:T(8,128)(2,1)S(1)}, u32[]{:S(2)}, u32[]{:S(2)}) collective-permute-start(bf16[512,256]{1,0:T(8,128)(2,1)S(1)} %bitcast.61), channel_id=1, source_target_pairs={{0,192},{64,0},{128,64},{192,128},{1,193},{65,1},{129,65},{193,129... | collective-permute-start | bytes 786440 | tf_op jit(solution)/shard_map/ppermute | solution.py:292
  64.2 1.4 %collective-permute-start.12 = (bf16[512,128]{1,0:T(8,128)(2,1)S(1)}, bf16[512,128]{1,0:T(8,128)(2,1)S(1)}, u32[]{:S(2)}, u32[]{:S(2)}) collective-permute-start(bf16[512,128]{1,0:T(8,128)(2,1)S(1)} %conv_back.6), channel_id=1, source_target_pairs={{1,4},{5,0},{9,12},{13,8},{17,20},{21,16},{25,28},{29,24},{33,36},... | collective-permute-start | bytes 393224 | tf_op jit(solution)/shard_map/ppermute | solution.py:366
  65.7 1.3 %collective-permute-start.13 = (bf16[512,128]{1,0:T(8,128)(2,1)S(1)}, bf16[512,128]{1,0:T(8,128)(2,1)S(1)}, u32[]{:S(2)}, u32[]{:S(2)}) collective-permute-start(bf16[512,128]{1,0:T(8,128)(2,1)S(1)} %conv_back.6), channel_id=1, source_target_pairs={{1,0},{5,4},{9,8},{13,12},{17,16},{21,20},{25,24},{29,28},{33,32},... | collective-permute-start | bytes 393224 | tf_op jit(solution)/shard_map/ppermute | solution.py:365
  67.0 1.0 collective-permute-done.16.refs_2_
  68.0 1.4 %collective-permute-start.17 = (bf16[256,256]{1,0:T(8,128)(2,1)S(1)}, bf16[256,256]{1,0:T(8,128)(2,1)S(1)}, u32[]{:S(2)}, u32[]{:S(2)}) collective-permute-start(bf16[256,256]{1,0:T(8,128)(2,1)S(1)} %bitcast.71), channel_id=1, source_target_pairs={{0,64},{64,128},{128,192},{192,0},{1,65},{65,129},{129,193},{193,1... | collective-permute-start | bytes 393224 | tf_op jit(solution)/shard_map/ppermute | solution.py:295
  70.2 12.8 %collective-permute-done.12 = bf16[512,128]{1,0:T(8,128)(2,1)S(1)} collective-permute-done((bf16[512,128]{1,0:T(8,128)(2,1)S(1)}, bf16[512,128]{1,0:T(8,128)(2,1)S(1)}, u32[]{:S(2)}, u32[]{:S(2)}) %collective-permute-start.12) | collective-permute-done | bytes 131104 | tf_op jit(solution)/shard_map/ppermute | solution.py:366
  83.3 2.0 %collective-permute-start.21 = (bf16[512,256]{1,0:T(8,128)(2,1)S(1)}, bf16[512,256]{1,0:T(8,128)(2,1)S(1)}, u32[]{:S(2)}, u32[]{:S(2)}) collective-permute-start(bf16[512,256]{1,0:T(8,128)(2,1)S(1)} %maximum_select_fusion.refs_4_), channel_id=1, source_target_pairs={{0,192},{64,0},{128,64},{192,128},{1,193},{65,1},{129,65},{193,129... | collective-permute-start | bytes 786440 | tf_op jit(solution)/shard_map/ppermute | solution.py:292
  85.3 3.0 %conv_back.7 = bf16[512,128]{1,0:T(8,128)(2,1)S(1)} custom-call(s32[3]{0:T(128)S(1)} %pad_add_fusion.flags.refs_0_, bf16[512,128]{1,0:T(8,128)(2,1)S(1)} %get-tuple-element.29.refs_0_, bf16[512,128]{1,0:T(8,128)(2,1)S(1)} %get-tuple-element.28.refs_1_, bf16[9,128,128]{2,1,0:T(8,128)(2,1)S(1)} %copy-done.1, bf16[1024,256]{1,0:T(8,128)(2,1)S(1)} %bitcast.56, ...), custom_call_target="tpu_custom_call" | custom-call | flops 905969664 | bytes 1769472 | tf_op jit(solution)/shard_map/conv_back/pallas_call | solution.py:195
  88.4 2.2 %collective-permute-done.14.refs_5_ = bf16[512,256]{1,0:T(8,128)(2,1)S(1)} collective-permute-done((bf16[512,256]{1,0:T(8,128)(2,1)S(1)}, bf16[512,256]{1,0:T(8,128)(2,1)S(1)}, u32[]{:S(2)}, u32[]{:S(2)}) %collective-permute-start.14) | collective-permute-done | bytes 262176 | tf_op jit(solution)/shard_map/ppermute | solution.py:291
  90.5 2.8 %collective-permute-start.20 = (bf16[256,256]{1,0:T(8,128)(2,1)S(1)}, bf16[256,256]{1,0:T(8,128)(2,1)S(1)}, u32[]{:S(2)}, u32[]{:S(2)}) collective-permute-start(bf16[256,256]{1,0:T(8,128)(2,1)S(1)} %bitcast.73), channel_id=1, source_target_pairs={{0,64},{64,128},{128,192},{192,0},{1,65},{65,129},{129,193},{193,1... | collective-permute-start | bytes 393224 | tf_op jit(solution)/shard_map/ppermute | solution.py:295
  93.7 3.8 %weight_first.1.refs_6_ = f32[8,128,256]{2,1,0:T(8,128)S(1)} custom-call(s32[3]{0:T(128)S(1)} %pad_add_fusion.flags.refs_0_, bf16[512,256]{1,0:T(8,128)(2,1)S(1)} %bitcast.62, bf16[512,256]{1,0:T(8,128)(2,1)S(1)} %collective-permute-done.16.refs_2_, bf16[512,256]{1,0:T(8,128)(2,1)S(1)} %collective-permute-done.18.refs_3_, ...), custom_call_target="tpu_custom_call" | custom-call | flops 1358954496 | bytes 4194304 | tf_op jit(solution)/shard_map/weight_first/pallas_call | solution.py:265
  97.5 2.4 %collective-permute-done.22.refs_4_ = bf16[256,256]{1,0:T(8,128)(2,1)S(1)} collective-permute-done((bf16[256,256]{1,0:T(8,128)(2,1)S(1)}, bf16[256,256]{1,0:T(8,128)(2,1)S(1)}, u32[]{:S(2)}, u32[]{:S(2)}) %collective-permute-start.22) | collective-permute-done | bytes 131104 | tf_op jit(solution)/shard_map/ppermute | solution.py:296
  99.8 2.6 %weight_last.1 = bf16[8,108,256]{2,1,0:T(8,128)(2,1)} custom-call(s32[3]{0:T(128)S(1)} %pad_add_fusion.flags.refs_0_, bf16[256,256]{1,0:T(8,128)(2,1)S(1)} %collective-permute-done.17.refs_1_, bf16[256,256]{1,0:T(8,128)(2,1)S(1)} %collective-permute-done.19.refs_2_, bf16[256,256]{1,0:T(8,128)(2,1)S(1)} %collective-permute-done.20.refs_3_, ...), custom_call_target="tpu_custom_call" | custom-call | flops 452984832 | bytes 4194304 | tf_op jit(solution)/shard_map/weight_last/pallas_call | solution.py:265
  102.4 3.5 %all-to-all-start.1 = ((bf16[8,108,256]{2,1,0:T(8,128)(2,1)}), bf16[8,108,256]{2,1,0:T(8,128)(2,1)S(1)}, u32[]{:S(2)}, u32[]{:S(2)}) async-start(bf16[8,108,256]{2,1,0:T(8,128)(2,1)} %weight_last.1), calls=%async_computation.1 | async-start | bytes 917504 | tf_op jit(solution)/shard_map/all_to_all | solution.py:380
  105.9 1.8 %collective-permute-start.15 = (bf16[4,2,32,128]{3,2,1,0:T(8,128)(2,1)S(1)}, bf16[4,2,32,128]{3,2,1,0:T(8,128)(2,1)S(1)}, u32[]{:S(2)}, u32[]{:S(2)}) collective-permute-start(bf16[4,2,32,128]{3,2,1,0:T(8,128)(2,1)S(1)} %get-tuple-element.23), channel_id=1, source_target_pairs={{0,4},{4,0},{1,5},{5,1},{2,6},{6,2},{3,7},{7,3},{8,12},{12,8},{9,1... | collective-permute-start | bytes 196616 | tf_op jit(solution)/shard_map/ppermute | solution.py:375
  107.7 4.0 %collective-permute-done.15 = bf16[4,2,32,128]{3,2,1,0:T(8,128)(2,1)S(1)} collective-permute-done((bf16[4,2,32,128]{3,2,1,0:T(8,128)(2,1)S(1)}, bf16[4,2,32,128]{3,2,1,0:T(8,128)(2,1)S(1)}, u32[]{:S(2)}, u32[]{:S(2)}) %collective-permute-start.15) | collective-permute-done | bytes 65568 | tf_op jit(solution)/shard_map/ppermute | solution.py:375
  112.6 8.2 %all-to-all-done.1 = bf16[8,108,256]{2,1,0:T(8,128)(2,1)S(1)} async-done(((bf16[8,108,256]{2,1,0:T(8,128)(2,1)}), bf16[8,108,256]{2,1,0:T(8,128)(2,1)S(1)}, u32[]{:S(2)}, u32[]{:S(2)}) %all-to-all-start.1) | async-done | bytes 442400 | tf_op jit(solution)/shard_map/all_to_all | solution.py:380
  (83 shorter events, 13.6 us)
Async XLA Ops:
  1.7 6.4 %collective-permute-start = (bf16[128,256]{1,0:T(8,128)(2,1)S(1)}, bf16[128,256]{1,0:T(8,128)(2,1)S(1)}, u32[]{:S(2)}, u32[]{:S(2)}) collective-permute-start(bf16[128,256]{1,0:T(8,128)(2,1)S(1)} %constant_dynamic-slice_fusion.8), channel_id=1, source_target_pairs={{0,4},{4,0},{1,5},{5,1},{2,6},{6,2},{3,7},{7,3},{8,12},{12,8},{9,1... | collective-permute-start | bytes 196616 | tf_op jit(solution)/shard_map/ppermute | solution.py:330
  7.2 12.9 %copy-start.10 = (bf16[1,2,4,8,4,256]{5,4,3,2,1,0:T(4,128)(2,1)S(1)}, bf16[1,2,4,8,4,256]{5,4,3,2,1,0:T(4,128)(2,1)}, u32[]{:S(2)}) copy-start(bf16[1,2,4,8,4,256]{5,4,3,2,1,0:T(4,128)(2,1)} %param.8) | copy-start | bytes 393220
  8.1 13.1 %copy-start.5 = (f32[1,256]{1,0:T(1,128)S(1)}, f32[1,256]{1,0:T(1,128)}, u32[]{:S(2)}) copy-start(f32[1,256]{1,0:T(1,128)} %shift_ref.1) | copy-start | bytes 3076
  8.1 13.1 %copy-start.7 = (f32[1,256]{1,0:T(1,128)S(1)}, f32[1,256]{1,0:T(1,128)}, u32[]{:S(2)}) copy-start(f32[1,256]{1,0:T(1,128)} %gain_ref.1) | copy-start | bytes 3076
  8.9 25.7 %all-to-all-start = ((bf16[8,128,256]{2,1,0:T(8,128)(2,1)}), bf16[8,128,256]{2,1,0:T(8,128)(2,1)S(1)}, u32[]{:S(2)}, u32[]{:S(2)}) async-start(bf16[8,128,256]{2,1,0:T(8,128)(2,1)} %broadcast_in_dim.2), calls=%async_computation | async-start | bytes 1048576 | tf_op jit(solution)/shard_map/all_to_all | solution.py:335
  17.4 6.6 %collective-permute-start.3 = (bf16[256,128]{1,0:T(8,128)(2,1)S(1)}, bf16[256,128]{1,0:T(8,128)(2,1)S(1)}, u32[]{:S(2)}, u32[]{:S(2)}) collective-permute-start(bf16[256,128]{1,0:T(8,128)(2,1)S(1)} %get-tuple-element.46), channel_id=1, source_target_pairs={{0,4},{4,0},{1,5},{5,1},{2,6},{6,2},{3,7},{7,3},{8,12},{12,8},{9,1... | collective-permute-start | bytes 196616 | tf_op jit(solution)/shard_map/ppermute | solution.py:339
  20.2 7.2 %collective-permute-start.2 = (bf16[4,1,64,256]{3,2,1,0:T(8,128)(2,1)S(1)}, bf16[4,1,64,256]{3,2,1,0:T(8,128)(2,1)S(1)}, u32[]{:S(2)}, u32[]{:S(2)}) collective-permute-start(bf16[4,1,64,256]{3,2,1,0:T(8,128)(2,1)S(1)} %bitcast.68), channel_id=1, source_target_pairs={{0,4},{4,0},{1,5},{5,1},{2,6},{6,2},{3,7},{7,3},{8,12},{12,8},{9,1... | collective-permute-start | bytes 393224 | tf_op jit(solution)/shard_map/ppermute | solution.py:344
  21.3 16.2 %collective-permute-start.4 = (bf16[4,1,64,256]{3,2,1,0:T(8,128)(2,1)S(1)}, bf16[4,1,64,256]{3,2,1,0:T(8,128)(2,1)S(1)}, u32[]{:S(2)}, u32[]{:S(2)}) collective-permute-start(bf16[4,1,64,256]{3,2,1,0:T(8,128)(2,1)S(1)} %bitcast.57), channel_id=1, source_target_pairs={{0,4},{4,0},{1,5},{5,1},{2,6},{6,2},{3,7},{7,3},{8,12},{12,8},{9,1... | collective-permute-start | bytes 393224 | tf_op jit(solution)/shard_map/ppermute | solution.py:347
  34.6 12.9 %collective-permute-start.1 = (bf16[1024,256]{1,0:T(8,128)(2,1)S(1)}, bf16[1024,256]{1,0:T(8,128)(2,1)S(1)}, u32[]{:S(2)}, u32[]{:S(2)}) collective-permute-start(bf16[1024,256]{1,0:T(8,128)(2,1)S(1)} %bitcast.51), channel_id=1, source_target_pairs={{0,64},{64,128},{128,192},{192,0},{1,65},{65,129},{129,193},{193,1... | collective-permute-start | bytes 1572872 | tf_op jit(solution)/shard_map/ppermute | solution.py:291
  35.1 14.2 %collective-permute-start.5 = (bf16[1024,256]{1,0:T(8,128)(2,1)S(1)}, bf16[1024,256]{1,0:T(8,128)(2,1)S(1)}, u32[]{:S(2)}, u32[]{:S(2)}) collective-permute-start(bf16[1024,256]{1,0:T(8,128)(2,1)S(1)} %bitcast.52), channel_id=1, source_target_pairs={{0,192},{64,0},{128,64},{192,128},{1,193},{65,1},{129,65},{193,129... | collective-permute-start | bytes 1572872 | tf_op jit(solution)/shard_map/ppermute | solution.py:292
  37.4 19.6 %copy-start.1 = (bf16[9,128,128]{2,1,0:T(8,128)(2,1)S(1)}, bf16[9,128,128]{2,1,0:T(8,128)(2,1)}, u32[]{:S(2)}) copy-start(bf16[9,128,128]{2,1,0:T(8,128)(2,1)} %constant.51.clone.refs_2_) | copy-start | bytes 884740
  47.6 6.5 %collective-permute-start.6 = (bf16[512,256]{1,0:T(8,128)(2,1)S(1)}, bf16[512,256]{1,0:T(8,128)(2,1)S(1)}, u32[]{:S(2)}, u32[]{:S(2)}) collective-permute-start(bf16[512,256]{1,0:T(8,128)(2,1)S(1)} %slice.18), channel_id=1, source_target_pairs={{0,64},{64,128},{128,192},{192,0},{1,65},{65,129},{129,193},{193,1... | collective-permute-start | bytes 786440 | tf_op jit(solution)/shard_map/ppermute | solution.py:295
  49.3 7.7 %collective-permute-start.7 = (bf16[512,256]{1,0:T(8,128)(2,1)S(1)}, bf16[512,256]{1,0:T(8,128)(2,1)S(1)}, u32[]{:S(2)}, u32[]{:S(2)}) collective-permute-start(bf16[512,256]{1,0:T(8,128)(2,1)S(1)} %slice.24), channel_id=1, source_target_pairs={{0,192},{64,0},{128,64},{192,128},{1,193},{65,1},{129,65},{193,129... | collective-permute-start | bytes 786440 | tf_op jit(solution)/shard_map/ppermute | solution.py:296
  58.2 1.4 %collective-permute-start.8 = (bf16[512,128]{1,0:T(8,128)(2,1)}, bf16[512,128]{1,0:T(8,128)(2,1)S(1)}, u32[]{:S(2)}, u32[]{:S(2)}) collective-permute-start(bf16[512,128]{1,0:T(8,128)(2,1)} %conv_back.4), channel_id=1, source_target_pairs={{3,6},{7,2},{11,14},{15,10},{19,22},{23,18},{27,30},{31,26},{35,38... | collective-permute-start | bytes 393224 | tf_op jit(solution)/shard_map/ppermute | solution.py:366
  58.9 0.7 collective-permute-start.9
  59.6 1.9 %copy-start.3 = (bf16[4,2,64,256]{3,2,1,0:T(8,128)(2,1)S(1)}, bf16[4,2,64,256]{3,2,1,0:T(8,128)(2,1)}, u32[]{:S(2)}) copy-start(bf16[4,2,64,256]{3,2,1,0:T(8,128)(2,1)} %pad_maximum_fusion.1) | copy-start | bytes 786436
  60.2 3.5 %collective-permute-start.10 = (bf16[512,128]{1,0:T(8,128)(2,1)S(1)}, bf16[512,128]{1,0:T(8,128)(2,1)S(1)}, u32[]{:S(2)}, u32[]{:S(2)}) collective-permute-start(bf16[512,128]{1,0:T(8,128)(2,1)S(1)} %conv_back.5), channel_id=1, source_target_pairs={{2,5},{6,1},{10,13},{14,9},{18,21},{22,17},{26,29},{30,25},{34,37}... | collective-permute-start | bytes 393224 | tf_op jit(solution)/shard_map/ppermute | solution.py:366
  60.8 2.8 %collective-permute-start.11 = (bf16[512,128]{1,0:T(8,128)(2,1)S(1)}, bf16[512,128]{1,0:T(8,128)(2,1)S(1)}, u32[]{:S(2)}, u32[]{:S(2)}) collective-permute-start(bf16[512,128]{1,0:T(8,128)(2,1)S(1)} %conv_back.5), channel_id=1, source_target_pairs={{2,1},{6,5},{10,9},{14,13},{18,17},{22,21},{26,25},{30,29},{34,33}... | collective-permute-start | bytes 393224 | tf_op jit(solution)/shard_map/ppermute | solution.py:365
  61.5 6.4 %collective-permute-start.16 = (bf16[512,256]{1,0:T(8,128)(2,1)S(1)}, bf16[512,256]{1,0:T(8,128)(2,1)S(1)}, u32[]{:S(2)}, u32[]{:S(2)}) collective-permute-start(bf16[512,256]{1,0:T(8,128)(2,1)S(1)} %bitcast.60), channel_id=1, source_target_pairs={{0,64},{64,128},{128,192},{192,0},{1,65},{65,129},{129,193},{193,1... | collective-permute-start | bytes 786440 | tf_op jit(solution)/shard_map/ppermute | solution.py:291
  61.6 7.8 %collective-permute-start.18 = (bf16[512,256]{1,0:T(8,128)(2,1)S(1)}, bf16[512,256]{1,0:T(8,128)(2,1)S(1)}, u32[]{:S(2)}, u32[]{:S(2)}) collective-permute-start(bf16[512,256]{1,0:T(8,128)(2,1)S(1)} %bitcast.61), channel_id=1, source_target_pairs={{0,192},{64,0},{128,64},{192,128},{1,193},{65,1},{129,65},{193,129... | collective-permute-start | bytes 786440 | tf_op jit(solution)/shard_map/ppermute | solution.py:292
  64.2 18.8 %copy-start.9 = (bf16[4,2,64,256]{3,2,1,0:T(8,128)(2,1)S(1)}, bf16[4,2,64,256]{3,2,1,0:T(8,128)(2,1)}, u32[]{:S(2)}) copy-start(bf16[4,2,64,256]{3,2,1,0:T(8,128)(2,1)} %copy-done.8) | copy-start | bytes 786436
  64.2 18.7 %collective-permute-start.12 = (bf16[512,128]{1,0:T(8,128)(2,1)S(1)}, bf16[512,128]{1,0:T(8,128)(2,1)S(1)}, u32[]{:S(2)}, u32[]{:S(2)}) collective-permute-start(bf16[512,128]{1,0:T(8,128)(2,1)S(1)} %conv_back.6), channel_id=1, source_target_pairs={{1,4},{5,0},{9,12},{13,8},{17,20},{21,16},{25,28},{29,24},{33,36},... | collective-permute-start | bytes 393224 | tf_op jit(solution)/shard_map/ppermute | solution.py:366
  65.7 17.3 %collective-permute-start.13 = (bf16[512,128]{1,0:T(8,128)(2,1)S(1)}, bf16[512,128]{1,0:T(8,128)(2,1)S(1)}, u32[]{:S(2)}, u32[]{:S(2)}) collective-permute-start(bf16[512,128]{1,0:T(8,128)(2,1)S(1)} %conv_back.6), channel_id=1, source_target_pairs={{1,0},{5,4},{9,8},{13,12},{17,16},{21,20},{25,24},{29,28},{33,32},... | collective-permute-start | bytes 393224 | tf_op jit(solution)/shard_map/ppermute | solution.py:365
  68.0 29.5 %collective-permute-start.17 = (bf16[256,256]{1,0:T(8,128)(2,1)S(1)}, bf16[256,256]{1,0:T(8,128)(2,1)S(1)}, u32[]{:S(2)}, u32[]{:S(2)}) collective-permute-start(bf16[256,256]{1,0:T(8,128)(2,1)S(1)} %bitcast.71), channel_id=1, source_target_pairs={{0,64},{64,128},{128,192},{192,0},{1,65},{65,129},{129,193},{193,1... | collective-permute-start | bytes 393224 | tf_op jit(solution)/shard_map/ppermute | solution.py:295
  69.5 28.0 %collective-permute-start.19 = (bf16[256,256]{1,0:T(8,128)(2,1)S(1)}, bf16[256,256]{1,0:T(8,128)(2,1)S(1)}, u32[]{:S(2)}, u32[]{:S(2)}) collective-permute-start(bf16[256,256]{1,0:T(8,128)(2,1)S(1)} %bitcast.72), channel_id=1, source_target_pairs={{0,192},{64,0},{128,64},{192,128},{1,193},{65,1},{129,65},{193,129... | collective-permute-start | bytes 393224 | tf_op jit(solution)/shard_map/ppermute | solution.py:296
  83.2 7.3 %collective-permute-start.14 = (bf16[512,256]{1,0:T(8,128)(2,1)S(1)}, bf16[512,256]{1,0:T(8,128)(2,1)S(1)}, u32[]{:S(2)}, u32[]{:S(2)}) collective-permute-start(bf16[512,256]{1,0:T(8,128)(2,1)S(1)} %maximum_select_fusion.refs_4_), channel_id=1, source_target_pairs={{0,64},{64,128},{128,192},{192,0},{1,65},{65,129},{129,193},{193,1... | collective-permute-start | bytes 786440 | tf_op jit(solution)/shard_map/ppermute | solution.py:291
  83.3 10.1 %collective-permute-start.21 = (bf16[512,256]{1,0:T(8,128)(2,1)S(1)}, bf16[512,256]{1,0:T(8,128)(2,1)S(1)}, u32[]{:S(2)}, u32[]{:S(2)}) collective-permute-start(bf16[512,256]{1,0:T(8,128)(2,1)S(1)} %maximum_select_fusion.refs_4_), channel_id=1, source_target_pairs={{0,192},{64,0},{128,64},{192,128},{1,193},{65,1},{129,65},{193,129... | collective-permute-start | bytes 786440 | tf_op jit(solution)/shard_map/ppermute | solution.py:292
  85.3 8.4 %copy-start.2 = (bf16[9,256,256]{2,1,0:T(8,128)(2,1)S(1)}, bf16[9,256,256]{2,1,0:T(8,128)(2,1)}, u32[]{:S(2)}) copy-start(bf16[9,256,256]{2,1,0:T(8,128)(2,1)} %constant.52.clone.refs_7_.refs_5_) | copy-start | bytes 3538948
  90.5 6.9 %collective-permute-start.20 = (bf16[256,256]{1,0:T(8,128)(2,1)S(1)}, bf16[256,256]{1,0:T(8,128)(2,1)S(1)}, u32[]{:S(2)}, u32[]{:S(2)}) collective-permute-start(bf16[256,256]{1,0:T(8,128)(2,1)S(1)} %bitcast.73), channel_id=1, source_target_pairs={{0,64},{64,128},{128,192},{192,0},{1,65},{65,129},{129,193},{193,1... | collective-permute-start | bytes 393224 | tf_op jit(solution)/shard_map/ppermute | solution.py:295
  93.4 6.5 %collective-permute-start.22 = (bf16[256,256]{1,0:T(8,128)(2,1)S(1)}, bf16[256,256]{1,0:T(8,128)(2,1)S(1)}, u32[]{:S(2)}, u32[]{:S(2)}) collective-permute-start(bf16[256,256]{1,0:T(8,128)(2,1)S(1)} %bitcast.74), channel_id=1, source_target_pairs={{0,192},{64,0},{128,64},{192,128},{1,193},{65,1},{129,65},{193,129... | collective-permute-start | bytes 393224 | tf_op jit(solution)/shard_map/ppermute | solution.py:296
  102.4 18.3 %all-to-all-start.1 = ((bf16[8,108,256]{2,1,0:T(8,128)(2,1)}), bf16[8,108,256]{2,1,0:T(8,128)(2,1)S(1)}, u32[]{:S(2)}, u32[]{:S(2)}) async-start(bf16[8,108,256]{2,1,0:T(8,128)(2,1)} %weight_last.1), calls=%async_computation.1 | async-start | bytes 917504 | tf_op jit(solution)/shard_map/all_to_all | solution.py:380
  105.9 5.9 %collective-permute-start.15 = (bf16[4,2,32,128]{3,2,1,0:T(8,128)(2,1)S(1)}, bf16[4,2,32,128]{3,2,1,0:T(8,128)(2,1)S(1)}, u32[]{:S(2)}, u32[]{:S(2)}) collective-permute-start(bf16[4,2,32,128]{3,2,1,0:T(8,128)(2,1)S(1)} %get-tuple-element.23), channel_id=1, source_target_pairs={{0,4},{4,0},{1,5},{5,1},{2,6},{6,2},{3,7},{7,3},{8,12},{12,8},{9,1... | collective-permute-start | bytes 196616 | tf_op jit(solution)/shard_map/ppermute | solution.py:375
  (4 other events, 2.9 us)
